TPU v7x, 256 devices: a whole 4x4x8 slice. The times are simulated.
256 devices in a mesh: dom: 64 (over y, x_hi, z), cls: 4 (over x_lo, core).
Axes of the slice: x: 4 (x_hi: 2, x_lo: 2; x = x_hi * 2 + x_lo), y: 4, z: 8, core: 2. Of those that a mesh axis runs over, the one named last changes fastest.
Arguments:
- images: bfloat16 [4096, 3072], P('dom'), may hold values from -160 to 160
- offsets: int32 [4096, 2], P('dom'), may hold values from -4 to 4
- class_lists: int32 [4096, 8], P('dom'), may hold values from 0 to 99, as said below
- noise_weight: float32 [1536], replicated, may hold values from 0.5 to 2
- references: bfloat16 [100, 24, 3072], P('cls', None, 'dom'), may hold values from -3 to 3
Outputs:
- class_sums: float32 [3072, 2400], P('dom', 'cls')
Inputs may be any that keep to these rules, and one draw needn't show every extreme that they name: `class_lists`: each particle names 8 different classes.
All inputs are finite; a program needn't handle non-finite values.
Results may differ from a plain program's by a relative error of at most 0.0023.
Values may be sent and summed in bfloat16 or wider, within the bound.
No kernel may reach another device: no remote copies, remote signals or barrier semaphores. Data moves between devices by JAX's collectives and lax.ppermute only.
A program may use at most 128 MiB of HBM per device.

v0:
```python
import math

import jax
import jax.numpy as jnp
from jax import lax
from jax.sharding import PartitionSpec as P

GRID = 5
BOX = 64


excluded = -1e30


def probe_images(images, offsets, noise_weight):
    half_width = images.shape[1] // 2
    shifts = GRID * GRID
    coeff_index = jnp.arange(half_width, dtype=jnp.int32)
    freq_x = (coeff_index % BOX - BOX // 2).astype(jnp.float32)
    freq_y = (coeff_index // BOX).astype(jnp.float32)
    shift_index = jnp.arange(shifts, dtype=jnp.int32)
    grid_x = shift_index % GRID - GRID // 2
    grid_y = shift_index // GRID - GRID // 2
    move_x = (offsets[:, 0:1] + grid_x[None, :]).astype(jnp.float32)
    move_y = (offsets[:, 1:2] + grid_y[None, :]).astype(jnp.float32)
    angles = (
        2.0
        * math.pi
        / BOX
        * (move_x[:, :, None] * freq_x[None, None, :] + move_y[:, :, None] * freq_y[None, None, :])
    )
    cosine = jnp.cos(angles)
    sine_part = jnp.sin(angles)
    values = images.astype(jnp.float32)
    real_part = values[:, None, :half_width]
    imag_part = values[:, None, half_width:]
    shifted_re = (real_part * cosine + imag_part * sine_part) * noise_weight
    shifted_im = (imag_part * cosine - real_part * sine_part) * noise_weight
    return jnp.concatenate([shifted_re, shifted_im], axis=-1).astype(jnp.bfloat16)


def per_device(images, offsets, class_lists, noise_weight, references):
    particles, width = images.shape
    local_classes, rotations, columns = references.shape
    shifts = GRID * GRID
    probes = probe_images(images, offsets, noise_weight)
    probe_rows = probes.reshape(particles * shifts, width)
    weight_cols = jnp.concatenate([noise_weight, noise_weight])
    piece = lax.all_gather(references, "dom", axis=2, tiled=True)
    count_cols = piece.shape[2]
    flat_piece = piece.reshape(local_classes * rotations, count_cols)
    probe_cols = probe_rows
    cross = lax.dot_general(
        probe_cols, flat_piece, (((1,), (1,)), ((), ())), preferred_element_type=jnp.float32
    )
    piece_f32 = flat_piece.astype(jnp.float32)
    energy = jnp.sum(piece_f32 * piece_f32 * weight_cols[None, :], axis=1)
    cross, energy = (cross, energy)
    scale_factor = 1.0 / math.sqrt(width)
    scores = ((cross - 0.5 * energy[None, :]) * scale_factor).reshape(
        particles, shifts, local_classes, rotations
    )
    class_ids = lax.axis_index("cls") * local_classes + jnp.arange(local_classes, dtype=jnp.int32)
    listed = jnp.any(class_lists[:, :, None] == class_ids[None, None, :], axis=1)
    keep = listed[:, None, :, None]
    masked = jnp.where(keep, scores, excluded)
    local_top = jnp.max(masked, axis=(1, 2, 3))
    top_score = lax.pmax(local_top, "cls")
    expo_local = jnp.where(keep, jnp.exp(masked - top_score[:, None, None, None]), 0.0)
    mass_total = lax.psum(jnp.sum(expo_local, axis=(1, 2, 3)), "cls")
    expo = jnp.where(keep, jnp.exp(masked - top_score[:, None, None, None]), 0.0)
    posterior = (expo / mass_total[:, None, None, None]).astype(jnp.bfloat16)
    post_rows = posterior.reshape(particles * shifts, local_classes * rotations)
    owned_rows = width // lax.axis_size("dom")
    probe_cols = probe_rows
    summed = lax.psum(
        lax.dot_general(
            probe_cols, post_rows, (((0,), (0,)), ((), ())), preferred_element_type=jnp.float32
        ),
        "dom",
    )
    return lax.dynamic_slice_in_dim(summed, lax.axis_index("dom") * owned_rows, owned_rows, 0)


def solution(mesh):
    in_specs = (P("dom", None), P("dom", None), P("dom", None), P(), P("cls", None, "dom"))
    out_specs = P("dom", "cls")
    return jax.shard_map(
        per_device, mesh=mesh, in_specs=in_specs, out_specs=out_specs, check_vma=False
    )
```

profile of v0, /device:TPU:2, one launch (start us, length us, event | category | flops | bytes accessed | tf_op | source)
XLA Modules:
  0.0 1034.7 jit_solution(16844019822587792002)
XLA Ops:
  6.5 1.9 copy.20
  8.5 0.8 slice_bitcast_fusion.1
  9.4 0.1 convert_element_type.51
  9.5 0.1 convert_element_type.54
  9.7 1.1 fusion.27
  10.8 6.2 mul.129
  17.0 10.8 %mul.130 = f32[1600,1536]{1,0:T(8,128)} reshape(f32[64,25,1536]{2,1,0:T(8,128)} %mul.129) | data formatting | bytes 19660800 | tf_op jit(solution)/shard_map/mul | solution.py:37
  27.8 6.2 mul.140
  33.9 10.8 %mul.141 = f32[1600,1536]{1,0:T(8,128)} reshape(f32[64,25,1536]{2,1,0:T(8,128)} %mul.140) | data formatting | bytes 19660800 | tf_op jit(solution)/shard_map/mul | solution.py:37
  44.8 0.1 compare_reduce_fusion
  44.9 3.6 broadcast_in_dim.24
  48.5 12.6 %broadcast_in_dim.25 = pred[1600,600]{0,1:T(8,128)(4,1)S(1)} reshape(pred[64,25,25,24]{1,0,3,2:T(8,128)(4,1)} %broadcast_in_dim.24) | data formatting | bytes 1920000 | tf_op jit(solution)/shard_map/jit(_where)/broadcast_in_dim | solution.py:71
  61.1 42.9 %multiply_convert_fusion.1 = (bf16[1600,1536]{1,0:T(8,128)(2,1)}, bf16[1600,1536]{1,0:T(8,128)(2,1)}) fusion(f32[1600,1536]{1,0:T(8,128)} %mul.141, f32[1600,1536]{1,0:T(8,128)} %mul.130, f32[1536]{0:T(1024)S(1)} %copy-done, f32[1536]{0:T(1024)S(1)} %get-tuple-element.16, f32[1600]{0:T(1024)S(1)} %convert_element_type.54, f32[1536]{0:T(1024)S(1)} %get-tuple-element.15, ...), kind=kLoop, calls=%fused_computation.2 | loop fusion | flops 34406400 | bytes 29522432 | tf_op jit(solution)/shard_map/convert
  104.1 134.1 %all-gather.2.cloned.1.call-done = bf16[25,24,3072]{0,1,2:T(8,128)(2,1)} async-done(((bf16[25,24,48]{0,1,2:T(8,128)(2,1)}), bf16[25,24,3072]{0,1,2:T(8,128)(2,1)}) %all-gather.2.cloned.1.call-update) | async-done | bytes 3686416 | tf_op jit(solution)/shard_map/all_gather | solution.py:49
  238.1 19.5 %copy.21 = bf16[25,24,3072]{2,1,0:T(8,128)(2,1)} copy(bf16[25,24,3072]{0,1,2:T(8,128)(2,1)} %all-gather.2.cloned.1.call-done) | data formatting | bytes 7372800 | tf_op jit(solution)/shard_map/all_gather | solution.py:49
  257.6 3.1 multiply_reduce_fusion
  260.7 0.1 copy.25
  260.8 0.1 copy.24
  260.8 0.1 mul.154
  260.9 13.9 %fusion.4 = (f32[1600]{0:T(1024)S(1)}, f32[1600,600]{0,1:T(8,128)}) fusion(pred[1600,600]{0,1:T(8,128)(4,1)S(1)} %broadcast_in_dim.25, f32[600]{0:T(1024)S(1)} %mul.154, bf16[600,3072]{1,0:T(8,128)(2,1)} %bitcast.10, bf16[1600,1536]{1,0:T(8,128)(2,1)} %get-tuple-element.6, bf16[1600,1536]{1,0:T(8,128)(2,1)} %get-tuple-element.5), kind=kOutput, calls=%fused_computation.12 | convolution fusion | flops 5921739264 | bytes 18325600 | tf_op jit(solution)/shard_map/dot_general | solution.py:53
  274.8 0.1 reduce_max.14
  275.0 0.1 reduce_max.18
  275.1 6.1 pmax.7
  281.2 0.1 sub.59
  281.4 3.6 fusion.5
  285.0 0.1 reduce_sum.27
  285.1 0.1 reduce_sum.28
  285.2 6.1 psum.14
  291.4 0.1 div.35
  291.6 17.0 %fusion.2 = f32[3072,600]{1,0:T(8,128)} fusion(bf16[1600,1536]{1,0:T(8,128)(2,1)} %get-tuple-element.6, bf16[1600,1536]{1,0:T(8,128)(2,1)} %get-tuple-element.5, pred[1600,600]{0,1:T(8,128)(4,1)S(1)} %broadcast_in_dim.25, f32[1600,600]{0,1:T(8,128)} %get-tuple-element.12, f32[1600]{0:T(1024)S(1)} %div.35, f32[1600]{0:T(1024)S(1)} %sub.59, f32[600]{0:T(1024)S(1)} %mul.154), kind=kOutput, calls=%fused_computation.7 | convolution fusion | flops 5924620800 | bytes 22018400 | tf_op jit(solution)/shard_map/dot_general | solution.py:77
  308.6 717.6 %all-reduce.2.cloned.1.call-done = f32[3072,600]{1,0:T(8,128)} async-done(((f32[3072,600]{1,0:T(8,128)}), f32[3072,600]{1,0:T(8,128)}) %all-reduce.2.cloned.1.call-update) | async-done | bytes 7372816 | tf_op jit(solution)/shard_map/psum | solution.py:76
  1026.3 1.6 constant_dynamic-slice_fusion
  (17 shorter events, 0.4 us)
Async XLA Ops:
  6.5 231.6 %all-gather.2.cloned.1.call-start = ((), (), s32[]{:S(2)}) async-start(), calls=%async_computation | async-start | bytes 19169280 | tf_op jit(solution)/shard_map/all_gather | solution.py:49
  8.5 1017.8 %all-reduce.2.cloned.1.call-start = ((), (), s32[]{:S(2)}) async-start(), calls=%async_computation.1 | async-start | bytes 15728640 | tf_op jit(solution)/shard_map/psum | solution.py:76
  33.9 10.9 %copy-start.1 = (s32[64,8]{0,1:T(8,128)S(1)}, s32[64,8]{0,1:T(8,128)}, u32[]{:S(2)}) copy-start(s32[64,8]{0,1:T(8,128)} %param.7) | copy-start | bytes 6148
  44.9 16.2 %copy-start = (f32[1536]{0:T(1024)S(1)}, f32[1536]{0:T(1024)}, u32[]{:S(2)}) copy-start(f32[1536]{0:T(1024)} %param.8) | copy-start | bytes 18436
Sparse Core Ops, SparseCore 0:
  11.0 227.0 all-gather.1
  308.7 717.4 all-reduce.1
where the time goes:
time: 1040 us; the launch traced here: 1030 us
  waiting for transfers between devices  852 us (82%)
  local copies, waits for them, and re-layouts  76.2 us (7%)
  other arithmetic  50 us (5%)
  matrix products  30.9 us (3%)
  between operations  13.5 us (1%)
  blocking collectives  12.2 us (1%)
    psum x1, waiting for transfers between devices, per_device(): lax.psum(lax.dot_general(probe_cols, post_rows, (((0,), (0,)), ((), ())),...  718 us
    all_gather x1, waiting for transfers between devices, per_device(): piece = lax.all_gather(references, 'dom', axis=2, tiled=True)  134 us
    another operation x1, other arithmetic  42.9 us
    mul x4, local copies, waits for them, and re-layouts, probe_images(): shifted_re = (real_part * cosine + imag_part * sine_part) * noise_weight  34 us
  transfers between devices with their start and end apart: 2, of which 2 were waited for; matrix products, arithmetic and copies ran while one was open for 9% of the time, Pallas kernels for 0%

commit v1 on v0

v1 whole, which is shorter than its diff:
```python
import functools
import math

import jax
import jax.numpy as jnp
import numpy as np
from jax import lax
from jax.experimental import pallas as pl
from jax.experimental.pallas import tpu as pltpu
from jax.sharding import Mesh, PartitionSpec as P

GRID = 5
BOX = 64
HALF = 1536
WIDTH = 3072
PARTS = 64
ROWS = 75
PAD = 80
LANES = 128
CHUNK = 384
GROUP = 8
NPART = PARTS * GROUP
SHIFTS = GRID * GRID
EXCLUDED = -1e30
SCALE = 1.0 / math.sqrt(WIDTH)
AXES = ("y", "xh", "z", "xl", "co")

f32 = jnp.float32
bf16 = jnp.bfloat16


def twiddles():
    k = np.arange(HALF)
    kx = k % BOX - BOX // 2
    ky = k // BOX
    rows = []
    for freq in (kx, ky):
        for g in (1, 2):
            angle = 2.0 * math.pi / BOX * ((g * freq) % BOX)
            rows += [np.cos(angle), np.sin(angle)]
    return np.stack(rows).astype(np.float32)


def sin_cos(turns):
    quarter = jnp.floor(turns * (1.0 / 16.0) + 0.5)
    rest = (turns - 16.0 * quarter) * (2.0 * math.pi / BOX)
    sq = rest * rest
    sin = rest * (
        1.0 + sq * (-1.0 / 6 + sq * (1.0 / 120 + sq * (-1.0 / 5040 + sq * (1.0 / 362880))))
    )
    cos = 1.0 + sq * (
        -0.5 + sq * (1.0 / 24 + sq * (-1.0 / 720 + sq * (1.0 / 40320 + sq * (-1.0 / 3628800))))
    )
    quad = quarter - 4.0 * jnp.floor(quarter * 0.25)
    swap = (quad == 1.0) | (quad == 3.0)
    sin_q = jnp.where(swap, cos, sin)
    cos_q = jnp.where(swap, sin, cos)
    sin_q = jnp.where(quad >= 2.0, -sin_q, sin_q)
    cos_q = jnp.where((quad == 1.0) | (quad == 2.0), -cos_q, cos_q)
    return sin_q, cos_q


def prep_kernel(img_ref, off_ref, list_ref, w_ref, out_ref):
    off = off_ref[...].astype(f32)
    ox, oy = off[:, 0:1], off[:, 1:2]
    for t in range(HALF // LANES):
        lanes = slice(t * LANES, (t + 1) * LANES)
        k = lax.broadcasted_iota(jnp.int32, (1, LANES), 1) + t * LANES
        kx = ((k & (BOX - 1)) - BOX // 2).astype(f32)
        ky = (k >> 6).astype(f32)
        sin, cos = sin_cos(ox * kx + oy * ky)
        a = img_ref[:, lanes].astype(f32)
        b = img_ref[:, HALF + t * LANES : HALF + (t + 1) * LANES].astype(f32)
        w = w_ref[:, lanes]
        out_ref[:, lanes] = (w * (a * cos + b * sin)).astype(bf16)
        out_ref[:, HALF + t * LANES : HALF + (t + 1) * LANES] = (w * (b * cos - a * sin)).astype(
            bf16
        )
    lists = list_ref[...]
    lane = lax.broadcasted_iota(jnp.int32, (PARTS, LANES), 1)
    listed = lists[:, 0:1] == lane
    for n in range(1, lists.shape[1]):
        listed = listed | (lists[:, n : n + 1] == lane)
    out_ref[:, WIDTH:] = jnp.where(listed, 1.0, 0.0).astype(bf16)


def prep(images, offsets, class_lists, weight):
    return pl.pallas_call(
        prep_kernel,
        out_shape=jax.ShapeDtypeStruct((PARTS, WIDTH + LANES), bf16),
    )(images, offsets, class_lists, weight)


def rotate_x(yr, yi, tab_ref, g, lanes):
    c = tab_ref[2 * g - 2 : 2 * g - 1, lanes]
    s = tab_ref[2 * g - 1 : 2 * g, lanes]
    cr, ci, sr, si = yr * c, yi * c, yr * s, yi * s
    return (cr - si, ci + sr), (cr + si, ci - sr)


def y_twiddle(tab_ref, step, lanes):
    two = (step == 0) | (step == 4)
    zero = step == 2
    sign = jnp.where(step < 2, -1.0, 1.0)
    c = jnp.where(two, tab_ref[6:7, lanes], tab_ref[4:5, lanes])
    s = jnp.where(two, tab_ref[7:8, lanes], tab_ref[5:6, lanes])
    return jnp.where(zero, 1.0, c), jnp.where(zero, 0.0, s * sign)


def estep_kernel(base_ref, p_ref, r_ref, tab_ref, w_ref, expo_ref, stat_ref, shifted, energy, mask, top):
    step = pl.program_id(0)

    @pl.when(step == 0)
    def _():
        total = jnp.zeros((PAD, LANES), f32)
        for g in range(GROUP):
            for t in range(CHUNK // LANES):
                r = r_ref[g, :, t * LANES : (t + 1) * LANES].astype(f32)
                at = (g % 4) * CHUNK + t * LANES
                total = total + r * r * w_ref[:, at : at + LANES]
        energy[...] = jnp.broadcast_to(0.5 * jnp.sum(total, axis=1, keepdims=True), energy.shape)
        row = lax.broadcasted_iota(jnp.int32, (PAD, LANES), 0)
        number = ((base_ref[0] + row) * 2731) >> 16
        lane = lax.broadcasted_iota(jnp.int32, (PAD, LANES), 1)
        pick = jnp.where((number == lane) & (row < ROWS), 1.0, 0.0).astype(bf16)
        mask[...] = lax.dot_general(
            pick, p_ref[:, WIDTH:], (((1,), (1,)), ((), ())), preferred_element_type=f32
        )
        top[...] = jnp.full(top.shape, EXCLUDED, f32)

    for g in range(4):
        for t in range(CHUNK // LANES):
            at = g * CHUNK + t * LANES
            lanes = slice(at, at + LANES)
            ims = slice(HALF + at, HALF + at + LANES)
            rr = r_ref[g, :, t * LANES : (t + 1) * LANES].astype(f32)
            ri = r_ref[g + 4, :, t * LANES : (t + 1) * LANES].astype(f32)
            cy, sy = y_twiddle(tab_ref, step, lanes)
            yr = rr * cy - ri * sy
            yi = ri * cy + rr * sy
            shifted[2 * PAD : 3 * PAD, lanes] = yr.astype(bf16)
            shifted[2 * PAD : 3 * PAD, ims] = yi.astype(bf16)
            for gx in (1, 2):
                plus, minus = rotate_x(yr, yi, tab_ref, gx, lanes)
                for at_row, (vr, vi) in (((2 + gx) * PAD, plus), ((2 - gx) * PAD, minus)):
                    shifted[at_row : at_row + PAD, lanes] = vr.astype(bf16)
                    shifted[at_row : at_row + PAD, ims] = vi.astype(bf16)
    cross = lax.dot_general(
        shifted[...], p_ref[:, :WIDTH], (((1,), (1,)), ((), ())), preferred_element_type=f32
    )
    half_energy = energy[:, 0:1]
    keep = mask[...] > 0.5
    best = top[...]
    for gx in range(GRID):
        score = (cross[gx * PAD : (gx + 1) * PAD] - half_energy) * SCALE
        score = jnp.where(keep, score, EXCLUDED)
        expo_ref[pl.ds(pl.multiple_of((step * GRID + gx) * PAD, PAD), PAD), :] = score
        best = jnp.maximum(best, jnp.max(score.reshape(PAD // 8, 8, NPART), axis=0))
    top[...] = best

    @pl.when(step == GRID - 1)
    def _():
        peak = jnp.max(top[...], axis=0, keepdims=True)

        def body(s, mass):
            at = pl.ds(pl.multiple_of(s * PAD, PAD), PAD)
            e = jnp.where(mask[...] > 0.5, jnp.exp(expo_ref[at, :] - peak), 0.0)
            expo_ref[at, :] = e
            return mass + jnp.sum(e.reshape(PAD // 8, 8, NPART), axis=0)

        mass = lax.fori_loop(0, SHIFTS, body, jnp.zeros((8, NPART), f32))
        stat_ref[0:1, :] = peak
        stat_ref[1:2, :] = jnp.sum(mass, axis=0, keepdims=True)


def full(shape):
    return pl.BlockSpec(shape, lambda i: (0,) * len(shape))


def estep(base, probes, refs, table, weight):
    return pl.pallas_call(
        estep_kernel,
        grid=(GRID,),
        in_specs=[
            pl.BlockSpec(memory_space=pltpu.SMEM),
            full((NPART, WIDTH + LANES)),
            full((GROUP, PAD, CHUNK)),
            full((8, HALF)),
            full((1, HALF)),
        ],
        out_specs=[full((SHIFTS * PAD, NPART)), full((2, NPART))],
        out_shape=[
            jax.ShapeDtypeStruct((SHIFTS * PAD, NPART), f32),
            jax.ShapeDtypeStruct((2, NPART), f32),
        ],
        scratch_shapes=[
            pltpu.VMEM((GRID * PAD, WIDTH), bf16),
            pltpu.VMEM((PAD, LANES), f32),
            pltpu.VMEM((PAD, NPART), f32),
            pltpu.VMEM((8, NPART), f32),
        ],
        compiler_params=pltpu.CompilerParams(vmem_limit_bytes=48 << 20),
    )(base, probes, refs, table, weight)


def mstep_kernel(stat_ref, all_ref, p_ref, expo_ref, tab_ref, out_ref, post, sums):
    step = pl.program_id(0)
    count = all_ref.shape[0]
    peak = all_ref[0, 0:1, :]
    for d in range(1, count):
        peak = jnp.maximum(peak, all_ref[d, 0:1, :])
    mass = jnp.zeros((1, NPART), f32)
    for d in range(count):
        mass = mass + all_ref[d, 1:2, :] * jnp.exp(all_ref[d, 0:1, :] - peak)
    factor = jnp.exp(stat_ref[0:1, :] - peak) / mass
    post[...] = (expo_ref[...] * factor).astype(bf16)
    sums[...] = jnp.dot(post[...], p_ref[:, :WIDTH], preferred_element_type=f32)
    for g in range(4):
        for t in range(CHUNK // LANES):
            at = g * CHUNK + t * LANES
            lanes = slice(at, at + LANES)
            ims = slice(HALF + at, HALF + at + LANES)
            re = sums[2 * PAD : 3 * PAD, lanes]
            im = sums[2 * PAD : 3 * PAD, ims]
            for gx in (1, 2):
                c = tab_ref[2 * gx - 2 : 2 * gx - 1, lanes]
                s = tab_ref[2 * gx - 1 : 2 * gx, lanes]
                hi = slice((2 + gx) * PAD, (3 + gx) * PAD)
                lo = slice((2 - gx) * PAD, (3 - gx) * PAD)
                pr, pi = sums[hi, lanes], sums[hi, ims]
                mr, mi = sums[lo, lanes], sums[lo, ims]
                re = re + c * (pr + mr) + s * (pi - mi)
                im = im + c * (pi + mi) - s * (pr - mr)
            cy, sy = y_twiddle(tab_ref, step, lanes)
            new_re = re * cy + im * sy
            new_im = im * cy - re * sy
            chunk = slice(t * LANES, (t + 1) * LANES)

            @pl.when(step == 0)
            def _():
                out_ref[g, :, chunk] = new_re
                out_ref[g + 4, :, chunk] = new_im

            @pl.when(step > 0)
            def _():
                out_ref[g, :, chunk] += new_re
                out_ref[g + 4, :, chunk] += new_im


def mstep(stat, stats, probes, expo, table):
    return pl.pallas_call(
        mstep_kernel,
        grid=(GRID,),
        in_specs=[
            full((2, NPART)),
            full(stats.shape),
            full((NPART, WIDTH + LANES)),
            pl.BlockSpec((GRID * PAD, NPART), lambda i: (i, 0)),
            full((8, HALF)),
        ],
        out_specs=full((GROUP, PAD, CHUNK)),
        out_shape=jax.ShapeDtypeStruct((GROUP, PAD, CHUNK), f32),
        scratch_shapes=[
            pltpu.VMEM((GRID * PAD, NPART), bf16),
            pltpu.VMEM((GRID * PAD, WIDTH), f32),
        ],
        compiler_params=pltpu.CompilerParams(vmem_limit_bytes=48 << 20),
    )(stat, stats, probes, expo, table)


def per_device(images, offsets, class_lists, noise_weight, references):
    weight = noise_weight.reshape(1, HALF)
    table = jnp.asarray(twiddles())
    own = prep(images, offsets, class_lists, weight)
    probes = lax.all_gather(own, "z").reshape(NPART, WIDTH + LANES)

    mine = references.reshape(GROUP, ROWS, 48)
    mine = lax.all_to_all(mine, "z", 0, 0)
    mine = jnp.transpose(mine, (1, 0, 2)).reshape(ROWS, CHUNK)
    mine = jnp.pad(mine, ((0, PAD - ROWS), (0, 0)))
    refs = lax.all_to_all(
        jnp.broadcast_to(mine, (GROUP, PAD, CHUNK)), ("y", "xh"), 0, 0
    )

    cls = lax.axis_index("xl") * 2 + lax.axis_index("co")
    base = (cls * (ROWS * GROUP) + lax.axis_index("z") * ROWS).astype(jnp.int32).reshape(1)
    expo, stat = estep(base, probes, refs, table, weight)
    stats = lax.all_to_all(
        jnp.broadcast_to(stat, (32, 2, NPART)), ("z", "xl", "co"), 0, 0
    )
    sums = mstep(stat, stats, probes, expo, table)

    sums = jnp.sum(lax.all_to_all(sums, ("y", "xh"), 0, 0), axis=0)
    sums = jnp.transpose(sums[:ROWS].reshape(ROWS, GROUP, 48), (1, 2, 0))
    sums = lax.all_to_all(sums, "z", 0, 0)
    return jnp.transpose(sums, (1, 0, 2)).reshape(48, GROUP * ROWS)


def solution(mesh):
    fine = Mesh(mesh.devices.reshape(4, 2, 8, 2, 2), AXES)
    dom, cls = ("y", "xh", "z"), ("xl", "co")
    in_specs = (P(dom, None), P(dom, None), P(dom, None), P(), P(cls, None, dom))
    return jax.shard_map(
        per_device, mesh=fine, in_specs=in_specs, out_specs=P(dom, cls), check_vma=False
    )
```

time: 1040 us -> 148 us (0.14)
  waiting for transfers between devices: 852 us -> 24.3 us
  local copies, waits for them, and re-layouts: 76.2 us -> 10.5 us
  blocking collectives: 12.2 us -> 65.7 us
  other arithmetic: 50 us -> 0.05 us
  matrix products: 30.9 us -> 0 us
  Pallas kernels: 0 us -> 27.7 us
    psum x1 -> x0, waiting for transfers between devices: 718 us -> none  [per_device(): lax.psum(lax.dot_general(probe_cols, post_rows, (((0,), (0,)), ((), ())),...]
    all_gather x1, waiting for transfers between devices: 134 us -> 14.2 us  [per_device(): probes = lax.all_gather(own, 'z').reshape(NPART, WIDTH + LANES)]
    all_to_all x0 -> x4, blocking collectives: none -> 65.7 us  [the longest x1 21.6 us: per_device(): sums = jnp.sum(lax.all_to_all(sums, ('y', 'xh'), 0, 0), axis=0)]
    another operation x1 -> x0, other arithmetic: 42.9 us -> none
    mul x6 -> x0, local copies, waits for them, and re-layouts: 34.2 us -> none  [the longest x4 34 us: probe_images(): shifted_re = (real_part * cosine + imag_part * sine_part) * noise_weight]
    dot_general x2 -> x0, matrix products: 30.9 us -> none  [the longest x1 17 us: per_device(): lax.dot_general(probe_cols, post_rows, (((0,), (0,)), ((), ())), preferre...]
    pallas_call x0 -> x3, Pallas kernels: none -> 27.7 us  [the longest x1 13.9 us: mstep(): pl.pallas_call(mstep_kernel, grid=(GRID,), in_specs=[full((2, NPART)), fu...]
    all_gather x1 -> x0, local copies, waits for them, and re-layouts: 19.5 us -> none  [per_device(): piece = lax.all_gather(references, 'dom', axis=2, tiled=True)]
  transfers between devices with their start and end apart: 2 -> 2, of which waited for: 2 -> 2; matrix products, arithmetic and copies ran while one was open for 9% -> 1% of each run, Pallas kernels for 0% -> 0%
where the time goes in v1:
time: 148 us
  blocking collectives  65.7 us (44%)
  Pallas kernels  27.7 us (19%)
  waiting for transfers between devices  24.3 us (16%)
  between operations  13.4 us (9%)
  local copies, waits for them, and re-layouts  10.5 us (7%)
  starting transfers between devices  6.13 us (4%)
    all_to_all x1, blocking collectives, per_device(): sums = jnp.sum(lax.all_to_all(sums, ('y', 'xh'), 0, 0), axis=0)  21.6 us
    all_to_all x1, blocking collectives, per_device(): mine = lax.all_to_all(mine, 'z', 0, 0)  17 us
    all_to_all x1, blocking collectives, per_device(): lax.all_to_all(jnp.broadcast_to(stat, (32, 2, NPART)), ('z', 'xl', 'co'),...  14.9 us
    all_gather x1, waiting for transfers between devices, per_device(): probes = lax.all_gather(own, 'z').reshape(NPART, WIDTH + LANES)  14.2 us
    pallas_call x1, Pallas kernels, mstep(): pl.pallas_call(mstep_kernel, grid=(GRID,), in_specs=[full((2, NPART)), fu...  13.9 us
    all_to_all x1, blocking collectives, per_device(): sums = lax.all_to_all(sums, 'z', 0, 0)  12.2 us
    pallas_call x1, Pallas kernels, estep(): pl.pallas_call(estep_kernel, grid=(GRID,), in_specs=[pl.BlockSpec(memory_...  11.3 us
    all_to_all x1, waiting for transfers between devices, per_device(): lax.all_to_all(jnp.broadcast_to(mine, (GROUP, PAD, CHUNK)), ('y', 'xh'),...  10 us
  transfers between devices with their start and end apart: 2, of which 2 were waited for; matrix products, arithmetic and copies ran while one was open for 1% of the time, Pallas kernels for 0%

profile of v1, /device:TPU:2, one launch (start us, length us, event | category | flops | bytes accessed | tf_op | source)
XLA Modules:
  0.0 147.8 jit_solution(9797070590894153277)
XLA Ops:
  6.5 0.0 all-gather.3.cloned.1.call-start
  6.5 1.3 reshape.22.w_ref
  7.8 1.4 copy.19.off_ref
  9.2 0.0 copy-start.3
  9.2 1.4 copy.20.list_ref
  10.6 2.6 %shard_map.64 = bf16[64,3200]{1,0:T(8,128)(2,1)} custom-call(bf16[64,3072]{1,0:T(8,128)(2,1)} %img_ref.1, s32[64,2]{1,0:T(8,128)} %copy.19.off_ref, s32[64,8]{1,0:T(8,128)} %copy.20.list_ref, f32[1,1536]{1,0:T(1,128)} %reshape.22.w_ref), custom_call_target="tpu_custom_call" | custom-call | tf_op jit(solution)/shard_map/pallas_call | solution.py:88
  13.2 0.0 all-gather.3.cloned.1.call-update
  13.2 1.0 reshape.24
  14.2 0.1 copy.21
  14.3 17.0 %all_to_all.25 = bf16[8,75,48]{1,2,0:T(8,128)(2,1)S(1)} all-to-all(bf16[8,75,48]{1,2,0:T(8,128)(2,1)S(1)} %copy.21), channel_id=1, replica_groups=mesh['y'=4,'xh'=2,'z'=8,'xl'=2,'co'=2] {'z'}, dimensions={0} | all-to-all | bytes 115200 | tf_op jit(solution)/shard_map/all_to_all | solution.py:278
  31.3 0.1 copy.25
  31.5 0.8 broadcast_in_dim.6
  32.3 6.1 %all-to-all-start.1 = ((bf16[8,80,384]{2,1,0:T(8,128)(2,1)}), bf16[8,80,384]{2,1,0:T(8,128)(2,1)S(1)}, u32[]{:S(2)}, u32[]{:S(2)}) async-start(bf16[8,80,384]{2,1,0:T(8,128)(2,1)} %broadcast_in_dim.6), calls=%async_computation.1 | async-start | bytes 983040 | tf_op jit(solution)/shard_map/all_to_all | solution.py:281
  38.4 10.0 %all-to-all-done.1.r_ref = bf16[8,80,384]{2,1,0:T(8,128)(2,1)S(1)} async-done(((bf16[8,80,384]{2,1,0:T(8,128)(2,1)}), bf16[8,80,384]{2,1,0:T(8,128)(2,1)S(1)}, u32[]{:S(2)}, u32[]{:S(2)}) %all-to-all-start.1) | async-done | bytes 491552 | tf_op jit(solution)/shard_map/all_to_all | solution.py:281
  48.4 14.2 %all-gather.3.cloned.1.call-done.p_ref = bf16[512,3200]{1,0:T(8,128)(2,1)} async-done(((bf16[64,3200]{1,0:T(8,128)(2,1)}), bf16[512,3200]{1,0:T(8,128)(2,1)}) %all-gather.3.cloned.1.call-update) | async-done | bytes 3276816 | tf_op jit(solution)/shard_map/all_gather | solution.py:275
  62.7 0.0 copy-start
  62.7 1.9 %copy-done = bf16[512,3200]{1,0:T(8,128)(2,1)S(1)} copy-done((bf16[512,3200]{1,0:T(8,128)(2,1)S(1)}, bf16[512,3200]{1,0:T(8,128)(2,1)}, u32[]{:S(2)}) %copy-start) | copy-done | bytes 3276824
  64.6 0.0 copy-start.2
  64.6 0.8 copy-done.2
  65.4 0.0 copy-start.4
  65.4 0.7 copy-done.4
  66.1 11.3 %shard_map.65 = (f32[2000,512]{1,0:T(8,128)}, f32[2,512]{1,0:T(2,128)S(1)}) custom-call(s32[1]{0:T(128)} %bitcast.base_ref, bf16[512,3200]{1,0:T(8,128)(2,1)S(1)} %copy-done, bf16[8,80,384]{2,1,0:T(8,128)(2,1)S(1)} %all-to-all-done.1.r_ref, f32[8,1536]{1,0:T(8,128)S(1)} %copy-done.2, f32[1,1536]{1,0:T(1,128)S(1)} %copy-done.4), custom_call_target="tpu_custom_call" | custom-call | tf_op jit(solution)/shard_map/pallas_call | solution.py:181
  77.4 14.9 %all_to_all.26.all_ref = f32[32,2,512]{2,1,0:T(2,128)S(1)} all-to-all(f32[32,2,512]{2,1,0:T(2,128)S(1)} %broadcast_in_dim.7), channel_id=1, replica_groups=mesh['y'=4,'xh'=2,'z'=8,'xl'=2,'co'=2] {'z','xl','co'}, dimensions={0} | all-to-all | bytes 262144 | tf_op jit(solution)/shard_map/all_to_all | solution.py:288
  92.3 0.0 copy-done.3
  92.3 0.0 copy-done.1
  92.3 13.9 %shard_map.66 = f32[8,80,384]{2,1,0:T(8,128)S(1)} custom-call(f32[2,512]{1,0:T(2,128)S(1)} %get-tuple-element.7.stat_ref, f32[32,2,512]{2,1,0:T(2,128)S(1)} %all_to_all.26.all_ref, bf16[512,3200]{1,0:T(8,128)(2,1)S(1)} %copy-done.1, f32[2000,512]{1,0:T(8,128)} %get-tuple-element.8.expo_ref, f32[8,1536]{1,0:T(8,128)S(1)} %copy-done.3), custom_call_target="tpu_custom_call" | custom-call | tf_op jit(solution)/shard_map/pallas_call | solution.py:251
  106.2 21.6 %all_to_all.27 = f32[8,80,384]{2,1,0:T(8,128)S(1)} all-to-all(f32[8,80,384]{2,1,0:T(8,128)S(1)} %shard_map.66), channel_id=1, replica_groups=mesh['y'=4,'xh'=2,'z'=8,'xl'=2,'co'=2] {'y','xh'}, dimensions={0} | all-to-all | bytes 1966080 | tf_op jit(solution)/shard_map/all_to_all | solution.py:293
  127.8 0.1 reduce_sum.9
  127.8 0.1 copy.23
  128.0 12.2 %all_to_all.28 = f32[8,48,75]{2,1,0:T(8,128)S(1)} all-to-all(f32[8,48,75]{2,1,0:T(8,128)S(1)} %bitcast.9), channel_id=1, replica_groups=mesh['y'=4,'xh'=2,'z'=8,'xl'=2,'co'=2] {'z'}, dimensions={0} | all-to-all | bytes 230400 | tf_op jit(solution)/shard_map/all_to_all | solution.py:295
  140.1 0.1 copy.24
  140.2 0.8 reshape.27
  (3 shorter events, 0.1 us)
Async XLA Ops:
  6.5 56.1 %all-gather.3.cloned.1.call-start = ((), (), s32[]{:S(2)}) async-start(), calls=%async_computation.5 | async-start | bytes 3686400 | tf_op jit(solution)/shard_map/all_gather | solution.py:275
  9.2 83.1 %copy-start.3 = (f32[8,1536]{1,0:T(8,128)S(1)}, f32[8,1536]{1,0:T(8,128)}, u32[]{:S(2)}) copy-start(f32[8,1536]{1,0:T(8,128)} %constant.25.clone.tab_ref) | copy-start | bytes 147460
  32.3 16.1 %all-to-all-start.1 = ((bf16[8,80,384]{2,1,0:T(8,128)(2,1)}), bf16[8,80,384]{2,1,0:T(8,128)(2,1)S(1)}, u32[]{:S(2)}, u32[]{:S(2)}) async-start(bf16[8,80,384]{2,1,0:T(8,128)(2,1)} %broadcast_in_dim.6), calls=%async_computation.1 | async-start | bytes 983040 | tf_op jit(solution)/shard_map/all_to_all | solution.py:281
  62.7 1.9 %copy-start = (bf16[512,3200]{1,0:T(8,128)(2,1)S(1)}, bf16[512,3200]{1,0:T(8,128)(2,1)}, u32[]{:S(2)}) copy-start(bf16[512,3200]{1,0:T(8,128)(2,1)} %all-gather.3.cloned.1.call-done.p_ref) | copy-start | bytes 9830404
  64.6 0.8 copy-start.2
  65.4 0.7 copy-start.4
  66.1 26.2 %copy-start.1 = (bf16[512,3200]{1,0:T(8,128)(2,1)S(1)}, bf16[512,3200]{1,0:T(8,128)(2,1)}, u32[]{:S(2)}) copy-start(bf16[512,3200]{1,0:T(8,128)(2,1)} %all-gather.3.cloned.1.call-done.p_ref) | copy-start | bytes 9830404
Sparse Core Ops, SparseCore 0:
  13.3 49.2 all-gather.2

commit v2 on v1

v2 whole, which is shorter than its diff:
```python
import functools
import math

import jax
import jax.numpy as jnp
import numpy as np
from jax import lax
from jax.experimental import pallas as pl
from jax.experimental.pallas import tpu as pltpu
from jax.sharding import Mesh, PartitionSpec as P

GRID = 5
BOX = 64
HALF = 1536
WIDTH = 3072
PARTS = 64
ROWS = 75
PAD = 80
LANES = 128
CHUNK = 384
GROUP = 8
NPART = PARTS * GROUP
SHIFTS = GRID * GRID
BLOCK = GRID * PAD
EXCLUDED = -1e30
SCALE = 1.0 / math.sqrt(WIDTH)
AXES = ("y", "xh", "z", "xl", "co")

f32 = jnp.float32
bf16 = jnp.bfloat16


def twiddles():
    k = np.arange(HALF)
    kx = k % BOX - BOX // 2
    ky = k // BOX
    rows = []
    for freq in (kx, ky):
        for g in (1, 2):
            angle = 2.0 * math.pi / BOX * ((g * freq) % BOX)
            rows += [np.cos(angle), np.sin(angle)]
    return np.stack(rows).astype(np.float32)


def sin_cos(turns):
    quarter = jnp.floor(turns * (1.0 / 16.0) + 0.5)
    rest = (turns - 16.0 * quarter) * (2.0 * math.pi / BOX)
    sq = rest * rest
    sin = rest * (
        1.0 + sq * (-1.0 / 6 + sq * (1.0 / 120 + sq * (-1.0 / 5040 + sq * (1.0 / 362880))))
    )
    cos = 1.0 + sq * (
        -0.5 + sq * (1.0 / 24 + sq * (-1.0 / 720 + sq * (1.0 / 40320 + sq * (-1.0 / 3628800))))
    )
    quad = quarter - 4.0 * jnp.floor(quarter * 0.25)
    swap = (quad == 1.0) | (quad == 3.0)
    sin_q = jnp.where(swap, cos, sin)
    cos_q = jnp.where(swap, sin, cos)
    sin_q = jnp.where(quad >= 2.0, -sin_q, sin_q)
    cos_q = jnp.where((quad == 1.0) | (quad == 2.0), -cos_q, cos_q)
    return sin_q, cos_q


def prep_kernel(where_ref, img_ref, offlist_ref, w_ref, out_ref, half_ref):
    eye = jnp.where(
        lax.broadcasted_iota(jnp.int32, (PARTS, PARTS), 0)
        == lax.broadcasted_iota(jnp.int32, (PARTS, PARTS), 1),
        1.0,
        0.0,
    ).astype(bf16)
    small = lax.dot_general(
        eye,
        offlist_ref[...].astype(f32).astype(bf16),
        (((1,), (1,)), ((), ())),
        preferred_element_type=f32,
    )
    ox, oy = small[:, 0:1], small[:, 1:2]
    first = where_ref[2] == 0

    def put(lanes, value):
        value = value.astype(bf16)
        out_ref[:, lanes] = value
        half_ref[:, lanes] = jnp.where(first, value[: PARTS // 2], value[PARTS // 2 :])

    for t in range(HALF // LANES):
        lanes = slice(t * LANES, (t + 1) * LANES)
        ims = slice(HALF + t * LANES, HALF + (t + 1) * LANES)
        k = lax.broadcasted_iota(jnp.int32, (1, LANES), 1) + t * LANES
        kx = ((k & (BOX - 1)) - BOX // 2).astype(f32)
        ky = (k >> 6).astype(f32)
        sin, cos = sin_cos(ox * kx + oy * ky)
        a = img_ref[:, lanes].astype(f32)
        b = img_ref[:, ims].astype(f32)
        w = w_ref[:, lanes]
        put(lanes, w * (a * cos + b * sin))
        put(ims, w * (b * cos - a * sin))
    lane = lax.broadcasted_iota(jnp.int32, (PARTS, LANES), 1).astype(f32)
    listed = small[:, 2:3] == lane
    for n in range(3, small.shape[1]):
        listed = listed | (small[:, n : n + 1] == lane)
    put(slice(WIDTH, WIDTH + LANES), jnp.where(listed, 1.0, 0.0))


def prep(where, images, offlist, weight):
    vmem = pl.BlockSpec(memory_space=pltpu.VMEM)
    return pl.pallas_call(
        prep_kernel,
        in_specs=[pl.BlockSpec(memory_space=pltpu.SMEM), vmem, vmem, vmem],
        out_shape=[
            jax.ShapeDtypeStruct((PARTS, WIDTH + LANES), bf16),
            jax.ShapeDtypeStruct((PARTS // 2, WIDTH + LANES), bf16),
        ],
    )(where, images, offlist, weight)


def y_shift(tab_ref, gy, lanes):
    row = 2 + 2 * abs(gy)
    c = tab_ref[row : row + 1, lanes]
    s = tab_ref[row + 1 : row + 2, lanes]
    return c, (s if gy > 0 else -s)


def shift_kernel(r_ref, tab_ref, w_ref, out_ref, energy_ref):
    step = pl.program_id(0)
    two = (step == 0) | (step == 4)
    zero = step == 2
    sign = jnp.where(step < 2, -1.0, 1.0)

    @pl.when(step == 0)
    def _():
        total = jnp.zeros((PAD, LANES), f32)
        for g in range(GROUP):
            for t in range(CHUNK // LANES):
                r = r_ref[g, :, t * LANES : (t + 1) * LANES].astype(f32)
                at = (g % 4) * CHUNK + t * LANES
                total = total + r * r * w_ref[:, at : at + LANES]
        energy_ref[...] = jnp.broadcast_to(
            0.5 * jnp.sum(total, axis=1, keepdims=True), energy_ref.shape
        )

    for g in range(4):
        for t in range(CHUNK // LANES):
            at = g * CHUNK + t * LANES
            lanes = slice(at, at + LANES)
            ims = slice(HALF + at, HALF + at + LANES)
            rr = r_ref[g, :, t * LANES : (t + 1) * LANES].astype(f32)
            ri = r_ref[g + 4, :, t * LANES : (t + 1) * LANES].astype(f32)
            cy = jnp.where(two, tab_ref[6:7, lanes], tab_ref[4:5, lanes])
            sy = jnp.where(two, tab_ref[7:8, lanes], tab_ref[5:6, lanes]) * sign
            cy, sy = jnp.where(zero, 1.0, cy), jnp.where(zero, 0.0, sy)
            yr = rr * cy - ri * sy
            yi = ri * cy + rr * sy
            out_ref[2 * PAD : 3 * PAD, lanes] = yr.astype(bf16)
            out_ref[2 * PAD : 3 * PAD, ims] = yi.astype(bf16)
            for gx in (1, 2):
                c = tab_ref[2 * gx - 2 : 2 * gx - 1, lanes]
                s = tab_ref[2 * gx - 1 : 2 * gx, lanes]
                cr, ci, sr, si = yr * c, yi * c, yr * s, yi * s
                hi = slice((2 + gx) * PAD, (3 + gx) * PAD)
                lo = slice((2 - gx) * PAD, (3 - gx) * PAD)
                out_ref[hi, lanes] = (cr - si).astype(bf16)
                out_ref[hi, ims] = (ci + sr).astype(bf16)
                out_ref[lo, lanes] = (cr + si).astype(bf16)
                out_ref[lo, ims] = (ci - sr).astype(bf16)


def full(shape):
    return pl.BlockSpec(shape, lambda i: (0,) * len(shape))


def shift_refs(refs, table, weight):
    return pl.pallas_call(
        shift_kernel,
        grid=(GRID,),
        in_specs=[full((GROUP, PAD, CHUNK)), full((8, HALF)), full((1, HALF))],
        out_specs=[pl.BlockSpec((BLOCK, WIDTH), lambda i: (i, 0)), full((PAD, LANES))],
        out_shape=[
            jax.ShapeDtypeStruct((SHIFTS * PAD, WIDTH), bf16),
            jax.ShapeDtypeStruct((PAD, LANES), f32),
        ],
        compiler_params=pltpu.CompilerParams(vmem_limit_bytes=32 << 20),
    )(refs, table, weight)


def block_copies(where_ref, pieces, probes, sem):
    z, co = where_ref[1], where_ref[2]
    half = PARTS // 2
    copies = []
    for n, (ref, far, mine, skip, rows) in enumerate(pieces):
        at = ((z + far + GROUP) & (GROUP - 1)) * PARTS + skip
        if mine is not None:
            at = at + half * (co if mine else 1 - co)
        at = pl.multiple_of(at, 16)
        copies.append(pltpu.make_async_copy(ref, probes.at[pl.ds(at, rows), :], sem.at[n]))
    return copies


def name_pieces(refs):
    half = PARTS // 2
    out = [(refs[0], 0, None, 0, PARTS)]
    for mine, part in ((True, refs[1:9]), (False, refs[9:17])):
        for n, far in enumerate((-1, -2, -3, 1, 2, 3)):
            out.append((part[n], far, mine, 0, half))
        out.append((part[6], 4, mine, 0, half // 2))
        out.append((part[7], 4, mine, half // 2, half // 2))
    return out


PIECES = 17


def estep_kernel(where_ref, *args):
    pieces, (shift_any, energy_ref, expo_ref, stat_ref, probes, shifted, sem, shift_sem) = (
        args[:PIECES],
        args[PIECES:],
    )
    copies = block_copies(where_ref, name_pieces(pieces), probes, sem)
    for c in copies:
        c.start()
    loads = [
        pltpu.make_async_copy(
            shift_any.at[pl.ds(b * BLOCK, BLOCK), :],
            shifted.at[pl.ds(b * BLOCK, BLOCK), :],
            shift_sem.at[b],
        )
        for b in range(GRID)
    ]
    for c in loads:
        c.start()
    row = lax.broadcasted_iota(jnp.int32, (PAD, LANES), 0)
    number = ((where_ref[0] + row) * 2731) >> 16
    lane = lax.broadcasted_iota(jnp.int32, (PAD, LANES), 1)
    pick = jnp.where((number == lane) & (row < ROWS), 1.0, 0.0).astype(bf16)
    half_energy = energy_ref[:, 0:1]
    for c in copies:
        c.wait()
    keep = (
        lax.dot_general(
            pick, probes[:, WIDTH:], (((1,), (1,)), ((), ())), preferred_element_type=f32
        )
        > 0.5
    )
    for b in range(GRID):
        loads[b].wait()
        cross = lax.dot_general(
            shifted[b * BLOCK : (b + 1) * BLOCK, :],
            probes[:, :WIDTH],
            (((1,), (1,)), ((), ())),
            preferred_element_type=f32,
        )
        best = jnp.full((8, NPART), EXCLUDED, f32)
        for gx in range(GRID):
            at = (b * GRID + gx) * PAD
            score = (cross[gx * PAD : (gx + 1) * PAD] - half_energy) * SCALE
            score = jnp.where(keep, score, EXCLUDED)
            expo_ref[at : at + PAD, :] = score
            best = jnp.maximum(best, jnp.max(score.reshape(PAD // 8, 8, NPART), axis=0))
        peak = jnp.max(best, axis=0, keepdims=True)
        mass = jnp.zeros((8, NPART), f32)
        for gx in range(GRID):
            at = (b * GRID + gx) * PAD
            e = jnp.where(keep, jnp.exp(expo_ref[at : at + PAD, :] - peak), 0.0)
            expo_ref[at : at + PAD, :] = e
            mass = mass + jnp.sum(e.reshape(PAD // 8, 8, NPART), axis=0)
        stat_ref[b : b + 1, :] = peak
        stat_ref[8 + b : 9 + b, :] = jnp.sum(mass, axis=0, keepdims=True)
    peaks = [stat_ref[b : b + 1, :] for b in range(GRID)]
    peak = functools.reduce(jnp.maximum, peaks)
    stat_ref[5:6, :] = peak
    stat_ref[6:7, :] = sum(
        stat_ref[8 + b : 9 + b, :] * jnp.exp(peaks[b] - peak) for b in range(GRID)
    )


def estep(where, pieces, shifted, energy):
    vmem = pl.BlockSpec(memory_space=pltpu.VMEM)
    anywhere = pl.BlockSpec(memory_space=pl.ANY)
    return pl.pallas_call(
        estep_kernel,
        in_specs=[pl.BlockSpec(memory_space=pltpu.SMEM)] + [anywhere] * (PIECES + 1) + [vmem],
        out_specs=[vmem, vmem],
        out_shape=[
            jax.ShapeDtypeStruct((SHIFTS * PAD, NPART), f32),
            jax.ShapeDtypeStruct((16, NPART), f32),
        ],
        scratch_shapes=[
            pltpu.VMEM((NPART, WIDTH + LANES), bf16),
            pltpu.VMEM((SHIFTS * PAD, WIDTH), bf16),
            pltpu.SemaphoreType.DMA((PIECES,)),
            pltpu.SemaphoreType.DMA((GRID,)),
        ],
        compiler_params=pltpu.CompilerParams(vmem_limit_bytes=48 << 20),
    )(where, *pieces, shifted, energy)


def mstep_kernel(where_ref, *args):
    pieces, (stat_ref, all_ref, expo_any, tab_ref, out_ref, probes, expo, sums, sem, expo_sem) = (
        args[:PIECES],
        args[PIECES:],
    )
    copies = block_copies(where_ref, name_pieces(pieces), probes, sem)
    for c in copies:
        c.start()
    loads = [
        pltpu.make_async_copy(
            expo_any.at[pl.ds(b * BLOCK, BLOCK), :],
            expo.at[pl.ds(b * BLOCK, BLOCK), :],
            expo_sem.at[b],
        )
        for b in range(GRID)
    ]
    for c in loads:
        c.start()
    count = all_ref.shape[0]
    peak = all_ref[0, 0:1, :]
    for d in range(1, count):
        peak = jnp.maximum(peak, all_ref[d, 0:1, :])
    mass = jnp.zeros((1, NPART), f32)
    for d in range(count):
        mass = mass + all_ref[d, 1:2, :] * jnp.exp(all_ref[d, 0:1, :] - peak)
    inverse = 1.0 / mass
    for c in copies:
        c.wait()
    for b in range(GRID):
        loads[b].wait()
        factor = jnp.exp(stat_ref[b : b + 1, :] - peak) * inverse
        post = (expo[b * BLOCK : (b + 1) * BLOCK, :] * factor).astype(bf16)
        sums[b % 2] = jnp.dot(post, probes[:, :WIDTH], preferred_element_type=f32)
        for g in range(4):
            for t in range(CHUNK // LANES):
                at = g * CHUNK + t * LANES
                lanes = slice(at, at + LANES)
                ims = slice(HALF + at, HALF + at + LANES)
                re = sums[b % 2, 2 * PAD : 3 * PAD, lanes]
                im = sums[b % 2, 2 * PAD : 3 * PAD, ims]
                for gx in (1, 2):
                    c = tab_ref[2 * gx - 2 : 2 * gx - 1, lanes]
                    s = tab_ref[2 * gx - 1 : 2 * gx, lanes]
                    hi = slice((2 + gx) * PAD, (3 + gx) * PAD)
                    lo = slice((2 - gx) * PAD, (3 - gx) * PAD)
                    pr, pi = sums[b % 2, hi, lanes], sums[b % 2, hi, ims]
                    mr, mi = sums[b % 2, lo, lanes], sums[b % 2, lo, ims]
                    re = re + c * (pr + mr) + s * (pi - mi)
                    im = im + c * (pi + mi) - s * (pr - mr)
                if b != 2:
                    cy, sy = y_shift(tab_ref, b - 2, lanes)
                    re, im = re * cy + im * sy, im * cy - re * sy
                chunk = slice(t * LANES, (t + 1) * LANES)
                if b == 0:
                    out_ref[g, :, chunk] = re
                    out_ref[g + 4, :, chunk] = im
                else:
                    out_ref[g, :, chunk] += re
                    out_ref[g + 4, :, chunk] += im


def mstep(where, pieces, stat, stats, expo, table):
    vmem = pl.BlockSpec(memory_space=pltpu.VMEM)
    anywhere = pl.BlockSpec(memory_space=pl.ANY)
    return pl.pallas_call(
        mstep_kernel,
        in_specs=[pl.BlockSpec(memory_space=pltpu.SMEM)]
        + [anywhere] * PIECES
        + [vmem, vmem, anywhere, vmem],
        out_specs=vmem,
        out_shape=jax.ShapeDtypeStruct((GROUP, PAD, CHUNK), f32),
        scratch_shapes=[
            pltpu.VMEM((NPART, WIDTH + LANES), bf16),
            pltpu.VMEM((SHIFTS * PAD, NPART), f32),
            pltpu.VMEM((2, BLOCK, WIDTH), f32),
            pltpu.SemaphoreType.DMA((PIECES,)),
            pltpu.SemaphoreType.DMA((GRID,)),
        ],
        compiler_params=pltpu.CompilerParams(vmem_limit_bytes=48 << 20),
    )(where, *pieces, stat, stats, expo, table)


def along_z(x, far):
    return lax.ppermute(x, "z", [(i, (i + far) % GROUP) for i in range(GROUP)])


def gather_pieces(own, half):
    up, down = [half], [half]
    for _ in range(3):
        up.append(along_z(up[-1], 1))
        down.append(along_z(down[-1], -1))
    cut = PARTS // 4
    mine = up[1:] + down[1:] + [along_z(up[-1][:cut], 1), along_z(down[-1][cut:], -1)]
    other = [lax.ppermute(x, "co", [(0, 1), (1, 0)]) for x in mine]
    return [own] + mine + other


def per_device(images, offsets, class_lists, noise_weight, references):
    weight = noise_weight.reshape(1, HALF)
    table = jnp.asarray(twiddles())
    z, co = lax.axis_index("z"), lax.axis_index("co")
    cls = lax.axis_index("xl") * 2 + co
    where = jnp.stack([cls * (ROWS * GROUP) + z * ROWS, z, co]).astype(jnp.int32)
    offlist = jnp.concatenate([offsets.T, class_lists.T], axis=0)
    own, half = prep(where, images, offlist, weight)
    pieces = gather_pieces(own, half)

    mine = references.reshape(GROUP, ROWS, 48)
    mine = lax.all_to_all(mine, "z", 0, 0)
    mine = jnp.transpose(mine, (1, 0, 2)).reshape(ROWS, CHUNK)
    mine = jnp.pad(mine, ((0, PAD - ROWS), (0, 0)))
    refs = lax.all_to_all(
        jnp.broadcast_to(mine, (GROUP, PAD, CHUNK)), ("y", "xh"), 0, 0
    )
    shifted, energy = shift_refs(refs, table, weight)

    expo, stat = estep(where, pieces, shifted, energy)
    stats = lax.all_to_all(
        jnp.broadcast_to(stat[5:7], (32, 2, NPART)), ("z", "xl", "co"), 0, 0
    )
    sums = mstep(where, pieces, stat, stats, expo, table)

    sums = jnp.sum(lax.all_to_all(sums, ("y", "xh"), 0, 0), axis=0)
    sums = jnp.transpose(sums[:ROWS].reshape(ROWS, GROUP, 48), (1, 2, 0))
    sums = lax.all_to_all(sums, "z", 0, 0)
    return jnp.transpose(sums, (1, 0, 2)).reshape(48, GROUP * ROWS)


def solution(mesh):
    fine = Mesh(mesh.devices.reshape(4, 2, 8, 2, 2), AXES)
    dom, cls = ("y", "xh", "z"), ("xl", "co")
    in_specs = (P(dom, None), P(dom, None), P(dom, None), P(), P(cls, None, dom))
    return jax.shard_map(
        per_device, mesh=fine, in_specs=in_specs, out_specs=P(dom, cls), check_vma=False
    )
```

time: 148 us -> 150 us (1.014)
  starting transfers between devices: 6.13 us -> 20.7 us
  between operations: 13.4 us -> 0.15 us
  waiting for transfers between devices: 24.3 us -> 13.1 us
  Pallas kernels: 27.7 us -> 38.9 us
  blocking collectives: 65.7 us -> 63 us
  other arithmetic: 0.05 us -> 1.97 us
  local copies, waits for them, and re-layouts: 10.5 us -> 12 us
    ppermute x0 -> x16, starting transfers between devices: none -> 14.7 us  [the longest x8 13.7 us: along_z(): return lax.ppermute(x, 'z', [(i, (i + far) % GROUP) for i in range(GROUP)])]
    all_gather x1 -> x0, waiting for transfers between devices: 14.2 us -> none  [per_device(): probes = lax.all_gather(own, 'z').reshape(NPART, WIDTH + LANES)]
    ppermute x0 -> x16, waiting for transfers between devices: none -> 13.1 us  [the longest x8 13.1 us: along_z(): return lax.ppermute(x, 'z', [(i, (i + far) % GROUP) for i in range(GROUP)])]
    pallas_call x3 -> x4, Pallas kernels: 27.7 us -> 38.9 us  [the longest x1 17.3 us: estep(): pl.pallas_call(estep_kernel, in_specs=[pl.BlockSpec(memory_space=pltpu.SM...]
    all_to_all x1, waiting for transfers between devices: 10 us -> 0.01 us  [per_device(): lax.all_to_all(jnp.broadcast_to(mine, (GROUP, PAD, CHUNK)), ('y', 'xh'),...]
    all_to_all x1, blocking collectives: 17 us -> 13 us  [per_device(): mine = lax.all_to_all(mine, 'z', 0, 0)]
  transfers between devices with their start and end apart: 2 -> 17, of which waited for: 2 -> 5; matrix products, arithmetic and copies ran while one was open for 1% -> 1% of each run, Pallas kernels for 0% -> 2%
where the time goes in v2:
time: 150 us
  blocking collectives  63 us (42%)
  Pallas kernels  38.9 us (26%)
  starting transfers between devices  20.7 us (14%)
  waiting for transfers between devices  13.1 us (9%)
  local copies, waits for them, and re-layouts  12 us (8%)
  other arithmetic  1.97 us (1%)
    all_to_all x1, blocking collectives, per_device(): sums = jnp.sum(lax.all_to_all(sums, ('y', 'xh'), 0, 0), axis=0)  22.9 us
    pallas_call x1, Pallas kernels, estep(): pl.pallas_call(estep_kernel, in_specs=[pl.BlockSpec(memory_space=pltpu.SM...  17.3 us
    pallas_call x1, Pallas kernels, mstep(): pl.pallas_call(mstep_kernel, in_specs=[pl.BlockSpec(memory_space=pltpu.SM...  15.2 us
    all_to_all x1, blocking collectives, per_device(): lax.all_to_all(jnp.broadcast_to(stat[5:7], (32, 2, NPART)), ('z', 'xl', '...  14.9 us
    ppermute x8, starting transfers between devices, along_z(): return lax.ppermute(x, 'z', [(i, (i + far) % GROUP) for i in range(GROUP)])  13.7 us
    ppermute x8, waiting for transfers between devices, along_z(): return lax.ppermute(x, 'z', [(i, (i + far) % GROUP) for i in range(GROUP)])  13.1 us
    all_to_all x1, blocking collectives, per_device(): mine = lax.all_to_all(mine, 'z', 0, 0)  13 us
    all_to_all x1, blocking collectives, per_device(): sums = lax.all_to_all(sums, 'z', 0, 0)  12.2 us
  transfers between devices with their start and end apart: 17, of which 5 were waited for; matrix products, arithmetic and copies ran while one was open for 1% of the time, Pallas kernels for 2%

profile of v2, /device:TPU:2, one launch (start us, length us, event | category | flops | bytes accessed | tf_op | source)
XLA Modules:
  0.0 149.7 jit_solution(2921087786186882925)
XLA Ops:
  0.0 1.3 reshape.15.w_ref
  1.3 1.3 pad_add_fusion.offlist_ref
  2.6 0.6 pad_add_fusion.1.where_ref
  3.2 2.9 %shard_map.64 = (bf16[64,3200]{1,0:T(8,128)(2,1)}, bf16[32,3200]{1,0:T(8,128)(2,1)}) custom-call(s32[3]{0:T(128)} %pad_add_fusion.1.where_ref, bf16[64,3072]{1,0:T(8,128)(2,1)} %img_ref.1, s32[10,64]{1,0:T(8,128)} %pad_add_fusion.offlist_ref, f32[1,1536]{1,0:T(1,128)} %reshape.15.w_ref), custom_call_target="tpu_custom_call" | custom-call | tf_op jit(solution)/shard_map/pallas_call | solution.py:106
  6.1 5.9 %collective-permute-start.3 = (bf16[32,3200]{1,0:T(8,128)(2,1)}, bf16[32,3200]{1,0:T(8,128)(2,1)S(1)}, u32[]{:S(2)}, u32[]{:S(2)}) collective-permute-start(bf16[32,3200]{1,0:T(8,128)(2,1)} %get-tuple-element.12), channel_id=1, source_target_pairs={{0,28},{4,0},{8,4},{12,8},{16,12},{20,16},{24,20},{28,24},{1,29},{... | collective-permute-start | bytes 614408 | tf_op jit(solution)/shard_map/ppermute | solution.py:379
  11.9 4.6 %collective-permute-done.3.args_4_ = bf16[32,3200]{1,0:T(8,128)(2,1)S(1)} collective-permute-done((bf16[32,3200]{1,0:T(8,128)(2,1)}, bf16[32,3200]{1,0:T(8,128)(2,1)S(1)}, u32[]{:S(2)}, u32[]{:S(2)}) %collective-permute-start.3) | collective-permute-done | bytes 204832 | tf_op jit(solution)/shard_map/ppermute | solution.py:379
  16.6 3.6 %collective-permute-start.4 = (bf16[32,3200]{1,0:T(8,128)(2,1)S(1)}, bf16[32,3200]{1,0:T(8,128)(2,1)S(1)}, u32[]{:S(2)}, u32[]{:S(2)}) collective-permute-start(bf16[32,3200]{1,0:T(8,128)(2,1)S(1)} %collective-permute-done.3.args_4_), channel_id=1, source_target_pairs={{0,28},{4,0},{8,4},{12,8},{16,12},{20,16},{24,20},{28,24},{1,29},{... | collective-permute-start | bytes 614408 | tf_op jit(solution)/shard_map/ppermute | solution.py:379
  20.2 1.0 reshape.16
  21.3 13.0 %all_to_all.25 = bf16[8,75,48]{1,2,0:T(8,128)(2,1)S(1)} all-to-all(bf16[8,75,48]{1,2,0:T(8,128)(2,1)S(1)} %copy.13), channel_id=1, replica_groups=mesh['y'=4,'xh'=2,'z'=8,'xl'=2,'co'=2] {'z'}, dimensions={0} | all-to-all | bytes 115200 | tf_op jit(solution)/shard_map/all_to_all | solution.py:404
  34.5 0.8 broadcast_in_dim.6
  35.3 6.0 %all-to-all-start.1 = ((bf16[8,80,384]{2,1,0:T(8,128)(2,1)}), bf16[8,80,384]{2,1,0:T(8,128)(2,1)S(1)}, u32[]{:S(2)}, u32[]{:S(2)}) async-start(bf16[8,80,384]{2,1,0:T(8,128)(2,1)} %broadcast_in_dim.6), calls=%async_computation.1 | async-start | bytes 983040 | tf_op jit(solution)/shard_map/all_to_all | solution.py:407
  41.3 0.3 collective-permute-start.5
  41.6 1.8 %collective-permute-start.2 = (bf16[32,3200]{1,0:T(8,128)(2,1)S(1)}, bf16[32,3200]{1,0:T(8,128)(2,1)S(1)}, u32[]{:S(2)}, u32[]{:S(2)}) collective-permute-start(bf16[32,3200]{1,0:T(8,128)(2,1)S(1)} %collective-permute-done.1.args_2_), channel_id=1, source_target_pairs={{0,4},{4,8},{8,12},{12,16},{16,20},{20,24},{24,28},{28,0},{1,5},{5... | collective-permute-start | bytes 614408 | tf_op jit(solution)/shard_map/ppermute | solution.py:379
  43.5 0.5 collective-permute-start.8
  44.0 3.2 %collective-permute-done.5.args_6_ = bf16[32,3200]{1,0:T(8,128)(2,1)S(1)} collective-permute-done((bf16[32,3200]{1,0:T(8,128)(2,1)S(1)}, bf16[32,3200]{1,0:T(8,128)(2,1)S(1)}, u32[]{:S(2)}, u32[]{:S(2)}) %collective-permute-start.5) | collective-permute-done | bytes 204832 | tf_op jit(solution)/shard_map/ppermute | solution.py:379
  47.2 1.4 collective-permute-done.2.args_3_
  48.7 2.0 %collective-permute-start.6 = (bf16[16,3200]{1,0:T(8,128)(2,1)S(1)}, bf16[16,3200]{1,0:T(8,128)(2,1)S(1)}, u32[]{:S(2)}, u32[]{:S(2)}) collective-permute-start(bf16[16,3200]{1,0:T(8,128)(2,1)S(1)} %slice.16), channel_id=1, source_target_pairs={{0,4},{4,8},{8,12},{12,16},{16,20},{20,24},{24,28},{28,0},{1,5},{5... | collective-permute-start | bytes 307208 | tf_op jit(solution)/shard_map/ppermute | solution.py:379
  50.7 0.5 collective-permute-start.10
  51.2 2.0 %collective-permute-done.7.args_8_ = bf16[16,3200]{1,0:T(8,128)(2,1)S(1)} collective-permute-done((bf16[16,3200]{1,0:T(8,128)(2,1)S(1)}, bf16[16,3200]{1,0:T(8,128)(2,1)S(1)}, u32[]{:S(2)}, u32[]{:S(2)}) %collective-permute-start.7) | collective-permute-done | bytes 102432 | tf_op jit(solution)/shard_map/ppermute | solution.py:379
  53.3 1.8 %collective-permute-done.6.args_7_ = bf16[16,3200]{1,0:T(8,128)(2,1)S(1)} collective-permute-done((bf16[16,3200]{1,0:T(8,128)(2,1)S(1)}, bf16[16,3200]{1,0:T(8,128)(2,1)S(1)}, u32[]{:S(2)}, u32[]{:S(2)}) %collective-permute-start.6) | collective-permute-done | bytes 102432 | tf_op jit(solution)/shard_map/ppermute | solution.py:379
  55.0 0.8 copy-done.2
  55.8 0.7 copy-done.4
  56.5 3.4 %shard_map.65 = (bf16[2000,3072]{1,0:T(8,128)(2,1)S(1)}, f32[80,128]{1,0:T(8,128)S(1)}) custom-call(bf16[8,80,384]{2,1,0:T(8,128)(2,1)S(1)} %all-to-all-done.1.r_ref, f32[8,1536]{1,0:T(8,128)S(1)} %copy-done.2, f32[1,1536]{1,0:T(1,128)S(1)} %copy-done.4), custom_call_target="tpu_custom_call" | custom-call | tf_op jit(solution)/shard_map/pallas_call | solution.py:172
  60.0 4.4 %copy-done = bf16[2000,3072]{1,0:T(8,128)(2,1)} copy-done((bf16[2000,3072]{1,0:T(8,128)(2,1)}, bf16[2000,3072]{1,0:T(8,128)(2,1)S(1)}, u32[]{:S(2)}) %copy-start) | copy-done | bytes 12288024
  64.5 1.0 copy-done.1
  65.5 0.6 copy-done.5
  66.1 17.3 %shard_map.66 = (f32[2000,512]{1,0:T(8,128)}, f32[16,512]{1,0:T(8,128)S(1)}) custom-call(s32[3]{0:T(128)S(1)} %copy-done.5, bf16[64,3200]{1,0:T(8,128)(2,1)S(1)} %copy-done.1, bf16[32,3200]{1,0:T(8,128)(2,1)S(1)} %collective-permute-done.args_1_, bf16[32,3200]{1,0:T(8,128)(2,1)S(1)} %collective-permute-done.1.args_2_, ...), custom_call_target="tpu_custom_call" | custom-call | tf_op jit(solution)/shard_map/pallas_call | solution.py:278
  83.5 14.9 %all_to_all.26.args_18_ = f32[32,2,512]{2,1,0:T(2,128)S(1)} all-to-all(f32[32,2,512]{2,1,0:T(2,128)S(1)} %broadcast_in_dim.7), channel_id=1, replica_groups=mesh['y'=4,'xh'=2,'z'=8,'xl'=2,'co'=2] {'z','xl','co'}, dimensions={0} | all-to-all | bytes 262144 | tf_op jit(solution)/shard_map/all_to_all | solution.py:413
  98.3 15.2 %shard_map.67 = f32[8,80,384]{2,1,0:T(8,128)S(1)} custom-call(s32[3]{0:T(128)S(1)} %copy-done.5, bf16[64,3200]{1,0:T(8,128)(2,1)S(1)} %copy-done.1, bf16[32,3200]{1,0:T(8,128)(2,1)S(1)} %collective-permute-done.args_1_, bf16[32,3200]{1,0:T(8,128)(2,1)S(1)} %collective-permute-done.1.args_2_, bf16[32,3200]{1,0:T(8,128)(2,1)S(1)} %collective-permute-done.2.args_3_, ...), custom_call_target="tpu_custom_call" | custom-call | tf_op jit(solution)/shard_map/pallas_call | solution.py:360
  113.6 22.9 %all_to_all.27 = f32[8,80,384]{2,1,0:T(8,128)S(1)} all-to-all(f32[8,80,384]{2,1,0:T(8,128)S(1)} %shard_map.67), channel_id=1, replica_groups=mesh['y'=4,'xh'=2,'z'=8,'xl'=2,'co'=2] {'y','xh'}, dimensions={0} | all-to-all | bytes 1966080 | tf_op jit(solution)/shard_map/all_to_all | solution.py:418
  136.7 12.2 %all_to_all.28 = f32[8,48,75]{2,1,0:T(8,128)S(1)} all-to-all(f32[8,48,75]{2,1,0:T(8,128)S(1)} %bitcast.13), channel_id=1, replica_groups=mesh['y'=4,'xh'=2,'z'=8,'xl'=2,'co'=2] {'z'}, dimensions={0} | all-to-all | bytes 230400 | tf_op jit(solution)/shard_map/all_to_all | solution.py:420
  148.9 0.8 reshape.19
  (38 shorter events, 0.8 us)
Async XLA Ops:
  0.0 98.3 %copy-start.3 = (f32[8,1536]{1,0:T(8,128)S(1)}, f32[8,1536]{1,0:T(8,128)}, u32[]{:S(2)}) copy-start(f32[8,1536]{1,0:T(8,128)} %constant.25.clone.tab_ref.args_20_) | copy-start | bytes 147460
  6.1 10.5 %collective-permute-start.3 = (bf16[32,3200]{1,0:T(8,128)(2,1)}, bf16[32,3200]{1,0:T(8,128)(2,1)S(1)}, u32[]{:S(2)}, u32[]{:S(2)}) collective-permute-start(bf16[32,3200]{1,0:T(8,128)(2,1)} %get-tuple-element.12), channel_id=1, source_target_pairs={{0,28},{4,0},{8,4},{12,8},{16,12},{20,16},{24,20},{28,24},{1,29},{... | collective-permute-start | bytes 614408 | tf_op jit(solution)/shard_map/ppermute | solution.py:379
  11.9 8.2 %collective-permute-start = (bf16[32,3200]{1,0:T(8,128)(2,1)}, bf16[32,3200]{1,0:T(8,128)(2,1)S(1)}, u32[]{:S(2)}, u32[]{:S(2)}) collective-permute-start(bf16[32,3200]{1,0:T(8,128)(2,1)} %get-tuple-element.12), channel_id=1, source_target_pairs={{0,4},{4,8},{8,12},{12,16},{16,20},{20,24},{24,28},{28,0},{1,5},{5... | collective-permute-start | bytes 614408 | tf_op jit(solution)/shard_map/ppermute | solution.py:379
  16.6 24.8 %collective-permute-start.4 = (bf16[32,3200]{1,0:T(8,128)(2,1)S(1)}, bf16[32,3200]{1,0:T(8,128)(2,1)S(1)}, u32[]{:S(2)}, u32[]{:S(2)}) collective-permute-start(bf16[32,3200]{1,0:T(8,128)(2,1)S(1)} %collective-permute-done.3.args_4_), channel_id=1, source_target_pairs={{0,28},{4,0},{8,4},{12,8},{16,12},{20,16},{24,20},{28,24},{1,29},{... | collective-permute-start | bytes 614408 | tf_op jit(solution)/shard_map/ppermute | solution.py:379
  20.2 21.5 %collective-permute-start.1 = (bf16[32,3200]{1,0:T(8,128)(2,1)S(1)}, bf16[32,3200]{1,0:T(8,128)(2,1)S(1)}, u32[]{:S(2)}, u32[]{:S(2)}) collective-permute-start(bf16[32,3200]{1,0:T(8,128)(2,1)S(1)} %collective-permute-done.args_1_), channel_id=1, source_target_pairs={{0,4},{4,8},{8,12},{12,16},{16,20},{20,24},{24,28},{28,0},{1,5},{5... | collective-permute-start | bytes 614408 | tf_op jit(solution)/shard_map/ppermute | solution.py:379
  35.3 19.7 %all-to-all-start.1 = ((bf16[8,80,384]{2,1,0:T(8,128)(2,1)}), bf16[8,80,384]{2,1,0:T(8,128)(2,1)S(1)}, u32[]{:S(2)}, u32[]{:S(2)}) async-start(bf16[8,80,384]{2,1,0:T(8,128)(2,1)} %broadcast_in_dim.6), calls=%async_computation.1 | async-start | bytes 983040 | tf_op jit(solution)/shard_map/all_to_all | solution.py:407
  41.3 5.8 %collective-permute-start.5 = (bf16[32,3200]{1,0:T(8,128)(2,1)S(1)}, bf16[32,3200]{1,0:T(8,128)(2,1)S(1)}, u32[]{:S(2)}, u32[]{:S(2)}) collective-permute-start(bf16[32,3200]{1,0:T(8,128)(2,1)S(1)} %collective-permute-done.4.args_5_), channel_id=1, source_target_pairs={{0,28},{4,0},{8,4},{12,8},{16,12},{20,16},{24,20},{28,24},{1,29},{... | collective-permute-start | bytes 614408 | tf_op jit(solution)/shard_map/ppermute | solution.py:379
  41.6 7.0 %collective-permute-start.2 = (bf16[32,3200]{1,0:T(8,128)(2,1)S(1)}, bf16[32,3200]{1,0:T(8,128)(2,1)S(1)}, u32[]{:S(2)}, u32[]{:S(2)}) collective-permute-start(bf16[32,3200]{1,0:T(8,128)(2,1)S(1)} %collective-permute-done.1.args_2_), channel_id=1, source_target_pairs={{0,4},{4,8},{8,12},{12,16},{16,20},{20,24},{24,28},{28,0},{1,5},{5... | collective-permute-start | bytes 614408 | tf_op jit(solution)/shard_map/ppermute | solution.py:379
  43.5 5.3 %collective-permute-start.11 = (bf16[32,3200]{1,0:T(8,128)(2,1)S(1)}, bf16[32,3200]{1,0:T(8,128)(2,1)S(1)}, u32[]{:S(2)}, u32[]{:S(2)}) collective-permute-start(bf16[32,3200]{1,0:T(8,128)(2,1)S(1)} %collective-permute-done.3.args_4_), channel_id=1, source_target_pairs={{0,1},{1,0},{2,3},{3,2},{4,5},{5,4},{6,7},{7,6},{8,9},{9,8},{10,11... | collective-permute-start | bytes 614408 | tf_op jit(solution)/shard_map/ppermute | solution.py:389
  43.5 7.3 %collective-permute-start.8 = (bf16[32,3200]{1,0:T(8,128)(2,1)S(1)}, bf16[32,3200]{1,0:T(8,128)(2,1)S(1)}, u32[]{:S(2)}, u32[]{:S(2)}) collective-permute-start(bf16[32,3200]{1,0:T(8,128)(2,1)S(1)} %collective-permute-done.args_1_), channel_id=1, source_target_pairs={{0,1},{1,0},{2,3},{3,2},{4,5},{5,4},{6,7},{7,6},{8,9},{9,8},{10,11... | collective-permute-start | bytes 614408 | tf_op jit(solution)/shard_map/ppermute | solution.py:389
  44.0 6.8 %collective-permute-start.12 = (bf16[32,3200]{1,0:T(8,128)(2,1)S(1)}, bf16[32,3200]{1,0:T(8,128)(2,1)S(1)}, u32[]{:S(2)}, u32[]{:S(2)}) collective-permute-start(bf16[32,3200]{1,0:T(8,128)(2,1)S(1)} %collective-permute-done.4.args_5_), channel_id=1, source_target_pairs={{0,1},{1,0},{2,3},{3,2},{4,5},{5,4},{6,7},{7,6},{8,9},{9,8},{10,11... | collective-permute-start | bytes 614408 | tf_op jit(solution)/shard_map/ppermute | solution.py:389
  47.2 17.3 %collective-permute-start.9 = (bf16[32,3200]{1,0:T(8,128)(2,1)S(1)}, bf16[32,3200]{1,0:T(8,128)(2,1)S(1)}, u32[]{:S(2)}, u32[]{:S(2)}) collective-permute-start(bf16[32,3200]{1,0:T(8,128)(2,1)S(1)} %collective-permute-done.1.args_2_), channel_id=1, source_target_pairs={{0,1},{1,0},{2,3},{3,2},{4,5},{5,4},{6,7},{7,6},{8,9},{9,8},{10,11... | collective-permute-start | bytes 614408 | tf_op jit(solution)/shard_map/ppermute | solution.py:389
  48.6 4.7 %collective-permute-start.7 = (bf16[16,3200]{1,0:T(8,128)(2,1)S(1)}, bf16[16,3200]{1,0:T(8,128)(2,1)S(1)}, u32[]{:S(2)}, u32[]{:S(2)}) collective-permute-start(bf16[16,3200]{1,0:T(8,128)(2,1)S(1)} %slice.17), channel_id=1, source_target_pairs={{0,28},{4,0},{8,4},{12,8},{16,12},{20,16},{24,20},{28,24},{1,29},{... | collective-permute-start | bytes 307208 | tf_op jit(solution)/shard_map/ppermute | solution.py:379
  48.7 6.3 %collective-permute-start.6 = (bf16[16,3200]{1,0:T(8,128)(2,1)S(1)}, bf16[16,3200]{1,0:T(8,128)(2,1)S(1)}, u32[]{:S(2)}, u32[]{:S(2)}) collective-permute-start(bf16[16,3200]{1,0:T(8,128)(2,1)S(1)} %slice.16), channel_id=1, source_target_pairs={{0,4},{4,8},{8,12},{12,16},{16,20},{20,24},{24,28},{28,0},{1,5},{5... | collective-permute-start | bytes 307208 | tf_op jit(solution)/shard_map/ppermute | solution.py:379
  50.7 13.7 %collective-permute-start.13 = (bf16[32,3200]{1,0:T(8,128)(2,1)S(1)}, bf16[32,3200]{1,0:T(8,128)(2,1)S(1)}, u32[]{:S(2)}, u32[]{:S(2)}) collective-permute-start(bf16[32,3200]{1,0:T(8,128)(2,1)S(1)} %collective-permute-done.5.args_6_), channel_id=1, source_target_pairs={{0,1},{1,0},{2,3},{3,2},{4,5},{5,4},{6,7},{7,6},{8,9},{9,8},{10,11... | collective-permute-start | bytes 614408 | tf_op jit(solution)/shard_map/ppermute | solution.py:389
  50.7 13.7 %collective-permute-start.10 = (bf16[32,3200]{1,0:T(8,128)(2,1)S(1)}, bf16[32,3200]{1,0:T(8,128)(2,1)S(1)}, u32[]{:S(2)}, u32[]{:S(2)}) collective-permute-start(bf16[32,3200]{1,0:T(8,128)(2,1)S(1)} %collective-permute-done.2.args_3_), channel_id=1, source_target_pairs={{0,1},{1,0},{2,3},{3,2},{4,5},{5,4},{6,7},{7,6},{8,9},{9,8},{10,11... | collective-permute-start | bytes 614408 | tf_op jit(solution)/shard_map/ppermute | solution.py:389
  53.3 11.2 %collective-permute-start.15 = (bf16[16,3200]{1,0:T(8,128)(2,1)S(1)}, bf16[16,3200]{1,0:T(8,128)(2,1)S(1)}, u32[]{:S(2)}, u32[]{:S(2)}) collective-permute-start(bf16[16,3200]{1,0:T(8,128)(2,1)S(1)} %collective-permute-done.7.args_8_), channel_id=1, source_target_pairs={{0,1},{1,0},{2,3},{3,2},{4,5},{5,4},{6,7},{7,6},{8,9},{9,8},{10,11... | collective-permute-start | bytes 307208 | tf_op jit(solution)/shard_map/ppermute | solution.py:389
  55.0 9.4 %collective-permute-start.14 = (bf16[16,3200]{1,0:T(8,128)(2,1)S(1)}, bf16[16,3200]{1,0:T(8,128)(2,1)S(1)}, u32[]{:S(2)}, u32[]{:S(2)}) collective-permute-start(bf16[16,3200]{1,0:T(8,128)(2,1)S(1)} %collective-permute-done.6.args_7_), channel_id=1, source_target_pairs={{0,1},{1,0},{2,3},{3,2},{4,5},{5,4},{6,7},{7,6},{8,9},{9,8},{10,11... | collective-permute-start | bytes 307208 | tf_op jit(solution)/shard_map/ppermute | solution.py:389
  55.0 0.8 copy-start.2
  55.8 0.7 copy-start.4
  60.0 4.4 %copy-start = (bf16[2000,3072]{1,0:T(8,128)(2,1)}, bf16[2000,3072]{1,0:T(8,128)(2,1)S(1)}, u32[]{:S(2)}) copy-start(bf16[2000,3072]{1,0:T(8,128)(2,1)S(1)} %get-tuple-element.13.args_17_) | copy-start | bytes 36864004
  64.5 1.0 copy-start.1
  65.5 0.6 copy-start.5

commit v3 on v2

v3 whole, which is shorter than its diff:
```python
import functools
import math

import jax
import jax.numpy as jnp
from jax import lax
from jax.experimental import pallas as pl
from jax.experimental.pallas import tpu as pltpu
from jax.sharding import Mesh, PartitionSpec as P

GRID = 5
BOX = 64
HALF = 1536
WIDTH = 3072
PARTS = 64
ROWS = 75
PAD = 80
LANES = 128
CHUNK = 384
GROUP = 8
NPART = PARTS * GROUP
SHIFTS = GRID * GRID
BLOCK = GRID * PAD
EXCLUDED = -1e30
SCALE = 1.0 / math.sqrt(WIDTH)
AXES = ("y", "xh", "z", "xl", "co")

f32 = jnp.float32
bf16 = jnp.bfloat16


def sin_cos(turns):
    quarter = jnp.floor(turns * (1.0 / 16.0) + 0.5)
    rest = (turns - 16.0 * quarter) * (2.0 * math.pi / BOX)
    sq = rest * rest
    sin = rest * (
        1.0 + sq * (-1.0 / 6 + sq * (1.0 / 120 + sq * (-1.0 / 5040 + sq * (1.0 / 362880))))
    )
    cos = 1.0 + sq * (
        -0.5 + sq * (1.0 / 24 + sq * (-1.0 / 720 + sq * (1.0 / 40320 + sq * (-1.0 / 3628800))))
    )
    quad = quarter - 4.0 * jnp.floor(quarter * 0.25)
    swap = (quad == 1.0) | (quad == 3.0)
    sin_q = jnp.where(swap, cos, sin)
    cos_q = jnp.where(swap, sin, cos)
    sin_q = jnp.where(quad >= 2.0, -sin_q, sin_q)
    cos_q = jnp.where((quad == 1.0) | (quad == 2.0), -cos_q, cos_q)
    return sin_q, cos_q


def prep_kernel(img_ref, off_ref, list_ref, w_ref, out_ref, half_ref, tab_ref):
    eye = jnp.where(
        lax.broadcasted_iota(jnp.int32, (PARTS, PARTS), 0)
        == lax.broadcasted_iota(jnp.int32, (PARTS, PARTS), 1),
        1.0,
        0.0,
    ).astype(bf16)

    def upright(ref):
        flat = ref[...].astype(f32).astype(bf16)
        return lax.dot_general(eye, flat, (((1,), (1,)), ((), ())), preferred_element_type=f32)

    off = upright(off_ref)
    ox, oy = off[:, 0:1], off[:, 1:2]
    first = lax.axis_index("co") == 0

    def put(lanes, value):
        value = value.astype(bf16)
        out_ref[:, lanes] = value
        half_ref[:, lanes] = jnp.where(first, value[: PARTS // 2], value[PARTS // 2 :])

    for t in range(HALF // LANES):
        lanes = slice(t * LANES, (t + 1) * LANES)
        ims = slice(HALF + t * LANES, HALF + (t + 1) * LANES)
        k = lax.broadcasted_iota(jnp.int32, (1, LANES), 1) + t * LANES
        kx = ((k & (BOX - 1)) - BOX // 2).astype(f32)
        ky = (k >> 6).astype(f32)
        sin, cos = sin_cos(ox * kx + oy * ky)
        a = img_ref[:, lanes].astype(f32)
        b = img_ref[:, ims].astype(f32)
        w = w_ref[lanes].reshape(1, LANES)
        put(lanes, w * (a * cos + b * sin))
        put(ims, w * (b * cos - a * sin))
        step = lax.broadcasted_iota(jnp.int32, (8, 1), 0)
        move = (((step >> 1) & 1) + 1).astype(f32)
        freq = jnp.where(step < 4, kx, ky)
        tab_sin, tab_cos = sin_cos(move * freq)
        tab_ref[0:8, lanes] = jnp.where((step & 1) == 0, tab_cos, tab_sin)
        tab_ref[8:16, lanes] = jnp.broadcast_to(w, (8, LANES))
    lists = upright(list_ref)
    lane = lax.broadcasted_iota(jnp.int32, (PARTS, LANES), 1).astype(f32)
    listed = lists[:, 0:1] == lane
    for n in range(1, lists.shape[1]):
        listed = listed | (lists[:, n : n + 1] == lane)
    put(slice(WIDTH, WIDTH + LANES), jnp.where(listed, 1.0, 0.0))


VMEM = pl.BlockSpec(memory_space=pltpu.VMEM)
ANYWHERE = pl.BlockSpec(memory_space=pl.ANY)


def prep(images, offsets, class_lists, weight):
    return pl.pallas_call(
        prep_kernel,
        in_specs=[VMEM] * 4,
        out_specs=[VMEM] * 3,
        out_shape=[
            jax.ShapeDtypeStruct((PARTS, WIDTH + LANES), bf16),
            jax.ShapeDtypeStruct((PARTS // 2, WIDTH + LANES), bf16),
            jax.ShapeDtypeStruct((16, HALF), f32),
        ],
        compiler_params=pltpu.CompilerParams(vmem_limit_bytes=4 << 20),
    )(images, offsets, class_lists, weight)


def y_shift(tab_ref, gy, lanes):
    row = 2 + 2 * abs(gy)
    c = tab_ref[row : row + 1, lanes]
    s = tab_ref[row + 1 : row + 2, lanes]
    return c, (s if gy > 0 else -s)


def shift_kernel(r_ref, tab_ref, out_ref, energy_ref, total):
    total[...] = jnp.zeros_like(total)

    def chunk(n, carry):
        at = pl.multiple_of(n * LANES, LANES)
        lanes, ims = pl.ds(at, LANES), pl.ds(HALF + at, LANES)
        rr = r_ref[lanes, :].astype(f32).T[:PAD]
        ri = r_ref[ims, :].astype(f32).T[:PAD]
        total[...] += (rr * rr + ri * ri) * tab_ref[8:9, lanes]
        for gy in range(-2, 3):
            yr, yi = rr, ri
            if gy:
                c, s = y_shift(tab_ref, gy, lanes)
                yr, yi = rr * c - ri * s, ri * c + rr * s
            mid = ((gy + 2) * GRID + 2) * PAD
            out_ref[mid : mid + PAD, lanes] = yr.astype(bf16)
            out_ref[mid : mid + PAD, ims] = yi.astype(bf16)
            for gx in (1, 2):
                c = tab_ref[2 * gx - 2 : 2 * gx - 1, lanes]
                s = tab_ref[2 * gx - 1 : 2 * gx, lanes]
                cr, ci, sr, si = yr * c, yi * c, yr * s, yi * s
                hi = slice(mid + gx * PAD, mid + (gx + 1) * PAD)
                lo = slice(mid - gx * PAD, mid - (gx - 1) * PAD)
                out_ref[hi, lanes] = (cr - si).astype(bf16)
                out_ref[hi, ims] = (ci + sr).astype(bf16)
                out_ref[lo, lanes] = (cr + si).astype(bf16)
                out_ref[lo, ims] = (ci - sr).astype(bf16)
        return carry

    lax.fori_loop(0, HALF // LANES, chunk, 0)
    energy_ref[...] = jnp.broadcast_to(
        0.5 * jnp.sum(total[...], axis=1, keepdims=True), energy_ref.shape
    )


def shift_refs(refs, table):
    return pl.pallas_call(
        shift_kernel,
        in_specs=[VMEM] * 2,
        out_specs=[VMEM] * 2,
        out_shape=[
            jax.ShapeDtypeStruct((SHIFTS * PAD, WIDTH), bf16),
            jax.ShapeDtypeStruct((PAD, LANES), f32),
        ],
        scratch_shapes=[pltpu.VMEM((PAD, LANES), f32)],
        compiler_params=pltpu.CompilerParams(vmem_limit_bytes=16 << 20),
    )(refs, table)


def block_copies(pieces, probes, sem):
    z, co = lax.axis_index("z"), lax.axis_index("co")
    half = PARTS // 2
    copies = []
    for n, (ref, far, mine, skip, rows) in enumerate(pieces):
        at = ((z + far + GROUP) & (GROUP - 1)) * PARTS + skip
        if mine is not None:
            at = at + half * (co if mine else 1 - co)
        at = pl.multiple_of(at, 16)
        copies.append(pltpu.make_async_copy(ref, probes.at[pl.ds(at, rows), :], sem.at[n]))
    return copies


def name_pieces(refs):
    half = PARTS // 2
    out = [(refs[0], 0, None, 0, PARTS)]
    for mine, part in ((True, refs[1:9]), (False, refs[9:17])):
        for n, far in enumerate((-1, -2, -3, 1, 2, 3)):
            out.append((part[n], far, mine, 0, half))
        out.append((part[6], 4, mine, 0, half // 2))
        out.append((part[7], 4, mine, half // 2, half // 2))
    return out


PIECES = 17


def estep_kernel(*args):
    pieces, (shifted, energy_ref, probes, expo_ref, stat_ref, sem) = args[:PIECES], args[PIECES:]
    copies = block_copies(name_pieces(pieces), probes, sem)
    for c in copies:
        c.start()
    cls = lax.axis_index("xl") * 2 + lax.axis_index("co")
    base = cls * (ROWS * GROUP) + lax.axis_index("z") * ROWS
    row = lax.broadcasted_iota(jnp.int32, (PAD, LANES), 0)
    number = ((base + row) * 2731) >> 16
    lane = lax.broadcasted_iota(jnp.int32, (PAD, LANES), 1)
    pick = jnp.where((number == lane) & (row < ROWS), 1.0, 0.0).astype(bf16)
    half_energy = energy_ref[:, 0:1]
    for c in copies:
        c.wait()
    keep = (
        lax.dot_general(
            pick, probes[:, WIDTH:], (((1,), (1,)), ((), ())), preferred_element_type=f32
        )
        > 0.5
    )
    for b in range(GRID):
        cross = lax.dot_general(
            shifted[b * BLOCK : (b + 1) * BLOCK, :],
            probes[:, :WIDTH],
            (((1,), (1,)), ((), ())),
            preferred_element_type=f32,
        )
        best = jnp.full((8, NPART), EXCLUDED, f32)
        for gx in range(GRID):
            at = (b * GRID + gx) * PAD
            score = (cross[gx * PAD : (gx + 1) * PAD] - half_energy) * SCALE
            score = jnp.where(keep, score, EXCLUDED)
            expo_ref[at : at + PAD, :] = score
            best = jnp.maximum(best, jnp.max(score.reshape(PAD // 8, 8, NPART), axis=0))
        peak = jnp.max(best, axis=0, keepdims=True)
        mass = jnp.zeros((8, NPART), f32)
        for gx in range(GRID):
            at = (b * GRID + gx) * PAD
            e = jnp.where(keep, jnp.exp(expo_ref[at : at + PAD, :] - peak), 0.0)
            expo_ref[at : at + PAD, :] = e
            mass = mass + jnp.sum(e.reshape(PAD // 8, 8, NPART), axis=0)
        stat_ref[b : b + 1, :] = peak
        stat_ref[8 + b : 9 + b, :] = jnp.sum(mass, axis=0, keepdims=True)
    peaks = [stat_ref[b : b + 1, :] for b in range(GRID)]
    peak = functools.reduce(jnp.maximum, peaks)
    stat_ref[5:6, :] = peak
    stat_ref[6:7, :] = sum(
        stat_ref[8 + b : 9 + b, :] * jnp.exp(peaks[b] - peak) for b in range(GRID)
    )


def estep(pieces, shifted, energy):
    return pl.pallas_call(
        estep_kernel,
        in_specs=[ANYWHERE] * PIECES + [VMEM] * 2,
        out_specs=[VMEM] * 3,
        out_shape=[
            jax.ShapeDtypeStruct((NPART, WIDTH + LANES), bf16),
            jax.ShapeDtypeStruct((SHIFTS * PAD, NPART), f32),
            jax.ShapeDtypeStruct((16, NPART), f32),
        ],
        scratch_shapes=[pltpu.SemaphoreType.DMA((PIECES,))],
        compiler_params=pltpu.CompilerParams(vmem_limit_bytes=26 << 20),
    )(*pieces, shifted, energy)


STRIP = 256


def mstep_kernel(stat_ref, all_ref, p_ref, expo_ref, tab_ref, out_ref, post, sums):
    count = all_ref.shape[0]
    peak = all_ref[0, 0:1, :]
    for d in range(1, count):
        peak = jnp.maximum(peak, all_ref[d, 0:1, :])
    mass = jnp.zeros((1, NPART), f32)
    for d in range(count):
        mass = mass + all_ref[d, 1:2, :] * jnp.exp(all_ref[d, 0:1, :] - peak)
    inverse = 1.0 / mass
    for b in range(GRID):
        rows = slice(b * BLOCK, (b + 1) * BLOCK)
        factor = jnp.exp(stat_ref[b : b + 1, :] - peak) * inverse
        post[rows, :] = (expo_ref[rows, :] * factor).astype(bf16)
    turn = 0
    for strip in range(HALF // STRIP):
        re_cols = slice(strip * STRIP, (strip + 1) * STRIP)
        im_cols = slice(HALF + strip * STRIP, HALF + (strip + 1) * STRIP)
        for b in range(GRID):
            rows = slice(b * BLOCK, (b + 1) * BLOCK)
            k = turn % 2
            turn += 1
            sums[k, :, :STRIP] = jnp.dot(
                post[rows, :], p_ref[:, re_cols], preferred_element_type=f32
            )
            sums[k, :, STRIP:] = jnp.dot(
                post[rows, :], p_ref[:, im_cols], preferred_element_type=f32
            )
            for t in range(STRIP // LANES):
                at = strip * STRIP + t * LANES
                lanes = slice(at, at + LANES)
                res = slice(t * LANES, (t + 1) * LANES)
                ims = slice(STRIP + t * LANES, STRIP + (t + 1) * LANES)
                re = sums[k, 2 * PAD : 3 * PAD, res]
                im = sums[k, 2 * PAD : 3 * PAD, ims]
                for gx in (1, 2):
                    c = tab_ref[2 * gx - 2 : 2 * gx - 1, lanes]
                    s = tab_ref[2 * gx - 1 : 2 * gx, lanes]
                    hi = slice((2 + gx) * PAD, (3 + gx) * PAD)
                    lo = slice((2 - gx) * PAD, (3 - gx) * PAD)
                    pr, pi = sums[k, hi, res], sums[k, hi, ims]
                    mr, mi = sums[k, lo, res], sums[k, lo, ims]
                    re = re + c * (pr + mr) + s * (pi - mi)
                    im = im + c * (pi + mi) - s * (pr - mr)
                if b != 2:
                    cy, sy = y_shift(tab_ref, b - 2, lanes)
                    re, im = re * cy + im * sy, im * cy - re * sy
                g, chunk = at // CHUNK, slice(at % CHUNK, at % CHUNK + LANES)
                if b == 0:
                    out_ref[g, :, chunk] = re
                    out_ref[g + 4, :, chunk] = im
                else:
                    out_ref[g, :, chunk] += re
                    out_ref[g + 4, :, chunk] += im


def mstep(stat, stats, probes, expo, table):
    return pl.pallas_call(
        mstep_kernel,
        in_specs=[VMEM] * 5,
        out_specs=VMEM,
        out_shape=jax.ShapeDtypeStruct((GROUP, PAD, CHUNK), f32),
        scratch_shapes=[
            pltpu.VMEM((SHIFTS * PAD, NPART), bf16),
            pltpu.VMEM((2, BLOCK, 2 * STRIP), f32),
        ],
        compiler_params=pltpu.CompilerParams(vmem_limit_bytes=20 << 20),
    )(stat, stats, probes, expo, table)


def along_z(x, far):
    return lax.ppermute(x, "z", [(i, (i + far) % GROUP) for i in range(GROUP)])


def gather_pieces(own, half):
    up, down = [half], [half]
    for _ in range(3):
        up.append(along_z(up[-1], 1))
        down.append(along_z(down[-1], -1))
    cut = PARTS // 4
    mine = up[1:] + down[1:] + [along_z(up[-1][:cut], 1), along_z(down[-1][cut:], -1)]
    other = [lax.ppermute(x, "co", [(0, 1), (1, 0)]) for x in mine]
    return [own] + mine + other


def per_device(images, offsets, class_lists, noise_weight, references):
    mine = references.reshape(GROUP, ROWS, 48)
    mine = jnp.pad(jnp.transpose(mine, (0, 2, 1)), ((0, 0), (0, 0), (0, PAD - ROWS)))
    mine = jnp.broadcast_to(mine[None], (GROUP, GROUP, 48, PAD)).reshape(-1, 48, PAD)
    refs = lax.all_to_all(mine, ("y", "xh", "z"), 0, 0).reshape(WIDTH, PAD)

    own, half, table = prep(images, offsets.T, class_lists.T, noise_weight)
    pieces = gather_pieces(own, half)
    shifted, energy = shift_refs(refs, table)

    probes, expo, stat = estep(pieces, shifted, energy)
    stats = lax.all_to_all(
        jnp.broadcast_to(stat[5:7], (32, 2, NPART)), ("z", "xl", "co"), 0, 0
    )
    sums = mstep(stat, stats, probes, expo, table)

    sums = jnp.sum(lax.all_to_all(sums, ("y", "xh"), 0, 0), axis=0)
    sums = jnp.transpose(sums[:ROWS].reshape(ROWS, GROUP, 48), (1, 2, 0))
    sums = lax.all_to_all(sums, "z", 0, 0)
    return jnp.transpose(sums, (1, 0, 2)).reshape(48, GROUP * ROWS)


def solution(mesh):
    fine = Mesh(mesh.devices.reshape(4, 2, 8, 2, 2), AXES)
    dom, cls = ("y", "xh", "z"), ("xl", "co")
    in_specs = (P(dom, None), P(dom, None), P(dom, None), P(), P(cls, None, dom))
    return jax.shard_map(
        per_device, mesh=fine, in_specs=in_specs, out_specs=P(dom, cls), check_vma=False
    )
```

time: 150 us -> 141 us (0.940)
  waiting for transfers between devices: 13.1 us -> 30 us
  Pallas kernels: 38.9 us -> 26.1 us
  blocking collectives: 63 us -> 52.8 us
  local copies, waits for them, and re-layouts: 12 us -> 6.19 us
  starting transfers between devices: 20.7 us -> 24.8 us
  other arithmetic: 1.97 us -> 0.05 us
    ppermute x8, waiting for transfers between devices: 13.1 us -> 30 us  [along_z(): return lax.ppermute(x, 'z', [(i, (i + far) % GROUP) for i in range(GROUP)])]
    all_to_all x1 -> x0, blocking collectives: 13 us -> none  [per_device(): mine = lax.all_to_all(mine, 'z', 0, 0)]
    pallas_call x4, Pallas kernels: 38.9 us -> 26.1 us  [the longest x1 12.4 us: estep(): pl.pallas_call(estep_kernel, in_specs=[ANYWHERE] * PIECES + [VMEM] * 2, o...]
    all_to_all x1, starting transfers between devices: 6.03 us -> 13.7 us  [per_device(): refs = lax.all_to_all(mine, ('y', 'xh', 'z'), 0, 0).reshape(WIDTH, PAD)]
    unnamed x13 -> x9, local copies, waits for them, and re-layouts: 7.69 us -> 3.2 us
    ppermute x8, starting transfers between devices: 13.7 us -> 10 us  [along_z(): return lax.ppermute(x, 'z', [(i, (i + far) % GROUP) for i in range(GROUP)])]
    all_to_all x1, blocking collectives: 14.9 us -> 18.1 us  [per_device(): lax.all_to_all(jnp.broadcast_to(stat[5:7], (32, 2, NPART)), ('z', 'xl', '...]
  transfers between devices with their start and end apart: 17 -> 17, of which waited for: 5 -> 6; matrix products, arithmetic and copies ran while one was open for 1% -> 0% of each run, Pallas kernels for 2% -> 4%
where the time goes in v3:
time: 141 us; the launch traced here: 140 us
  blocking collectives  52.8 us (37%)
  waiting for transfers between devices  30 us (21%)
  Pallas kernels  26.1 us (19%)
  starting transfers between devices  24.8 us (18%)
  local copies, waits for them, and re-layouts  6.19 us (4%)
    ppermute x8, waiting for transfers between devices, along_z(): return lax.ppermute(x, 'z', [(i, (i + far) % GROUP) for i in range(GROUP)])  30 us
    all_to_all x1, blocking collectives, per_device(): sums = jnp.sum(lax.all_to_all(sums, ('y', 'xh'), 0, 0), axis=0)  22.6 us
    all_to_all x1, blocking collectives, per_device(): lax.all_to_all(jnp.broadcast_to(stat[5:7], (32, 2, NPART)), ('z', 'xl', '...  18.1 us
    all_to_all x1, starting transfers between devices, per_device(): refs = lax.all_to_all(mine, ('y', 'xh', 'z'), 0, 0).reshape(WIDTH, PAD)  13.7 us
    pallas_call x1, Pallas kernels, estep(): pl.pallas_call(estep_kernel, in_specs=[ANYWHERE] * PIECES + [VMEM] * 2, o...  12.4 us
    all_to_all x1, blocking collectives, per_device(): sums = lax.all_to_all(sums, 'z', 0, 0)  12.2 us
    ppermute x8, starting transfers between devices, along_z(): return lax.ppermute(x, 'z', [(i, (i + far) % GROUP) for i in range(GROUP)])  10 us
    pallas_call x1, Pallas kernels, mstep(): pl.pallas_call(mstep_kernel, in_specs=[VMEM] * 5, out_specs=VMEM, out_sha...  7.41 us
  transfers between devices with their start and end apart: 17, of which 6 were waited for; matrix products, arithmetic and copies ran while one was open for 0% of the time, Pallas kernels for 4%

profile of v3, /device:TPU:2, one launch (start us, length us, event | category | flops | bytes accessed | tf_op | source)
XLA Modules:
  0.0 140.2 jit_solution(9688223310842285329)
XLA Ops:
  0.0 1.0 reshape.16
  1.0 0.1 copy.13
  1.1 1.0 broadcast_in_dim.4
  2.1 13.7 %all-to-all-start = ((bf16[64,48,80]{2,1,0:T(8,128)(2,1)}), bf16[64,48,80]{2,1,0:T(8,128)(2,1)S(1)}, u32[]{:S(2)}, u32[]{:S(2)}) async-start(bf16[64,48,80]{2,1,0:T(8,128)(2,1)} %bitcast.3), calls=%async_computation | async-start | bytes 1572864 | tf_op jit(solution)/shard_map/all_to_all | solution.py:356
  15.8 1.0 copy-done
  16.8 0.7 copy-done.1
  17.5 0.7 copy-done.2
  18.2 0.7 copy-done.3
  18.9 1.0 shard_map.55
  19.8 2.9 %collective-permute-start.3 = (bf16[32,3200]{1,0:T(8,128)(2,1)S(1)}, bf16[32,3200]{1,0:T(8,128)(2,1)S(1)}, u32[]{:S(2)}, u32[]{:S(2)}) collective-permute-start(bf16[32,3200]{1,0:T(8,128)(2,1)S(1)} %get-tuple-element.14), channel_id=1, source_target_pairs={{0,28},{4,0},{8,4},{12,8},{16,12},{20,16},{24,20},{28,24},{1,29},{... | collective-permute-start | bytes 614408 | tf_op jit(solution)/shard_map/ppermute | solution.py:338
  22.7 15.9 %collective-permute-done.3.args_4_ = bf16[32,3200]{1,0:T(8,128)(2,1)S(1)} collective-permute-done((bf16[32,3200]{1,0:T(8,128)(2,1)S(1)}, bf16[32,3200]{1,0:T(8,128)(2,1)S(1)}, u32[]{:S(2)}, u32[]{:S(2)}) %collective-permute-start.3) | collective-permute-done | bytes 204832 | tf_op jit(solution)/shard_map/ppermute | solution.py:338
  38.6 1.8 %collective-permute-start.4 = (bf16[32,3200]{1,0:T(8,128)(2,1)S(1)}, bf16[32,3200]{1,0:T(8,128)(2,1)S(1)}, u32[]{:S(2)}, u32[]{:S(2)}) collective-permute-start(bf16[32,3200]{1,0:T(8,128)(2,1)S(1)} %collective-permute-done.3.args_4_), channel_id=1, source_target_pairs={{0,28},{4,0},{8,4},{12,8},{16,12},{20,16},{24,20},{28,24},{1,29},{... | collective-permute-start | bytes 614408 | tf_op jit(solution)/shard_map/ppermute | solution.py:338
  40.4 0.2 collective-permute-start.1
  40.6 3.9 %collective-permute-done.4.args_5_ = bf16[32,3200]{1,0:T(8,128)(2,1)S(1)} collective-permute-done((bf16[32,3200]{1,0:T(8,128)(2,1)S(1)}, bf16[32,3200]{1,0:T(8,128)(2,1)S(1)}, u32[]{:S(2)}, u32[]{:S(2)}) %collective-permute-start.4) | collective-permute-done | bytes 204832 | tf_op jit(solution)/shard_map/ppermute | solution.py:338
  44.5 3.0 %collective-permute-start.5 = (bf16[32,3200]{1,0:T(8,128)(2,1)S(1)}, bf16[32,3200]{1,0:T(8,128)(2,1)S(1)}, u32[]{:S(2)}, u32[]{:S(2)}) collective-permute-start(bf16[32,3200]{1,0:T(8,128)(2,1)S(1)} %collective-permute-done.4.args_5_), channel_id=1, source_target_pairs={{0,28},{4,0},{8,4},{12,8},{16,12},{20,16},{24,20},{28,24},{1,29},{... | collective-permute-start | bytes 614408 | tf_op jit(solution)/shard_map/ppermute | solution.py:338
  47.5 0.5 collective-permute-start.8
  48.0 0.1 collective-permute-start.12
  48.1 2.7 %collective-permute-done.5.args_6_ = bf16[32,3200]{1,0:T(8,128)(2,1)S(1)} collective-permute-done((bf16[32,3200]{1,0:T(8,128)(2,1)S(1)}, bf16[32,3200]{1,0:T(8,128)(2,1)S(1)}, u32[]{:S(2)}, u32[]{:S(2)}) %collective-permute-start.5) | collective-permute-done | bytes 204832 | tf_op jit(solution)/shard_map/ppermute | solution.py:338
  50.8 3.7 %collective-permute-done.2.args_3_ = bf16[32,3200]{1,0:T(8,128)(2,1)S(1)} collective-permute-done((bf16[32,3200]{1,0:T(8,128)(2,1)S(1)}, bf16[32,3200]{1,0:T(8,128)(2,1)S(1)}, u32[]{:S(2)}, u32[]{:S(2)}) %collective-permute-start.2) | collective-permute-done | bytes 204832 | tf_op jit(solution)/shard_map/ppermute | solution.py:338
  54.5 0.1 collective-permute-start.7
  54.6 2.0 %collective-permute-start.6 = (bf16[16,3200]{1,0:T(8,128)(2,1)S(1)}, bf16[16,3200]{1,0:T(8,128)(2,1)}, u32[]{:S(2)}, u32[]{:S(2)}) collective-permute-start(bf16[16,3200]{1,0:T(8,128)(2,1)S(1)} %slice.16), channel_id=1, source_target_pairs={{0,4},{4,8},{8,12},{12,16},{16,20},{20,24},{24,28},{28,0},{1,5},{5... | collective-permute-start | bytes 307208 | tf_op jit(solution)/shard_map/ppermute | solution.py:338
  56.6 0.5 collective-permute-start.10
  57.1 2.1 %collective-permute-done.7.args_8_ = bf16[16,3200]{1,0:T(8,128)(2,1)} collective-permute-done((bf16[16,3200]{1,0:T(8,128)(2,1)S(1)}, bf16[16,3200]{1,0:T(8,128)(2,1)}, u32[]{:S(2)}, u32[]{:S(2)}) %collective-permute-start.7) | collective-permute-done | bytes 102432 | tf_op jit(solution)/shard_map/ppermute | solution.py:338
  59.2 1.8 %collective-permute-done.6.args_7_ = bf16[16,3200]{1,0:T(8,128)(2,1)} collective-permute-done((bf16[16,3200]{1,0:T(8,128)(2,1)S(1)}, bf16[16,3200]{1,0:T(8,128)(2,1)}, u32[]{:S(2)}, u32[]{:S(2)}) %collective-permute-start.6) | collective-permute-done | bytes 102432 | tf_op jit(solution)/shard_map/ppermute | solution.py:338
  61.0 5.3 %shard_map.56 = (bf16[2000,3072]{1,0:T(8,128)(2,1)S(1)}, f32[80,128]{1,0:T(8,128)S(1)}) custom-call(bf16[3072,80]{1,0:T(8,128)(2,1)S(1)} %bitcast.10, f32[16,1536]{1,0:T(8,128)S(1)} %get-tuple-element.15.tab_ref), custom_call_target="tpu_custom_call" | custom-call | tf_op jit(solution)/shard_map/pallas_call | solution.py:159
  66.4 12.4 %shard_map.57 = (bf16[512,3200]{1,0:T(8,128)(2,1)S(1)}, f32[2000,512]{1,0:T(8,128)S(1)}, f32[16,512]{1,0:T(8,128)S(1)}) custom-call(bf16[64,3200]{1,0:T(8,128)(2,1)S(1)} %get-tuple-element.13.args_0_, bf16[32,3200]{1,0:T(8,128)(2,1)S(1)} %collective-permute-done.args_1_, bf16[32,3200]{1,0:T(8,128)(2,1)S(1)} %collective-permute-done.1.args_2_, ...), custom_call_target="tpu_custom_call" | custom-call | tf_op jit(solution)/shard_map/pallas_call | solution.py:251
  78.9 18.1 %all_to_all.20.all_ref = f32[32,2,512]{2,1,0:T(2,128)S(1)} all-to-all(f32[32,2,512]{2,1,0:T(2,128)S(1)} %broadcast_in_dim.10), channel_id=1, replica_groups=mesh['y'=4,'xh'=2,'z'=8,'xl'=2,'co'=2] {'z','xl','co'}, dimensions={0} | all-to-all | bytes 262144 | tf_op jit(solution)/shard_map/all_to_all | solution.py:363
  96.9 7.4 %shard_map.58 = f32[8,80,384]{2,1,0:T(8,128)S(1)} custom-call(f32[16,512]{1,0:T(8,128)S(1)} %get-tuple-element.18.stat_ref, f32[32,2,512]{2,1,0:T(2,128)S(1)} %all_to_all.20.all_ref, bf16[512,3200]{1,0:T(8,128)(2,1)S(1)} %get-tuple-element.19.p_ref, f32[2000,512]{1,0:T(8,128)S(1)} %get-tuple-element.20.expo_ref, f32[16,1536]{1,0:T(8,128)S(1)} %get-tuple-element.15.tab_ref), custom_call_target="tpu_custom_call" | custom-call | tf_op jit(solution)/shard_map/pallas_call | solution.py:324
  104.3 22.6 %all_to_all.21 = f32[8,80,384]{2,1,0:T(8,128)S(1)} all-to-all(f32[8,80,384]{2,1,0:T(8,128)S(1)} %shard_map.58), channel_id=1, replica_groups=mesh['y'=4,'xh'=2,'z'=8,'xl'=2,'co'=2] {'y','xh'}, dimensions={0} | all-to-all | bytes 1966080 | tf_op jit(solution)/shard_map/all_to_all | solution.py:368
  127.0 0.1 copy.11
  127.1 12.2 %all_to_all.22 = f32[8,48,75]{2,1,0:T(8,128)S(1)} all-to-all(f32[8,48,75]{2,1,0:T(8,128)S(1)} %bitcast.13), channel_id=1, replica_groups=mesh['y'=4,'xh'=2,'z'=8,'xl'=2,'co'=2] {'z'}, dimensions={0} | all-to-all | bytes 230400 | tf_op jit(solution)/shard_map/all_to_all | solution.py:370
  139.4 0.8 reshape.20
  (29 shorter events, 0.3 us)
Async XLA Ops:
  2.1 58.9 %all-to-all-start = ((bf16[64,48,80]{2,1,0:T(8,128)(2,1)}), bf16[64,48,80]{2,1,0:T(8,128)(2,1)S(1)}, u32[]{:S(2)}, u32[]{:S(2)}) async-start(bf16[64,48,80]{2,1,0:T(8,128)(2,1)} %bitcast.3), calls=%async_computation | async-start | bytes 1572864 | tf_op jit(solution)/shard_map/all_to_all | solution.py:356
  15.8 1.0 copy-start
  16.8 0.7 copy-start.1
  17.5 0.7 copy-start.2
  18.2 0.7 copy-start.3
  19.8 18.7 %collective-permute-start.3 = (bf16[32,3200]{1,0:T(8,128)(2,1)S(1)}, bf16[32,3200]{1,0:T(8,128)(2,1)S(1)}, u32[]{:S(2)}, u32[]{:S(2)}) collective-permute-start(bf16[32,3200]{1,0:T(8,128)(2,1)S(1)} %get-tuple-element.14), channel_id=1, source_target_pairs={{0,28},{4,0},{8,4},{12,8},{16,12},{20,16},{24,20},{28,24},{1,29},{... | collective-permute-start | bytes 614408 | tf_op jit(solution)/shard_map/ppermute | solution.py:338
  22.7 17.7 %collective-permute-start = (bf16[32,3200]{1,0:T(8,128)(2,1)S(1)}, bf16[32,3200]{1,0:T(8,128)(2,1)S(1)}, u32[]{:S(2)}, u32[]{:S(2)}) collective-permute-start(bf16[32,3200]{1,0:T(8,128)(2,1)S(1)} %get-tuple-element.14), channel_id=1, source_target_pairs={{0,4},{4,8},{8,12},{12,16},{16,20},{20,24},{24,28},{28,0},{1,5},{5... | collective-permute-start | bytes 614408 | tf_op jit(solution)/shard_map/ppermute | solution.py:338
  38.6 5.9 %collective-permute-start.4 = (bf16[32,3200]{1,0:T(8,128)(2,1)S(1)}, bf16[32,3200]{1,0:T(8,128)(2,1)S(1)}, u32[]{:S(2)}, u32[]{:S(2)}) collective-permute-start(bf16[32,3200]{1,0:T(8,128)(2,1)S(1)} %collective-permute-done.3.args_4_), channel_id=1, source_target_pairs={{0,28},{4,0},{8,4},{12,8},{16,12},{20,16},{24,20},{28,24},{1,29},{... | collective-permute-start | bytes 614408 | tf_op jit(solution)/shard_map/ppermute | solution.py:338
  40.4 7.1 %collective-permute-start.1 = (bf16[32,3200]{1,0:T(8,128)(2,1)S(1)}, bf16[32,3200]{1,0:T(8,128)(2,1)S(1)}, u32[]{:S(2)}, u32[]{:S(2)}) collective-permute-start(bf16[32,3200]{1,0:T(8,128)(2,1)S(1)} %collective-permute-done.args_1_), channel_id=1, source_target_pairs={{0,4},{4,8},{8,12},{12,16},{16,20},{20,24},{24,28},{28,0},{1,5},{5... | collective-permute-start | bytes 614408 | tf_op jit(solution)/shard_map/ppermute | solution.py:338
  44.5 6.3 %collective-permute-start.5 = (bf16[32,3200]{1,0:T(8,128)(2,1)S(1)}, bf16[32,3200]{1,0:T(8,128)(2,1)S(1)}, u32[]{:S(2)}, u32[]{:S(2)}) collective-permute-start(bf16[32,3200]{1,0:T(8,128)(2,1)S(1)} %collective-permute-done.4.args_5_), channel_id=1, source_target_pairs={{0,28},{4,0},{8,4},{12,8},{16,12},{20,16},{24,20},{28,24},{1,29},{... | collective-permute-start | bytes 614408 | tf_op jit(solution)/shard_map/ppermute | solution.py:338
  47.5 7.0 %collective-permute-start.2 = (bf16[32,3200]{1,0:T(8,128)(2,1)S(1)}, bf16[32,3200]{1,0:T(8,128)(2,1)S(1)}, u32[]{:S(2)}, u32[]{:S(2)}) collective-permute-start(bf16[32,3200]{1,0:T(8,128)(2,1)S(1)} %collective-permute-done.1.args_2_), channel_id=1, source_target_pairs={{0,4},{4,8},{8,12},{12,16},{16,20},{20,24},{24,28},{28,0},{1,5},{5... | collective-permute-start | bytes 614408 | tf_op jit(solution)/shard_map/ppermute | solution.py:338
  47.5 7.1 %collective-permute-start.11 = (bf16[32,3200]{1,0:T(8,128)(2,1)S(1)}, bf16[32,3200]{1,0:T(8,128)(2,1)S(1)}, u32[]{:S(2)}, u32[]{:S(2)}) collective-permute-start(bf16[32,3200]{1,0:T(8,128)(2,1)S(1)} %collective-permute-done.3.args_4_), channel_id=1, source_target_pairs={{0,1},{1,0},{2,3},{3,2},{4,5},{5,4},{6,7},{7,6},{8,9},{9,8},{10,11... | collective-permute-start | bytes 614408 | tf_op jit(solution)/shard_map/ppermute | solution.py:348
  47.5 9.1 %collective-permute-start.8 = (bf16[32,3200]{1,0:T(8,128)(2,1)S(1)}, bf16[32,3200]{1,0:T(8,128)(2,1)S(1)}, u32[]{:S(2)}, u32[]{:S(2)}) collective-permute-start(bf16[32,3200]{1,0:T(8,128)(2,1)S(1)} %collective-permute-done.args_1_), channel_id=1, source_target_pairs={{0,1},{1,0},{2,3},{3,2},{4,5},{5,4},{6,7},{7,6},{8,9},{9,8},{10,11... | collective-permute-start | bytes 614408 | tf_op jit(solution)/shard_map/ppermute | solution.py:348
  48.0 8.6 %collective-permute-start.12 = (bf16[32,3200]{1,0:T(8,128)(2,1)S(1)}, bf16[32,3200]{1,0:T(8,128)(2,1)S(1)}, u32[]{:S(2)}, u32[]{:S(2)}) collective-permute-start(bf16[32,3200]{1,0:T(8,128)(2,1)S(1)} %collective-permute-done.4.args_5_), channel_id=1, source_target_pairs={{0,1},{1,0},{2,3},{3,2},{4,5},{5,4},{6,7},{7,6},{8,9},{9,8},{10,11... | collective-permute-start | bytes 614408 | tf_op jit(solution)/shard_map/ppermute | solution.py:348
  50.8 15.5 %collective-permute-start.9 = (bf16[32,3200]{1,0:T(8,128)(2,1)S(1)}, bf16[32,3200]{1,0:T(8,128)(2,1)S(1)}, u32[]{:S(2)}, u32[]{:S(2)}) collective-permute-start(bf16[32,3200]{1,0:T(8,128)(2,1)S(1)} %collective-permute-done.1.args_2_), channel_id=1, source_target_pairs={{0,1},{1,0},{2,3},{3,2},{4,5},{5,4},{6,7},{7,6},{8,9},{9,8},{10,11... | collective-permute-start | bytes 614408 | tf_op jit(solution)/shard_map/ppermute | solution.py:348
  54.5 4.8 %collective-permute-start.7 = (bf16[16,3200]{1,0:T(8,128)(2,1)S(1)}, bf16[16,3200]{1,0:T(8,128)(2,1)}, u32[]{:S(2)}, u32[]{:S(2)}) collective-permute-start(bf16[16,3200]{1,0:T(8,128)(2,1)S(1)} %slice.17), channel_id=1, source_target_pairs={{0,28},{4,0},{8,4},{12,8},{16,12},{20,16},{24,20},{28,24},{1,29},{... | collective-permute-start | bytes 307208 | tf_op jit(solution)/shard_map/ppermute | solution.py:338
  54.6 6.4 %collective-permute-start.6 = (bf16[16,3200]{1,0:T(8,128)(2,1)S(1)}, bf16[16,3200]{1,0:T(8,128)(2,1)}, u32[]{:S(2)}, u32[]{:S(2)}) collective-permute-start(bf16[16,3200]{1,0:T(8,128)(2,1)S(1)} %slice.16), channel_id=1, source_target_pairs={{0,4},{4,8},{8,12},{12,16},{16,20},{20,24},{24,28},{28,0},{1,5},{5... | collective-permute-start | bytes 307208 | tf_op jit(solution)/shard_map/ppermute | solution.py:338
  56.6 9.7 %collective-permute-start.13 = (bf16[32,3200]{1,0:T(8,128)(2,1)S(1)}, bf16[32,3200]{1,0:T(8,128)(2,1)S(1)}, u32[]{:S(2)}, u32[]{:S(2)}) collective-permute-start(bf16[32,3200]{1,0:T(8,128)(2,1)S(1)} %collective-permute-done.5.args_6_), channel_id=1, source_target_pairs={{0,1},{1,0},{2,3},{3,2},{4,5},{5,4},{6,7},{7,6},{8,9},{9,8},{10,11... | collective-permute-start | bytes 614408 | tf_op jit(solution)/shard_map/ppermute | solution.py:348
  56.6 9.7 %collective-permute-start.10 = (bf16[32,3200]{1,0:T(8,128)(2,1)S(1)}, bf16[32,3200]{1,0:T(8,128)(2,1)}, u32[]{:S(2)}, u32[]{:S(2)}) collective-permute-start(bf16[32,3200]{1,0:T(8,128)(2,1)S(1)} %collective-permute-done.2.args_3_), channel_id=1, source_target_pairs={{0,1},{1,0},{2,3},{3,2},{4,5},{5,4},{6,7},{7,6},{8,9},{9,8},{10,11... | collective-permute-start | bytes 614408 | tf_op jit(solution)/shard_map/ppermute | solution.py:348
  59.2 7.1 %collective-permute-start.15 = (bf16[16,3200]{1,0:T(8,128)(2,1)}, bf16[16,3200]{1,0:T(8,128)(2,1)}, u32[]{:S(2)}, u32[]{:S(2)}) collective-permute-start(bf16[16,3200]{1,0:T(8,128)(2,1)} %collective-permute-done.7.args_8_), channel_id=1, source_target_pairs={{0,1},{1,0},{2,3},{3,2},{4,5},{5,4},{6,7},{7,6},{8,9},{9,8},{10,11... | collective-permute-start | bytes 307208 | tf_op jit(solution)/shard_map/ppermute | solution.py:348
  61.0 5.3 %collective-permute-start.14 = (bf16[16,3200]{1,0:T(8,128)(2,1)}, bf16[16,3200]{1,0:T(8,128)(2,1)}, u32[]{:S(2)}, u32[]{:S(2)}) collective-permute-start(bf16[16,3200]{1,0:T(8,128)(2,1)} %collective-permute-done.6.args_7_), channel_id=1, source_target_pairs={{0,1},{1,0},{2,3},{3,2},{4,5},{5,4},{6,7},{7,6},{8,9},{9,8},{10,11... | collective-permute-start | bytes 307208 | tf_op jit(solution)/shard_map/ppermute | solution.py:348

commit v4 on v3

--- a/solution.py
+++ b/solution.py
@@ -96,7 +96,6 @@
 
 
 VMEM = pl.BlockSpec(memory_space=pltpu.VMEM)
-ANYWHERE = pl.BlockSpec(memory_space=pl.ANY)
 
 
 def prep(images, offsets, class_lists, weight):
@@ -109,7 +108,7 @@
             jax.ShapeDtypeStruct((PARTS // 2, WIDTH + LANES), bf16),
             jax.ShapeDtypeStruct((16, HALF), f32),
         ],
-        compiler_params=pltpu.CompilerParams(vmem_limit_bytes=4 << 20),
+        cost_estimate=pl.CostEstimate(flops=4 << 20, bytes_accessed=1 << 20, transcendentals=0),
     )(images, offsets, class_lists, weight)
 
 
@@ -166,20 +165,18 @@
         ],
         scratch_shapes=[pltpu.VMEM((PAD, LANES), f32)],
         compiler_params=pltpu.CompilerParams(vmem_limit_bytes=16 << 20),
+        cost_estimate=pl.CostEstimate(flops=40 << 20, bytes_accessed=14 << 20, transcendentals=0),
     )(refs, table)
 
 
-def block_copies(pieces, probes, sem):
+def assemble(pieces, probes):
     z, co = lax.axis_index("z"), lax.axis_index("co")
     half = PARTS // 2
-    copies = []
-    for n, (ref, far, mine, skip, rows) in enumerate(pieces):
+    for ref, far, mine, skip, rows in pieces:
         at = ((z + far + GROUP) & (GROUP - 1)) * PARTS + skip
         if mine is not None:
             at = at + half * (co if mine else 1 - co)
-        at = pl.multiple_of(at, 16)
-        copies.append(pltpu.make_async_copy(ref, probes.at[pl.ds(at, rows), :], sem.at[n]))
-    return copies
+        probes[pl.ds(pl.multiple_of(at, 16), rows), :] = ref[...]
 
 
 def name_pieces(refs):
@@ -197,10 +194,8 @@
 
 
 def estep_kernel(*args):
-    pieces, (shifted, energy_ref, probes, expo_ref, stat_ref, sem) = args[:PIECES], args[PIECES:]
-    copies = block_copies(name_pieces(pieces), probes, sem)
-    for c in copies:
-        c.start()
+    pieces, (shifted, energy_ref, probes, expo_ref, stat_ref) = args[:PIECES], args[PIECES:]
+    assemble(name_pieces(pieces), probes)
     cls = lax.axis_index("xl") * 2 + lax.axis_index("co")
     base = cls * (ROWS * GROUP) + lax.axis_index("z") * ROWS
     row = lax.broadcasted_iota(jnp.int32, (PAD, LANES), 0)
@@ -208,8 +203,6 @@
     lane = lax.broadcasted_iota(jnp.int32, (PAD, LANES), 1)
     pick = jnp.where((number == lane) & (row < ROWS), 1.0, 0.0).astype(bf16)
     half_energy = energy_ref[:, 0:1]
-    for c in copies:
-        c.wait()
     keep = (
         lax.dot_general(
             pick, probes[:, WIDTH:], (((1,), (1,)), ((), ())), preferred_element_type=f32
@@ -250,15 +243,19 @@
 def estep(pieces, shifted, energy):
     return pl.pallas_call(
         estep_kernel,
-        in_specs=[ANYWHERE] * PIECES + [VMEM] * 2,
+        in_specs=[VMEM] * (PIECES + 2),
         out_specs=[VMEM] * 3,
         out_shape=[
             jax.ShapeDtypeStruct((NPART, WIDTH + LANES), bf16),
             jax.ShapeDtypeStruct((SHIFTS * PAD, NPART), f32),
             jax.ShapeDtypeStruct((16, NPART), f32),
         ],
-        scratch_shapes=[pltpu.SemaphoreType.DMA((PIECES,))],
-        compiler_params=pltpu.CompilerParams(vmem_limit_bytes=26 << 20),
+        compiler_params=pltpu.CompilerParams(vmem_limit_bytes=30 << 20),
+        cost_estimate=pl.CostEstimate(
+            flops=2 * SHIFTS * PAD * NPART * WIDTH,
+            bytes_accessed=24 << 20,
+            transcendentals=SHIFTS * PAD * NPART,
+        ),
     )(*pieces, shifted, energy)
 
 
@@ -331,6 +328,9 @@
             pltpu.VMEM((2, BLOCK, 2 * STRIP), f32),
         ],
         compiler_params=pltpu.CompilerParams(vmem_limit_bytes=20 << 20),
+        cost_estimate=pl.CostEstimate(
+            flops=2 * SHIFTS * PAD * NPART * WIDTH, bytes_accessed=9 << 20, transcendentals=0
+        ),
     )(stat, stats, probes, expo, table)
 
 
@@ -351,9 +351,10 @@
 
 def per_device(images, offsets, class_lists, noise_weight, references):
     mine = references.reshape(GROUP, ROWS, 48)
-    mine = jnp.pad(jnp.transpose(mine, (0, 2, 1)), ((0, 0), (0, 0), (0, PAD - ROWS)))
-    mine = jnp.broadcast_to(mine[None], (GROUP, GROUP, 48, PAD)).reshape(-1, 48, PAD)
-    refs = lax.all_to_all(mine, ("y", "xh", "z"), 0, 0).reshape(WIDTH, PAD)
+    mine = jnp.pad(jnp.transpose(mine, (0, 2, 1)), ((0, 0), (0, 0), (0, LANES - ROWS)))
+    mine = lax.all_to_all(mine, "z", 0, 0).reshape(CHUNK, LANES)
+    mine = jnp.broadcast_to(mine, (GROUP, CHUNK, LANES))
+    refs = lax.all_to_all(mine, ("y", "xh"), 0, 0).reshape(WIDTH, LANES)
 
     own, half, table = prep(images, offsets.T, class_lists.T, noise_weight)
     pieces = gather_pieces(own, half)
@@ -366,8 +367,8 @@
     sums = mstep(stat, stats, probes, expo, table)
 
     sums = jnp.sum(lax.all_to_all(sums, ("y", "xh"), 0, 0), axis=0)
-    sums = jnp.transpose(sums[:ROWS].reshape(ROWS, GROUP, 48), (1, 2, 0))
-    sums = lax.all_to_all(sums, "z", 0, 0)
+    sums = jnp.pad(sums.T, ((0, 0), (0, LANES - PAD))).reshape(GROUP, 48, LANES)
+    sums = lax.all_to_all(sums, "z", 0, 0)[:, :, :ROWS]
     return jnp.transpose(sums, (1, 0, 2)).reshape(48, GROUP * ROWS)
 
 

time: 141 us -> 123 us (0.87)
  waiting for transfers between devices: 30 us -> 16.4 us
  blocking collectives: 52.8 us -> 50.4 us
  Pallas kernels: 26.1 us -> 24.3 us
    ppermute x8, waiting for transfers between devices: 30 us -> 13.7 us  [along_z(): return lax.ppermute(x, 'z', [(i, (i + far) % GROUP) for i in range(GROUP)])]
    pallas_call x1, Pallas kernels: 12.4 us -> 8.8 us  [estep(): pl.pallas_call(estep_kernel, in_specs=[VMEM] * (PIECES + 2), out_specs=[V...]
    all_to_all x1, blocking collectives: 18.1 us -> 15.3 us  [per_device(): lax.all_to_all(jnp.broadcast_to(stat[5:7], (32, 2, NPART)), ('z', 'xl', '...]
    all_to_all x1 -> x2, waiting for transfers between devices: 0.01 us -> 2.65 us  [the longest x1 2.65 us: per_device(): mine = lax.all_to_all(mine, 'z', 0, 0).reshape(CHUNK, LANES)]
    pallas_call x1, Pallas kernels: 0.98 us -> 2.84 us  [prep(): pl.pallas_call(prep_kernel, in_specs=[VMEM] * 4, out_specs=[VMEM] * 3, ou...]
    unnamed x9 -> x8, local copies, waits for them, and re-layouts: 3.2 us -> 2.16 us
    all_to_all x1 -> x2, starting transfers between devices: 13.7 us -> 14.5 us  [the longest x1 8.47 us: per_device(): mine = lax.all_to_all(mine, 'z', 0, 0).reshape(CHUNK, LANES)]
  transfers between devices with their start and end apart: 17 -> 18, of which waited for: 6 -> 6; matrix products, arithmetic and copies ran while one was open for 0% -> 1% of each run, Pallas kernels for 4% -> 7%
where the time goes in v4:
time: 123 us; the launch traced here: 122 us
  blocking collectives  50.4 us (41%)
  starting transfers between devices  25 us (20%)
  Pallas kernels  24.3 us (20%)
  waiting for transfers between devices  16.4 us (13%)
  local copies, waits for them, and re-layouts  5.68 us (5%)
    all_to_all x1, blocking collectives, per_device(): sums = jnp.sum(lax.all_to_all(sums, ('y', 'xh'), 0, 0), axis=0)  22.9 us
    all_to_all x1, blocking collectives, per_device(): lax.all_to_all(jnp.broadcast_to(stat[5:7], (32, 2, NPART)), ('z', 'xl', '...  15.3 us
    ppermute x8, waiting for transfers between devices, along_z(): return lax.ppermute(x, 'z', [(i, (i + far) % GROUP) for i in range(GROUP)])  13.7 us
    all_to_all x1, blocking collectives, per_device(): sums = lax.all_to_all(sums, 'z', 0, 0)[:, :, :ROWS]  12.2 us
    ppermute x8, starting transfers between devices, along_z(): return lax.ppermute(x, 'z', [(i, (i + far) % GROUP) for i in range(GROUP)])  9.47 us
    pallas_call x1, Pallas kernels, estep(): pl.pallas_call(estep_kernel, in_specs=[VMEM] * (PIECES + 2), out_specs=[V...  8.8 us
    all_to_all x1, starting transfers between devices, per_device(): mine = lax.all_to_all(mine, 'z', 0, 0).reshape(CHUNK, LANES)  8.47 us
    pallas_call x1, Pallas kernels, mstep(): pl.pallas_call(mstep_kernel, in_specs=[VMEM] * 5, out_specs=VMEM, out_sha...  7.43 us
  transfers between devices with their start and end apart: 18, of which 6 were waited for; matrix products, arithmetic and copies ran while one was open for 1% of the time, Pallas kernels for 7%

profile of v4, /device:TPU:2, one launch (start us, length us, event | category | flops | bytes accessed | tf_op | source)
XLA Modules:
  0.0 122.1 jit_solution(9450758067958541185)
XLA Ops:
  0.0 1.0 reshape.15
  1.0 0.1 copy.12
  1.1 0.7 pad.8.clone
  1.8 8.5 %all-to-all-start = ((bf16[8,48,128]{2,1,0:T(8,128)(2,1)}), bf16[8,48,128]{2,1,0:T(8,128)(2,1)S(1)}, u32[]{:S(2)}, u32[]{:S(2)}) async-start(bf16[8,48,128]{2,1,0:T(8,128)(2,1)} %pad.8.clone), calls=%async_computation | async-start | bytes 196608 | tf_op jit(solution)/shard_map/all_to_all | solution.py:355
  10.2 2.8 %shard_map.55 = (bf16[64,3200]{1,0:T(8,128)(2,1)}, bf16[32,3200]{1,0:T(8,128)(2,1)}, f32[16,1536]{1,0:T(8,128)}) custom-call(bf16[64,3072]{1,0:T(8,128)(2,1)} %img_ref.1, s32[2,64]{1,0:T(2,128)} %bitcast.15, s32[8,64]{1,0:T(8,128)} %bitcast.14, f32[1536]{0:T(1024)} %w_ref.1), custom_call_target="tpu_custom_call" | custom-call | flops 4194304 | bytes 1048576 | tf_op jit(solution)/shard_map/pallas_call | solution.py:102
  13.1 3.2 %collective-permute-start.3 = (bf16[32,3200]{1,0:T(8,128)(2,1)}, bf16[32,3200]{1,0:T(8,128)(2,1)S(1)}, u32[]{:S(2)}, u32[]{:S(2)}) collective-permute-start(bf16[32,3200]{1,0:T(8,128)(2,1)} %get-tuple-element.14), channel_id=1, source_target_pairs={{0,28},{4,0},{8,4},{12,8},{16,12},{20,16},{24,20},{28,24},{1,29},{... | collective-permute-start | bytes 614408 | tf_op jit(solution)/shard_map/ppermute | solution.py:338
  16.3 2.6 %all-to-all-done = bf16[8,48,128]{2,1,0:T(8,128)(2,1)S(1)} async-done(((bf16[8,48,128]{2,1,0:T(8,128)(2,1)}), bf16[8,48,128]{2,1,0:T(8,128)(2,1)S(1)}, u32[]{:S(2)}, u32[]{:S(2)}) %all-to-all-start) | async-done | bytes 98336 | tf_op jit(solution)/shard_map/all_to_all | solution.py:355
  19.0 1.0 broadcast_in_dim.6
  19.9 6.0 %all-to-all-start.1 = ((bf16[8,384,128]{2,1,0:T(8,128)(2,1)}), bf16[8,384,128]{2,1,0:T(8,128)(2,1)S(1)}, u32[]{:S(2)}, u32[]{:S(2)}) async-start(bf16[8,384,128]{2,1,0:T(8,128)(2,1)} %broadcast_in_dim.6), calls=%async_computation.1 | async-start | bytes 1572864 | tf_op jit(solution)/shard_map/all_to_all | solution.py:357
  26.0 0.7 collective-permute-start.4
  26.7 1.4 %collective-permute-start.1 = (bf16[32,3200]{1,0:T(8,128)(2,1)S(1)}, bf16[32,3200]{1,0:T(8,128)(2,1)S(1)}, u32[]{:S(2)}, u32[]{:S(2)}) collective-permute-start(bf16[32,3200]{1,0:T(8,128)(2,1)S(1)} %collective-permute-done.args_1_), channel_id=1, source_target_pairs={{0,4},{4,8},{8,12},{12,16},{16,20},{20,24},{24,28},{28,0},{1,5},{5... | collective-permute-start | bytes 614408 | tf_op jit(solution)/shard_map/ppermute | solution.py:338
  28.1 4.1 %collective-permute-done.4.args_5_ = bf16[32,3200]{1,0:T(8,128)(2,1)S(1)} collective-permute-done((bf16[32,3200]{1,0:T(8,128)(2,1)S(1)}, bf16[32,3200]{1,0:T(8,128)(2,1)S(1)}, u32[]{:S(2)}, u32[]{:S(2)}) %collective-permute-start.4) | collective-permute-done | bytes 204832 | tf_op jit(solution)/shard_map/ppermute | solution.py:338
  32.1 1.5 %collective-permute-start.5 = (bf16[32,3200]{1,0:T(8,128)(2,1)S(1)}, bf16[32,3200]{1,0:T(8,128)(2,1)S(1)}, u32[]{:S(2)}, u32[]{:S(2)}) collective-permute-start(bf16[32,3200]{1,0:T(8,128)(2,1)S(1)} %collective-permute-done.4.args_5_), channel_id=1, source_target_pairs={{0,28},{4,0},{8,4},{12,8},{16,12},{20,16},{24,20},{28,24},{1,29},{... | collective-permute-start | bytes 614408 | tf_op jit(solution)/shard_map/ppermute | solution.py:338
  33.6 0.5 collective-permute-start.2
  34.2 0.5 collective-permute-start.8
  34.7 3.2 %collective-permute-done.5.args_6_ = bf16[32,3200]{1,0:T(8,128)(2,1)S(1)} collective-permute-done((bf16[32,3200]{1,0:T(8,128)(2,1)S(1)}, bf16[32,3200]{1,0:T(8,128)(2,1)S(1)}, u32[]{:S(2)}, u32[]{:S(2)}) %collective-permute-start.5) | collective-permute-done | bytes 204832 | tf_op jit(solution)/shard_map/ppermute | solution.py:338
  37.9 2.7 %collective-permute-done.2.args_3_ = bf16[32,3200]{1,0:T(8,128)(2,1)S(1)} collective-permute-done((bf16[32,3200]{1,0:T(8,128)(2,1)S(1)}, bf16[32,3200]{1,0:T(8,128)(2,1)S(1)}, u32[]{:S(2)}, u32[]{:S(2)}) %collective-permute-start.2) | collective-permute-done | bytes 204832 | tf_op jit(solution)/shard_map/ppermute | solution.py:338
  40.6 0.1 collective-permute-start.7
  40.7 2.0 %collective-permute-start.6 = (bf16[16,3200]{1,0:T(8,128)(2,1)S(1)}, bf16[16,3200]{1,0:T(8,128)(2,1)S(1)}, u32[]{:S(2)}, u32[]{:S(2)}) collective-permute-start(bf16[16,3200]{1,0:T(8,128)(2,1)S(1)} %slice.16), channel_id=1, source_target_pairs={{0,4},{4,8},{8,12},{12,16},{16,20},{20,24},{24,28},{28,0},{1,5},{5... | collective-permute-start | bytes 307208 | tf_op jit(solution)/shard_map/ppermute | solution.py:338
  42.7 0.5 collective-permute-start.10
  43.2 2.0 %collective-permute-done.7.args_8_ = bf16[16,3200]{1,0:T(8,128)(2,1)S(1)} collective-permute-done((bf16[16,3200]{1,0:T(8,128)(2,1)S(1)}, bf16[16,3200]{1,0:T(8,128)(2,1)S(1)}, u32[]{:S(2)}, u32[]{:S(2)}) %collective-permute-start.7) | collective-permute-done | bytes 102432 | tf_op jit(solution)/shard_map/ppermute | solution.py:338
  45.3 1.8 %collective-permute-done.6.args_7_ = bf16[16,3200]{1,0:T(8,128)(2,1)S(1)} collective-permute-done((bf16[16,3200]{1,0:T(8,128)(2,1)S(1)}, bf16[16,3200]{1,0:T(8,128)(2,1)S(1)}, u32[]{:S(2)}, u32[]{:S(2)}) %collective-permute-start.6) | collective-permute-done | bytes 102432 | tf_op jit(solution)/shard_map/ppermute | solution.py:338
  47.0 0.9 copy-done
  47.9 5.3 %shard_map.56 = (bf16[2000,3072]{1,0:T(8,128)(2,1)S(1)}, f32[80,128]{1,0:T(8,128)S(1)}) custom-call(bf16[3072,128]{1,0:T(8,128)(2,1)S(1)} %bitcast.9, f32[16,1536]{1,0:T(8,128)S(1)} %copy-done), custom_call_target="tpu_custom_call" | custom-call | flops 41943040 | bytes 14680064 | tf_op jit(solution)/shard_map/pallas_call | solution.py:158
  53.3 1.0 copy-done.2
  54.3 8.8 %shard_map.57 = (bf16[512,3200]{1,0:T(8,128)(2,1)S(1)}, f32[2000,512]{1,0:T(8,128)S(1)}, f32[16,512]{1,0:T(8,128)S(1)}) custom-call(bf16[64,3200]{1,0:T(8,128)(2,1)S(1)} %copy-done.2, bf16[32,3200]{1,0:T(8,128)(2,1)S(1)} %collective-permute-done.args_1_, bf16[32,3200]{1,0:T(8,128)(2,1)S(1)} %collective-permute-done.1.args_2_, ...), custom_call_target="tpu_custom_call" | custom-call | flops 6291456000 | bytes 25165824 | tf_op jit(solution)/shard_map/pallas_call | solution.py:244
  63.1 15.3 %all_to_all.25.all_ref = f32[32,2,512]{2,1,0:T(2,128)S(1)} all-to-all(f32[32,2,512]{2,1,0:T(2,128)S(1)} %broadcast_in_dim.7), channel_id=1, replica_groups=mesh['y'=4,'xh'=2,'z'=8,'xl'=2,'co'=2] {'z','xl','co'}, dimensions={0} | all-to-all | bytes 262144 | tf_op jit(solution)/shard_map/all_to_all | solution.py:364
  78.5 7.4 %shard_map.58 = f32[8,80,384]{2,1,0:T(8,128)S(1)} custom-call(f32[16,512]{1,0:T(8,128)S(1)} %get-tuple-element.18.stat_ref, f32[32,2,512]{2,1,0:T(2,128)S(1)} %all_to_all.25.all_ref, bf16[512,3200]{1,0:T(8,128)(2,1)S(1)} %get-tuple-element.19.p_ref, f32[2000,512]{1,0:T(8,128)S(1)} %get-tuple-element.20.expo_ref, f32[16,1536]{1,0:T(8,128)S(1)} %copy-done.1), custom_call_target="tpu_custom_call" | custom-call | flops 6291456000 | bytes 9437184 | tf_op jit(solution)/shard_map/pallas_call | solution.py:321
  85.9 22.9 %all_to_all.26 = f32[8,80,384]{2,1,0:T(8,128)S(1)} all-to-all(f32[8,80,384]{2,1,0:T(8,128)S(1)} %shard_map.58), channel_id=1, replica_groups=mesh['y'=4,'xh'=2,'z'=8,'xl'=2,'co'=2] {'y','xh'}, dimensions={0} | all-to-all | bytes 1966080 | tf_op jit(solution)/shard_map/all_to_all | solution.py:369
  108.9 0.1 copy.13
  109.0 12.2 %all_to_all.27 = f32[8,48,128]{2,1,0:T(8,128)S(1)} all-to-all(f32[8,48,128]{2,1,0:T(8,128)S(1)} %bitcast.10), channel_id=1, replica_groups=mesh['y'=4,'xh'=2,'z'=8,'xl'=2,'co'=2] {'z'}, dimensions={0} | all-to-all | bytes 393216 | tf_op jit(solution)/shard_map/all_to_all | solution.py:371
  121.3 0.8 reshape.19
  (31 shorter events, 0.3 us)
Async XLA Ops:
  1.8 17.2 %all-to-all-start = ((bf16[8,48,128]{2,1,0:T(8,128)(2,1)}), bf16[8,48,128]{2,1,0:T(8,128)(2,1)S(1)}, u32[]{:S(2)}, u32[]{:S(2)}) async-start(bf16[8,48,128]{2,1,0:T(8,128)(2,1)} %pad.8.clone), calls=%async_computation | async-start | bytes 196608 | tf_op jit(solution)/shard_map/all_to_all | solution.py:355
  13.1 12.9 %collective-permute-start.3 = (bf16[32,3200]{1,0:T(8,128)(2,1)}, bf16[32,3200]{1,0:T(8,128)(2,1)S(1)}, u32[]{:S(2)}, u32[]{:S(2)}) collective-permute-start(bf16[32,3200]{1,0:T(8,128)(2,1)} %get-tuple-element.14), channel_id=1, source_target_pairs={{0,28},{4,0},{8,4},{12,8},{16,12},{20,16},{24,20},{28,24},{1,29},{... | collective-permute-start | bytes 614408 | tf_op jit(solution)/shard_map/ppermute | solution.py:338
  16.3 10.3 %collective-permute-start = (bf16[32,3200]{1,0:T(8,128)(2,1)}, bf16[32,3200]{1,0:T(8,128)(2,1)S(1)}, u32[]{:S(2)}, u32[]{:S(2)}) collective-permute-start(bf16[32,3200]{1,0:T(8,128)(2,1)} %get-tuple-element.14), channel_id=1, source_target_pairs={{0,4},{4,8},{8,12},{12,16},{16,20},{20,24},{24,28},{28,0},{1,5},{5... | collective-permute-start | bytes 614408 | tf_op jit(solution)/shard_map/ppermute | solution.py:338
  19.9 27.1 %all-to-all-start.1 = ((bf16[8,384,128]{2,1,0:T(8,128)(2,1)}), bf16[8,384,128]{2,1,0:T(8,128)(2,1)S(1)}, u32[]{:S(2)}, u32[]{:S(2)}) async-start(bf16[8,384,128]{2,1,0:T(8,128)(2,1)} %broadcast_in_dim.6), calls=%async_computation.1 | async-start | bytes 1572864 | tf_op jit(solution)/shard_map/all_to_all | solution.py:357
  26.0 6.2 %collective-permute-start.4 = (bf16[32,3200]{1,0:T(8,128)(2,1)S(1)}, bf16[32,3200]{1,0:T(8,128)(2,1)S(1)}, u32[]{:S(2)}, u32[]{:S(2)}) collective-permute-start(bf16[32,3200]{1,0:T(8,128)(2,1)S(1)} %collective-permute-done.3.args_4_), channel_id=1, source_target_pairs={{0,28},{4,0},{8,4},{12,8},{16,12},{20,16},{24,20},{28,24},{1,29},{... | collective-permute-start | bytes 614408 | tf_op jit(solution)/shard_map/ppermute | solution.py:338
  26.7 7.0 %collective-permute-start.1 = (bf16[32,3200]{1,0:T(8,128)(2,1)S(1)}, bf16[32,3200]{1,0:T(8,128)(2,1)S(1)}, u32[]{:S(2)}, u32[]{:S(2)}) collective-permute-start(bf16[32,3200]{1,0:T(8,128)(2,1)S(1)} %collective-permute-done.args_1_), channel_id=1, source_target_pairs={{0,4},{4,8},{8,12},{12,16},{16,20},{20,24},{24,28},{28,0},{1,5},{5... | collective-permute-start | bytes 614408 | tf_op jit(solution)/shard_map/ppermute | solution.py:338
  32.1 5.8 %collective-permute-start.5 = (bf16[32,3200]{1,0:T(8,128)(2,1)S(1)}, bf16[32,3200]{1,0:T(8,128)(2,1)S(1)}, u32[]{:S(2)}, u32[]{:S(2)}) collective-permute-start(bf16[32,3200]{1,0:T(8,128)(2,1)S(1)} %collective-permute-done.4.args_5_), channel_id=1, source_target_pairs={{0,28},{4,0},{8,4},{12,8},{16,12},{20,16},{24,20},{28,24},{1,29},{... | collective-permute-start | bytes 614408 | tf_op jit(solution)/shard_map/ppermute | solution.py:338
  33.6 7.0 %collective-permute-start.2 = (bf16[32,3200]{1,0:T(8,128)(2,1)S(1)}, bf16[32,3200]{1,0:T(8,128)(2,1)S(1)}, u32[]{:S(2)}, u32[]{:S(2)}) collective-permute-start(bf16[32,3200]{1,0:T(8,128)(2,1)S(1)} %collective-permute-done.1.args_2_), channel_id=1, source_target_pairs={{0,4},{4,8},{8,12},{12,16},{16,20},{20,24},{24,28},{28,0},{1,5},{5... | collective-permute-start | bytes 614408 | tf_op jit(solution)/shard_map/ppermute | solution.py:338
  34.2 6.5 %collective-permute-start.11 = (bf16[32,3200]{1,0:T(8,128)(2,1)S(1)}, bf16[32,3200]{1,0:T(8,128)(2,1)S(1)}, u32[]{:S(2)}, u32[]{:S(2)}) collective-permute-start(bf16[32,3200]{1,0:T(8,128)(2,1)S(1)} %collective-permute-done.3.args_4_), channel_id=1, source_target_pairs={{0,1},{1,0},{2,3},{3,2},{4,5},{5,4},{6,7},{7,6},{8,9},{9,8},{10,11... | collective-permute-start | bytes 614408 | tf_op jit(solution)/shard_map/ppermute | solution.py:348
  34.2 8.5 %collective-permute-start.8 = (bf16[32,3200]{1,0:T(8,128)(2,1)S(1)}, bf16[32,3200]{1,0:T(8,128)(2,1)S(1)}, u32[]{:S(2)}, u32[]{:S(2)}) collective-permute-start(bf16[32,3200]{1,0:T(8,128)(2,1)S(1)} %collective-permute-done.args_1_), channel_id=1, source_target_pairs={{0,1},{1,0},{2,3},{3,2},{4,5},{5,4},{6,7},{7,6},{8,9},{9,8},{10,11... | collective-permute-start | bytes 614408 | tf_op jit(solution)/shard_map/ppermute | solution.py:348
  34.7 8.0 %collective-permute-start.12 = (bf16[32,3200]{1,0:T(8,128)(2,1)S(1)}, bf16[32,3200]{1,0:T(8,128)(2,1)S(1)}, u32[]{:S(2)}, u32[]{:S(2)}) collective-permute-start(bf16[32,3200]{1,0:T(8,128)(2,1)S(1)} %collective-permute-done.4.args_5_), channel_id=1, source_target_pairs={{0,1},{1,0},{2,3},{3,2},{4,5},{5,4},{6,7},{7,6},{8,9},{9,8},{10,11... | collective-permute-start | bytes 614408 | tf_op jit(solution)/shard_map/ppermute | solution.py:348
  37.9 15.3 %collective-permute-start.9 = (bf16[32,3200]{1,0:T(8,128)(2,1)S(1)}, bf16[32,3200]{1,0:T(8,128)(2,1)S(1)}, u32[]{:S(2)}, u32[]{:S(2)}) collective-permute-start(bf16[32,3200]{1,0:T(8,128)(2,1)S(1)} %collective-permute-done.1.args_2_), channel_id=1, source_target_pairs={{0,1},{1,0},{2,3},{3,2},{4,5},{5,4},{6,7},{7,6},{8,9},{9,8},{10,11... | collective-permute-start | bytes 614408 | tf_op jit(solution)/shard_map/ppermute | solution.py:348
  40.6 4.7 %collective-permute-start.7 = (bf16[16,3200]{1,0:T(8,128)(2,1)S(1)}, bf16[16,3200]{1,0:T(8,128)(2,1)S(1)}, u32[]{:S(2)}, u32[]{:S(2)}) collective-permute-start(bf16[16,3200]{1,0:T(8,128)(2,1)S(1)} %slice.17), channel_id=1, source_target_pairs={{0,28},{4,0},{8,4},{12,8},{16,12},{20,16},{24,20},{28,24},{1,29},{... | collective-permute-start | bytes 307208 | tf_op jit(solution)/shard_map/ppermute | solution.py:338
  40.7 6.3 %collective-permute-start.6 = (bf16[16,3200]{1,0:T(8,128)(2,1)S(1)}, bf16[16,3200]{1,0:T(8,128)(2,1)S(1)}, u32[]{:S(2)}, u32[]{:S(2)}) collective-permute-start(bf16[16,3200]{1,0:T(8,128)(2,1)S(1)} %slice.16), channel_id=1, source_target_pairs={{0,4},{4,8},{8,12},{12,16},{16,20},{20,24},{24,28},{28,0},{1,5},{5... | collective-permute-start | bytes 307208 | tf_op jit(solution)/shard_map/ppermute | solution.py:338
  42.7 10.5 %collective-permute-start.13 = (bf16[32,3200]{1,0:T(8,128)(2,1)S(1)}, bf16[32,3200]{1,0:T(8,128)(2,1)S(1)}, u32[]{:S(2)}, u32[]{:S(2)}) collective-permute-start(bf16[32,3200]{1,0:T(8,128)(2,1)S(1)} %collective-permute-done.5.args_6_), channel_id=1, source_target_pairs={{0,1},{1,0},{2,3},{3,2},{4,5},{5,4},{6,7},{7,6},{8,9},{9,8},{10,11... | collective-permute-start | bytes 614408 | tf_op jit(solution)/shard_map/ppermute | solution.py:348
  42.7 10.5 %collective-permute-start.10 = (bf16[32,3200]{1,0:T(8,128)(2,1)S(1)}, bf16[32,3200]{1,0:T(8,128)(2,1)S(1)}, u32[]{:S(2)}, u32[]{:S(2)}) collective-permute-start(bf16[32,3200]{1,0:T(8,128)(2,1)S(1)} %collective-permute-done.2.args_3_), channel_id=1, source_target_pairs={{0,1},{1,0},{2,3},{3,2},{4,5},{5,4},{6,7},{7,6},{8,9},{9,8},{10,11... | collective-permute-start | bytes 614408 | tf_op jit(solution)/shard_map/ppermute | solution.py:348
  45.3 8.0 %collective-permute-start.15 = (bf16[16,3200]{1,0:T(8,128)(2,1)S(1)}, bf16[16,3200]{1,0:T(8,128)(2,1)S(1)}, u32[]{:S(2)}, u32[]{:S(2)}) collective-permute-start(bf16[16,3200]{1,0:T(8,128)(2,1)S(1)} %collective-permute-done.7.args_8_), channel_id=1, source_target_pairs={{0,1},{1,0},{2,3},{3,2},{4,5},{5,4},{6,7},{7,6},{8,9},{9,8},{10,11... | collective-permute-start | bytes 307208 | tf_op jit(solution)/shard_map/ppermute | solution.py:348
  47.0 6.2 %collective-permute-start.14 = (bf16[16,3200]{1,0:T(8,128)(2,1)S(1)}, bf16[16,3200]{1,0:T(8,128)(2,1)}, u32[]{:S(2)}, u32[]{:S(2)}) collective-permute-start(bf16[16,3200]{1,0:T(8,128)(2,1)S(1)} %collective-permute-done.6.args_7_), channel_id=1, source_target_pairs={{0,1},{1,0},{2,3},{3,2},{4,5},{5,4},{6,7},{7,6},{8,9},{9,8},{10,11... | collective-permute-start | bytes 307208 | tf_op jit(solution)/shard_map/ppermute | solution.py:348
  47.0 0.9 copy-start
  53.3 1.0 copy-start.2
  54.3 24.2 %copy-start.1 = (f32[16,1536]{1,0:T(8,128)S(1)}, f32[16,1536]{1,0:T(8,128)}, u32[]{:S(2)}) copy-start(f32[16,1536]{1,0:T(8,128)} %get-tuple-element.15.tab_ref) | copy-start | bytes 294916

commit v5 on v4

--- a/solution.py
+++ b/solution.py
@@ -108,6 +108,7 @@
             jax.ShapeDtypeStruct((PARTS // 2, WIDTH + LANES), bf16),
             jax.ShapeDtypeStruct((16, HALF), f32),
         ],
+        compiler_params=pltpu.CompilerParams(vmem_limit_bytes=8 << 20),
         cost_estimate=pl.CostEstimate(flops=4 << 20, bytes_accessed=1 << 20, transcendentals=0),
     )(images, offsets, class_lists, weight)
 
@@ -119,36 +120,39 @@
     return c, (s if gy > 0 else -s)
 
 
-def shift_kernel(r_ref, tab_ref, out_ref, energy_ref, total):
+def shift_kernel(*args):
+    pieces, (tab_ref, out_ref, energy_ref, r_ref, total) = args[:4], args[4:]
+    y, xh = lax.axis_index("y"), lax.axis_index("xh")
+    for far, ref in enumerate(pieces):
+        for n in range(2):
+            place = ((y + 4 - far) & 3) * 2 + (xh if n == 0 else 1 - xh)
+            at = pl.multiple_of(place * CHUNK, CHUNK)
+            r_ref[pl.ds(at, CHUNK), :] = ref[n * CHUNK : (n + 1) * CHUNK, :]
     total[...] = jnp.zeros_like(total)
-
-    def chunk(n, carry):
-        at = pl.multiple_of(n * LANES, LANES)
-        lanes, ims = pl.ds(at, LANES), pl.ds(HALF + at, LANES)
-        rr = r_ref[lanes, :].astype(f32).T[:PAD]
-        ri = r_ref[ims, :].astype(f32).T[:PAD]
-        total[...] += (rr * rr + ri * ri) * tab_ref[8:9, lanes]
-        for gy in range(-2, 3):
-            yr, yi = rr, ri
-            if gy:
-                c, s = y_shift(tab_ref, gy, lanes)
-                yr, yi = rr * c - ri * s, ri * c + rr * s
-            mid = ((gy + 2) * GRID + 2) * PAD
-            out_ref[mid : mid + PAD, lanes] = yr.astype(bf16)
-            out_ref[mid : mid + PAD, ims] = yi.astype(bf16)
-            for gx in (1, 2):
-                c = tab_ref[2 * gx - 2 : 2 * gx - 1, lanes]
-                s = tab_ref[2 * gx - 1 : 2 * gx, lanes]
-                cr, ci, sr, si = yr * c, yi * c, yr * s, yi * s
-                hi = slice(mid + gx * PAD, mid + (gx + 1) * PAD)
-                lo = slice(mid - gx * PAD, mid - (gx - 1) * PAD)
-                out_ref[hi, lanes] = (cr - si).astype(bf16)
-                out_ref[hi, ims] = (ci + sr).astype(bf16)
-                out_ref[lo, lanes] = (cr + si).astype(bf16)
-                out_ref[lo, ims] = (ci - sr).astype(bf16)
-        return carry
-
-    lax.fori_loop(0, HALF // LANES, chunk, 0)
+    for at in range(0, HALF, LANES):
+        lanes, ims = slice(at, at + LANES), slice(HALF + at, HALF + at + LANES)
+        all_re = r_ref[lanes, :].astype(f32).T[:PAD]
+        all_im = r_ref[ims, :].astype(f32).T[:PAD]
+        total[...] += (all_re * all_re + all_im * all_im) * tab_ref[8:9, lanes]
+        for p in range(0, PAD, 16):
+            for gy in range(-2, 3):
+                yr, yi = all_re[p : p + 16], all_im[p : p + 16]
+                if gy:
+                    c, s = y_shift(tab_ref, gy, lanes)
+                    yr, yi = yr * c - yi * s, yi * c + yr * s
+                mid = ((gy + 2) * GRID + 2) * PAD + p
+                out_ref[mid : mid + 16, lanes] = yr.astype(bf16)
+                out_ref[mid : mid + 16, ims] = yi.astype(bf16)
+                for gx in (1, 2):
+                    c = tab_ref[2 * gx - 2 : 2 * gx - 1, lanes]
+                    s = tab_ref[2 * gx - 1 : 2 * gx, lanes]
+                    cr, ci, sr, si = yr * c, yi * c, yr * s, yi * s
+                    hi = slice(mid + gx * PAD, mid + gx * PAD + 16)
+                    lo = slice(mid - gx * PAD, mid - gx * PAD + 16)
+                    out_ref[hi, lanes] = (cr - si).astype(bf16)
+                    out_ref[hi, ims] = (ci + sr).astype(bf16)
+                    out_ref[lo, lanes] = (cr + si).astype(bf16)
+                    out_ref[lo, ims] = (ci - sr).astype(bf16)
     energy_ref[...] = jnp.broadcast_to(
         0.5 * jnp.sum(total[...], axis=1, keepdims=True), energy_ref.shape
     )
@@ -157,16 +161,16 @@
 def shift_refs(refs, table):
     return pl.pallas_call(
         shift_kernel,
-        in_specs=[VMEM] * 2,
+        in_specs=[VMEM] * 5,
         out_specs=[VMEM] * 2,
         out_shape=[
             jax.ShapeDtypeStruct((SHIFTS * PAD, WIDTH), bf16),
             jax.ShapeDtypeStruct((PAD, LANES), f32),
         ],
-        scratch_shapes=[pltpu.VMEM((PAD, LANES), f32)],
+        scratch_shapes=[pltpu.VMEM((WIDTH, LANES), bf16), pltpu.VMEM((PAD, LANES), f32)],
         compiler_params=pltpu.CompilerParams(vmem_limit_bytes=16 << 20),
-        cost_estimate=pl.CostEstimate(flops=40 << 20, bytes_accessed=14 << 20, transcendentals=0),
-    )(refs, table)
+        cost_estimate=pl.CostEstimate(flops=1, bytes_accessed=1, transcendentals=0),
+    )(*refs, table)
 
 
 def assemble(pieces, probes):
@@ -338,27 +342,31 @@
     return lax.ppermute(x, "z", [(i, (i + far) % GROUP) for i in range(GROUP)])
 
 
-def gather_pieces(own, half):
+def to_other_core(x):
+    return lax.ppermute(x, "co", [(0, 1), (1, 0)])
+
+
+def per_device(images, offsets, class_lists, noise_weight, references):
+    own, half, table = prep(images, offsets.T, class_lists.T, noise_weight)
+
+    part = references.reshape(GROUP, ROWS, 48)
+    part = jnp.pad(jnp.transpose(part, (0, 2, 1)), ((0, 0), (0, 0), (0, LANES - ROWS)))
+    part = lax.all_to_all(part, "z", 0, 0).reshape(CHUNK, LANES)
+    part, table = lax.optimization_barrier((part, table))
+    part = jnp.concatenate([part, lax.ppermute(part, "xh", [(0, 1), (1, 0)])])
+    refs = [part]
+    for far in (1, 2, 3):
+        refs.append(lax.ppermute(part, "y", [(i, (i + far) % 4) for i in range(4)]))
+    shifted, energy = shift_refs(refs, table)
+
     up, down = [half], [half]
     for _ in range(3):
         up.append(along_z(up[-1], 1))
         down.append(along_z(down[-1], -1))
     cut = PARTS // 4
     mine = up[1:] + down[1:] + [along_z(up[-1][:cut], 1), along_z(down[-1][cut:], -1)]
-    other = [lax.ppermute(x, "co", [(0, 1), (1, 0)]) for x in mine]
-    return [own] + mine + other
-
-
-def per_device(images, offsets, class_lists, noise_weight, references):
-    mine = references.reshape(GROUP, ROWS, 48)
-    mine = jnp.pad(jnp.transpose(mine, (0, 2, 1)), ((0, 0), (0, 0), (0, LANES - ROWS)))
-    mine = lax.all_to_all(mine, "z", 0, 0).reshape(CHUNK, LANES)
-    mine = jnp.broadcast_to(mine, (GROUP, CHUNK, LANES))
-    refs = lax.all_to_all(mine, ("y", "xh"), 0, 0).reshape(WIDTH, LANES)
-
-    own, half, table = prep(images, offsets.T, class_lists.T, noise_weight)
-    pieces = gather_pieces(own, half)
-    shifted, energy = shift_refs(refs, table)
+    mine[6], mine[7], shifted = lax.optimization_barrier((mine[6], mine[7], shifted))
+    pieces = [own] + mine + [to_other_core(x) for x in mine]
 
     probes, expo, stat = estep(pieces, shifted, energy)
     stats = lax.all_to_all(

time: 123 us -> 116 us (0.943)
  Pallas kernels: 24.3 us -> 18.8 us
  blocking collectives: 50.4 us -> 46.9 us
  starting transfers between devices: 25 us -> 27.2 us
    ppermute x8, waiting for transfers between devices: 13.7 us -> 1.68 us  [along_z(): return lax.ppermute(x, 'z', [(i, (i + far) % GROUP) for i in range(GROUP)])]
    all_to_all x2 -> x1, starting transfers between devices: 14.5 us -> 4.63 us  [per_device(): part = lax.all_to_all(part, 'z', 0, 0).reshape(CHUNK, LANES)]
    ppermute x8 -> x12, waiting for transfers between devices: 0.02 us -> 8.47 us  [the longest x3 5.49 us: per_device(): refs.append(lax.ppermute(part, 'y', [(i, (i + far) % 4) for i in range(4)]))]
    ppermute x8 -> x12, starting transfers between devices: 1.03 us -> 8.68 us  [the longest x3 5.16 us: per_device(): refs.append(lax.ppermute(part, 'y', [(i, (i + far) % 4) for i in range(4)]))]
    ppermute x8, starting transfers between devices: 9.47 us -> 13.9 us  [along_z(): return lax.ppermute(x, 'z', [(i, (i + far) % GROUP) for i in range(GROUP)])]
    all_to_all x2 -> x1, waiting for transfers between devices: 2.65 us -> 5.97 us  [per_device(): part = lax.all_to_all(part, 'z', 0, 0).reshape(CHUNK, LANES)]
    pallas_call x1, Pallas kernels: 5.28 us -> 3.01 us  [shift_refs(): pl.pallas_call(shift_kernel, in_specs=[VMEM] * 5, out_specs=[VMEM] * 2, o...]
    all_to_all x1, blocking collectives: 15.3 us -> 13.4 us  [per_device(): lax.all_to_all(jnp.broadcast_to(stat[5:7], (32, 2, NPART)), ('z', 'xl', '...]
  transfers between devices with their start and end apart: 18 -> 21, of which waited for: 6 -> 8; matrix products, arithmetic and copies ran while one was open for 1% -> 2% of each run, Pallas kernels for 7% -> 3%
where the time goes in v5:
time: 116 us; the launch traced here: 115 us
  blocking collectives  46.9 us (40%)
  starting transfers between devices  27.2 us (23%)
  Pallas kernels  18.8 us (16%)
  waiting for transfers between devices  16.1 us (14%)
  local copies, waits for them, and re-layouts  5.89 us (5%)
    all_to_all x1, blocking collectives, per_device(): sums = jnp.sum(lax.all_to_all(sums, ('y', 'xh'), 0, 0), axis=0)  21.4 us
    ppermute x8, starting transfers between devices, along_z(): return lax.ppermute(x, 'z', [(i, (i + far) % GROUP) for i in range(GROUP)])  13.9 us
    all_to_all x1, blocking collectives, per_device(): lax.all_to_all(jnp.broadcast_to(stat[5:7], (32, 2, NPART)), ('z', 'xl', '...  13.4 us
    all_to_all x1, blocking collectives, per_device(): sums = lax.all_to_all(sums, 'z', 0, 0)[:, :, :ROWS]  12.2 us
    pallas_call x1, Pallas kernels, estep(): pl.pallas_call(estep_kernel, in_specs=[VMEM] * (PIECES + 2), out_specs=[V...  7.81 us
    pallas_call x1, Pallas kernels, mstep(): pl.pallas_call(mstep_kernel, in_specs=[VMEM] * 5, out_specs=VMEM, out_sha...  7.05 us
    all_to_all x1, waiting for transfers between devices, per_device(): part = lax.all_to_all(part, 'z', 0, 0).reshape(CHUNK, LANES)  5.97 us
    ppermute x3, waiting for transfers between devices, per_device(): refs.append(lax.ppermute(part, 'y', [(i, (i + far) % 4) for i in range(4)]))  5.49 us
  transfers between devices with their start and end apart: 21, of which 8 were waited for; matrix products, arithmetic and copies ran while one was open for 2% of the time, Pallas kernels for 3%

profile of v5, /device:TPU:2, one launch (start us, length us, event | category | flops | bytes accessed | tf_op | source)
XLA Modules:
  0.0 115.2 jit_solution(7961995027061869794)
XLA Ops:
  0.0 1.0 copy-done
  1.0 0.7 copy-done.1
  1.7 0.7 copy-done.2
  2.4 0.7 copy-done.3
  3.1 1.0 shard_map.55
  4.0 5.9 %collective-permute-start.3 = (bf16[32,3200]{1,0:T(8,128)(2,1)S(1)}, bf16[32,3200]{1,0:T(8,128)(2,1)S(1)}, u32[]{:S(2)}, u32[]{:S(2)}) collective-permute-start(bf16[32,3200]{1,0:T(8,128)(2,1)S(1)} %get-tuple-element.19), channel_id=1, source_target_pairs={{0,28},{4,0},{8,4},{12,8},{16,12},{20,16},{24,20},{28,24},{1,29},{... | collective-permute-start | bytes 614408 | tf_op jit(solution)/shard_map/ppermute | solution.py:342
  10.0 1.0 reshape.12
  11.1 0.7 pad.8.clone
  11.7 4.6 %all-to-all-start = ((bf16[8,48,128]{2,1,0:T(8,128)(2,1)}), bf16[8,48,128]{2,1,0:T(8,128)(2,1)S(1)}, u32[]{:S(2)}, u32[]{:S(2)}) async-start(bf16[8,48,128]{2,1,0:T(8,128)(2,1)} %pad.8.clone), calls=%async_computation | async-start | bytes 196608 | tf_op jit(solution)/shard_map/all_to_all | solution.py:354
  16.4 3.2 %collective-permute-start.4 = (bf16[32,3200]{1,0:T(8,128)(2,1)S(1)}, bf16[32,3200]{1,0:T(8,128)(2,1)S(1)}, u32[]{:S(2)}, u32[]{:S(2)}) collective-permute-start(bf16[32,3200]{1,0:T(8,128)(2,1)S(1)} %collective-permute-done.3.args_4_), channel_id=1, source_target_pairs={{0,28},{4,0},{8,4},{12,8},{16,12},{20,16},{24,20},{28,24},{1,29},{... | collective-permute-start | bytes 614408 | tf_op jit(solution)/shard_map/ppermute | solution.py:342
  19.6 6.0 %all-to-all-done = bf16[8,48,128]{2,1,0:T(8,128)(2,1)S(1)} async-done(((bf16[8,48,128]{2,1,0:T(8,128)(2,1)}), bf16[8,48,128]{2,1,0:T(8,128)(2,1)S(1)}, u32[]{:S(2)}, u32[]{:S(2)}) %all-to-all-start) | async-done | bytes 98336 | tf_op jit(solution)/shard_map/all_to_all | solution.py:354
  25.6 2.1 %collective-permute-start.8 = (bf16[384,128]{1,0:T(8,128)(2,1)S(1)}, bf16[384,128]{1,0:T(8,128)(2,1)S(1)}, u32[]{:S(2)}, u32[]{:S(2)}) collective-permute-start(bf16[384,128]{1,0:T(8,128)(2,1)S(1)} %bitcast.13), channel_id=1, source_target_pairs={{0,32},{32,0},{1,33},{33,1},{2,34},{34,2},{3,35},{35,3},{4,36},{36... | collective-permute-start | bytes 294920 | tf_op jit(solution)/shard_map/ppermute | solution.py:356
  27.8 0.7 collective-permute-start.5
  28.6 1.4 %collective-permute-start.2 = (bf16[32,3200]{1,0:T(8,128)(2,1)S(1)}, bf16[32,3200]{1,0:T(8,128)(2,1)S(1)}, u32[]{:S(2)}, u32[]{:S(2)}) collective-permute-start(bf16[32,3200]{1,0:T(8,128)(2,1)S(1)} %collective-permute-done.1.args_2_), channel_id=1, source_target_pairs={{0,4},{4,8},{8,12},{12,16},{16,20},{20,24},{24,28},{28,0},{1,5},{5... | collective-permute-start | bytes 614408 | tf_op jit(solution)/shard_map/ppermute | solution.py:342
  29.9 1.8 %collective-permute-done.8 = bf16[384,128]{1,0:T(8,128)(2,1)S(1)} collective-permute-done((bf16[384,128]{1,0:T(8,128)(2,1)S(1)}, bf16[384,128]{1,0:T(8,128)(2,1)S(1)}, u32[]{:S(2)}, u32[]{:S(2)}) %collective-permute-start.8) | collective-permute-done | bytes 98336 | tf_op jit(solution)/shard_map/ppermute | solution.py:356
  31.7 3.1 %collective-permute-start.11 = (bf16[768,128]{1,0:T(8,128)(2,1)S(1)}, bf16[768,128]{1,0:T(8,128)(2,1)S(1)}, u32[]{:S(2)}, u32[]{:S(2)}) collective-permute-start(bf16[768,128]{1,0:T(8,128)(2,1)S(1)} %constant_dynamic-update-slice_fusion.args_0_), channel_id=1, source_target_pairs={{0,192},{64,0},{128,64},{192,128},{1,193},{65,1},{129,65},{193,129... | collective-permute-start | bytes 589832 | tf_op jit(solution)/shard_map/ppermute | solution.py:359
  34.8 0.6 collective-permute-start.10
  35.5 1.4 %collective-permute-start.9 = (bf16[768,128]{1,0:T(8,128)(2,1)S(1)}, bf16[768,128]{1,0:T(8,128)(2,1)S(1)}, u32[]{:S(2)}, u32[]{:S(2)}) collective-permute-start(bf16[768,128]{1,0:T(8,128)(2,1)S(1)} %constant_dynamic-update-slice_fusion.args_0_), channel_id=1, source_target_pairs={{0,64},{64,128},{128,192},{192,0},{1,65},{65,129},{129,193},{193,1... | collective-permute-start | bytes 589832 | tf_op jit(solution)/shard_map/ppermute | solution.py:359
  37.1 1.9 %collective-permute-start.7 = (bf16[16,3200]{1,0:T(8,128)(2,1)S(1)}, bf16[16,3200]{1,0:T(8,128)(2,1)S(1)}, u32[]{:S(2)}, u32[]{:S(2)}) collective-permute-start(bf16[16,3200]{1,0:T(8,128)(2,1)S(1)} %slice.17), channel_id=1, source_target_pairs={{0,28},{4,0},{8,4},{12,8},{16,12},{20,16},{24,20},{28,24},{1,29},{... | collective-permute-start | bytes 307208 | tf_op jit(solution)/shard_map/ppermute | solution.py:342
  39.0 2.5 %collective-permute-done.11.args_3_ = bf16[768,128]{1,0:T(8,128)(2,1)S(1)} collective-permute-done((bf16[768,128]{1,0:T(8,128)(2,1)S(1)}, bf16[768,128]{1,0:T(8,128)(2,1)S(1)}, u32[]{:S(2)}, u32[]{:S(2)}) %collective-permute-start.11) | collective-permute-done | bytes 196640 | tf_op jit(solution)/shard_map/ppermute | solution.py:359
  41.5 0.7 collective-permute-start.6
  42.1 1.9 %collective-permute-done.10.args_2_ = bf16[768,128]{1,0:T(8,128)(2,1)S(1)} collective-permute-done((bf16[768,128]{1,0:T(8,128)(2,1)S(1)}, bf16[768,128]{1,0:T(8,128)(2,1)S(1)}, u32[]{:S(2)}, u32[]{:S(2)}) %collective-permute-start.10) | collective-permute-done | bytes 196640 | tf_op jit(solution)/shard_map/ppermute | solution.py:359
  44.0 1.2 %collective-permute-done.9.args_1_ = bf16[768,128]{1,0:T(8,128)(2,1)S(1)} collective-permute-done((bf16[768,128]{1,0:T(8,128)(2,1)S(1)}, bf16[768,128]{1,0:T(8,128)(2,1)S(1)}, u32[]{:S(2)}, u32[]{:S(2)}) %collective-permute-start.9) | collective-permute-done | bytes 196640 | tf_op jit(solution)/shard_map/ppermute | solution.py:359
  45.7 1.6 %collective-permute-done.6.args_7_ = bf16[16,3200]{1,0:T(8,128)(2,1)S(1)} collective-permute-done((bf16[16,3200]{1,0:T(8,128)(2,1)S(1)}, bf16[16,3200]{1,0:T(8,128)(2,1)S(1)}, u32[]{:S(2)}, u32[]{:S(2)}) %collective-permute-start.6) | collective-permute-done | bytes 102432 | tf_op jit(solution)/shard_map/ppermute | solution.py:342
  47.3 3.0 %shard_map.56 = (bf16[2000,3072]{1,0:T(8,128)(2,1)S(1)}, f32[80,128]{1,0:T(8,128)S(1)}) custom-call(bf16[768,128]{1,0:T(8,128)(2,1)S(1)} %constant_dynamic-update-slice_fusion.args_0_, bf16[768,128]{1,0:T(8,128)(2,1)S(1)} %collective-permute-done.9.args_1_, bf16[768,128]{1,0:T(8,128)(2,1)S(1)} %collective-permute-done.10.args_2_, ...), custom_call_target="tpu_custom_call" | custom-call | flops 1 | bytes 1 | tf_op jit(solution)/shard_map/pallas_call | solution.py:162
  51.1 0.8 collective-permute-done.18.args_15_
  52.3 7.8 %shard_map.57 = (bf16[512,3200]{1,0:T(8,128)(2,1)S(1)}, f32[2000,512]{1,0:T(8,128)S(1)}, f32[16,512]{1,0:T(8,128)S(1)}) custom-call(bf16[64,3200]{1,0:T(8,128)(2,1)S(1)} %get-tuple-element.18.args_0_, bf16[32,3200]{1,0:T(8,128)(2,1)S(1)} %collective-permute-done.args_1_, bf16[32,3200]{1,0:T(8,128)(2,1)S(1)} %collective-permute-done.1.args_2_, ...), custom_call_target="tpu_custom_call" | custom-call | flops 6291456000 | bytes 25165824 | tf_op jit(solution)/shard_map/pallas_call | solution.py:248
  60.1 13.4 %all_to_all.20.all_ref = f32[32,2,512]{2,1,0:T(2,128)S(1)} all-to-all(f32[32,2,512]{2,1,0:T(2,128)S(1)} %broadcast_in_dim.3), channel_id=1, replica_groups=mesh['y'=4,'xh'=2,'z'=8,'xl'=2,'co'=2] {'z','xl','co'}, dimensions={0} | all-to-all | bytes 262144 | tf_op jit(solution)/shard_map/all_to_all | solution.py:372
  73.6 7.0 %shard_map.58 = f32[8,80,384]{2,1,0:T(8,128)S(1)} custom-call(f32[16,512]{1,0:T(8,128)S(1)} %get-tuple-element.28.stat_ref, f32[32,2,512]{2,1,0:T(2,128)S(1)} %all_to_all.20.all_ref, bf16[512,3200]{1,0:T(8,128)(2,1)S(1)} %get-tuple-element.29.p_ref, f32[2000,512]{1,0:T(8,128)S(1)} %get-tuple-element.30.expo_ref, f32[16,1536]{1,0:T(8,128)S(1)} %get-tuple-element.22.args_4_.tab_ref), custom_call_target="tpu_custom_call" | custom-call | flops 6291456000 | bytes 9437184 | tf_op jit(solution)/shard_map/pallas_call | solution.py:325
  80.6 21.4 %all_to_all.21 = f32[8,80,384]{2,1,0:T(8,128)S(1)} all-to-all(f32[8,80,384]{2,1,0:T(8,128)S(1)} %shard_map.58), channel_id=1, replica_groups=mesh['y'=4,'xh'=2,'z'=8,'xl'=2,'co'=2] {'y','xh'}, dimensions={0} | all-to-all | bytes 1966080 | tf_op jit(solution)/shard_map/all_to_all | solution.py:377
  102.2 12.2 %all_to_all.22 = f32[8,48,128]{2,1,0:T(8,128)S(1)} all-to-all(f32[8,48,128]{2,1,0:T(8,128)S(1)} %bitcast.10), channel_id=1, replica_groups=mesh['y'=4,'xh'=2,'z'=8,'xl'=2,'co'=2] {'z'}, dimensions={0} | all-to-all | bytes 393216 | tf_op jit(solution)/shard_map/all_to_all | solution.py:379
  114.5 0.8 reshape.15
  (40 shorter events, 2.3 us)
Async XLA Ops:
  0.0 1.0 copy-start
  1.0 0.7 copy-start.1
  1.7 0.7 copy-start.2
  2.4 0.7 copy-start.3
  4.0 12.3 %collective-permute-start.3 = (bf16[32,3200]{1,0:T(8,128)(2,1)S(1)}, bf16[32,3200]{1,0:T(8,128)(2,1)S(1)}, u32[]{:S(2)}, u32[]{:S(2)}) collective-permute-start(bf16[32,3200]{1,0:T(8,128)(2,1)S(1)} %get-tuple-element.19), channel_id=1, source_target_pairs={{0,28},{4,0},{8,4},{12,8},{16,12},{20,16},{24,20},{28,24},{1,29},{... | collective-permute-start | bytes 614408 | tf_op jit(solution)/shard_map/ppermute | solution.py:342
  10.0 9.7 %collective-permute-start = (bf16[32,3200]{1,0:T(8,128)(2,1)S(1)}, bf16[32,3200]{1,0:T(8,128)(2,1)S(1)}, u32[]{:S(2)}, u32[]{:S(2)}) collective-permute-start(bf16[32,3200]{1,0:T(8,128)(2,1)S(1)} %get-tuple-element.19), channel_id=1, source_target_pairs={{0,4},{4,8},{8,12},{12,16},{16,20},{20,24},{24,28},{28,0},{1,5},{5... | collective-permute-start | bytes 614408 | tf_op jit(solution)/shard_map/ppermute | solution.py:342
  11.7 13.9 %all-to-all-start = ((bf16[8,48,128]{2,1,0:T(8,128)(2,1)}), bf16[8,48,128]{2,1,0:T(8,128)(2,1)S(1)}, u32[]{:S(2)}, u32[]{:S(2)}) async-start(bf16[8,48,128]{2,1,0:T(8,128)(2,1)} %pad.8.clone), calls=%async_computation | async-start | bytes 196608 | tf_op jit(solution)/shard_map/all_to_all | solution.py:354
  16.4 11.4 %collective-permute-start.4 = (bf16[32,3200]{1,0:T(8,128)(2,1)S(1)}, bf16[32,3200]{1,0:T(8,128)(2,1)S(1)}, u32[]{:S(2)}, u32[]{:S(2)}) collective-permute-start(bf16[32,3200]{1,0:T(8,128)(2,1)S(1)} %collective-permute-done.3.args_4_), channel_id=1, source_target_pairs={{0,28},{4,0},{8,4},{12,8},{16,12},{20,16},{24,20},{28,24},{1,29},{... | collective-permute-start | bytes 614408 | tf_op jit(solution)/shard_map/ppermute | solution.py:342
  19.6 9.0 %collective-permute-start.1 = (bf16[32,3200]{1,0:T(8,128)(2,1)S(1)}, bf16[32,3200]{1,0:T(8,128)(2,1)S(1)}, u32[]{:S(2)}, u32[]{:S(2)}) collective-permute-start(bf16[32,3200]{1,0:T(8,128)(2,1)S(1)} %collective-permute-done.args_1_), channel_id=1, source_target_pairs={{0,4},{4,8},{8,12},{12,16},{16,20},{20,24},{24,28},{28,0},{1,5},{5... | collective-permute-start | bytes 614408 | tf_op jit(solution)/shard_map/ppermute | solution.py:342
  25.6 6.1 %collective-permute-start.8 = (bf16[384,128]{1,0:T(8,128)(2,1)S(1)}, bf16[384,128]{1,0:T(8,128)(2,1)S(1)}, u32[]{:S(2)}, u32[]{:S(2)}) collective-permute-start(bf16[384,128]{1,0:T(8,128)(2,1)S(1)} %bitcast.13), channel_id=1, source_target_pairs={{0,32},{32,0},{1,33},{33,1},{2,34},{34,2},{3,35},{35,3},{4,36},{36... | collective-permute-start | bytes 294920 | tf_op jit(solution)/shard_map/ppermute | solution.py:356
  27.7 9.3 %collective-permute-start.15 = (bf16[32,3200]{1,0:T(8,128)(2,1)S(1)}, bf16[32,3200]{1,0:T(8,128)(2,1)S(1)}, u32[]{:S(2)}, u32[]{:S(2)}) collective-permute-start(bf16[32,3200]{1,0:T(8,128)(2,1)S(1)} %collective-permute-done.3.args_4_), channel_id=1, source_target_pairs={{0,1},{1,0},{2,3},{3,2},{4,5},{5,4},{6,7},{7,6},{8,9},{9,8},{10,11... | collective-permute-start | bytes 614408 | tf_op jit(solution)/shard_map/ppermute | solution.py:346
  27.8 7.6 %collective-permute-start.5 = (bf16[32,3200]{1,0:T(8,128)(2,1)S(1)}, bf16[32,3200]{1,0:T(8,128)(2,1)S(1)}, u32[]{:S(2)}, u32[]{:S(2)}) collective-permute-start(bf16[32,3200]{1,0:T(8,128)(2,1)S(1)} %collective-permute-done.4.args_5_), channel_id=1, source_target_pairs={{0,28},{4,0},{8,4},{12,8},{16,12},{20,16},{24,20},{28,24},{1,29},{... | collective-permute-start | bytes 614408 | tf_op jit(solution)/shard_map/ppermute | solution.py:342
  28.6 8.3 %collective-permute-start.2 = (bf16[32,3200]{1,0:T(8,128)(2,1)S(1)}, bf16[32,3200]{1,0:T(8,128)(2,1)S(1)}, u32[]{:S(2)}, u32[]{:S(2)}) collective-permute-start(bf16[32,3200]{1,0:T(8,128)(2,1)S(1)} %collective-permute-done.1.args_2_), channel_id=1, source_target_pairs={{0,4},{4,8},{8,12},{12,16},{16,20},{20,24},{24,28},{28,0},{1,5},{5... | collective-permute-start | bytes 614408 | tf_op jit(solution)/shard_map/ppermute | solution.py:342
  31.7 9.7 %collective-permute-start.11 = (bf16[768,128]{1,0:T(8,128)(2,1)S(1)}, bf16[768,128]{1,0:T(8,128)(2,1)S(1)}, u32[]{:S(2)}, u32[]{:S(2)}) collective-permute-start(bf16[768,128]{1,0:T(8,128)(2,1)S(1)} %constant_dynamic-update-slice_fusion.args_0_), channel_id=1, source_target_pairs={{0,192},{64,0},{128,64},{192,128},{1,193},{65,1},{129,65},{193,129... | collective-permute-start | bytes 589832 | tf_op jit(solution)/shard_map/ppermute | solution.py:359
  34.8 9.2 %collective-permute-start.10 = (bf16[768,128]{1,0:T(8,128)(2,1)S(1)}, bf16[768,128]{1,0:T(8,128)(2,1)S(1)}, u32[]{:S(2)}, u32[]{:S(2)}) collective-permute-start(bf16[768,128]{1,0:T(8,128)(2,1)S(1)} %constant_dynamic-update-slice_fusion.args_0_), channel_id=1, source_target_pairs={{0,128},{64,192},{128,0},{192,64},{1,129},{65,193},{129,1},{193,65... | collective-permute-start | bytes 589832 | tf_op jit(solution)/shard_map/ppermute | solution.py:359
  35.5 9.7 %collective-permute-start.9 = (bf16[768,128]{1,0:T(8,128)(2,1)S(1)}, bf16[768,128]{1,0:T(8,128)(2,1)S(1)}, u32[]{:S(2)}, u32[]{:S(2)}) collective-permute-start(bf16[768,128]{1,0:T(8,128)(2,1)S(1)} %constant_dynamic-update-slice_fusion.args_0_), channel_id=1, source_target_pairs={{0,64},{64,128},{128,192},{192,0},{1,65},{65,129},{129,193},{193,1... | collective-permute-start | bytes 589832 | tf_op jit(solution)/shard_map/ppermute | solution.py:359
  36.9 13.4 %collective-permute-start.12 = (bf16[32,3200]{1,0:T(8,128)(2,1)S(1)}, bf16[32,3200]{1,0:T(8,128)(2,1)S(1)}, u32[]{:S(2)}, u32[]{:S(2)}) collective-permute-start(bf16[32,3200]{1,0:T(8,128)(2,1)S(1)} %collective-permute-done.args_1_), channel_id=1, source_target_pairs={{0,1},{1,0},{2,3},{3,2},{4,5},{5,4},{6,7},{7,6},{8,9},{9,8},{10,11... | collective-permute-start | bytes 614408 | tf_op jit(solution)/shard_map/ppermute | solution.py:346
  37.1 8.1 %collective-permute-start.7 = (bf16[16,3200]{1,0:T(8,128)(2,1)S(1)}, bf16[16,3200]{1,0:T(8,128)(2,1)S(1)}, u32[]{:S(2)}, u32[]{:S(2)}) collective-permute-start(bf16[16,3200]{1,0:T(8,128)(2,1)S(1)} %slice.17), channel_id=1, source_target_pairs={{0,28},{4,0},{8,4},{12,8},{16,12},{20,16},{24,20},{28,24},{1,29},{... | collective-permute-start | bytes 307208 | tf_op jit(solution)/shard_map/ppermute | solution.py:342
  41.5 5.9 %collective-permute-start.6 = (bf16[16,3200]{1,0:T(8,128)(2,1)S(1)}, bf16[16,3200]{1,0:T(8,128)(2,1)S(1)}, u32[]{:S(2)}, u32[]{:S(2)}) collective-permute-start(bf16[16,3200]{1,0:T(8,128)(2,1)S(1)} %slice.16), channel_id=1, source_target_pairs={{0,4},{4,8},{8,12},{12,16},{16,20},{20,24},{24,28},{28,0},{1,5},{5... | collective-permute-start | bytes 307208 | tf_op jit(solution)/shard_map/ppermute | solution.py:342
  44.0 7.0 %collective-permute-start.16 = (bf16[32,3200]{1,0:T(8,128)(2,1)S(1)}, bf16[32,3200]{1,0:T(8,128)(2,1)S(1)}, u32[]{:S(2)}, u32[]{:S(2)}) collective-permute-start(bf16[32,3200]{1,0:T(8,128)(2,1)S(1)} %collective-permute-done.4.args_5_), channel_id=1, source_target_pairs={{0,1},{1,0},{2,3},{3,2},{4,5},{5,4},{6,7},{7,6},{8,9},{9,8},{10,11... | collective-permute-start | bytes 614408 | tf_op jit(solution)/shard_map/ppermute | solution.py:346
  45.2 5.9 %collective-permute-start.13 = (bf16[32,3200]{1,0:T(8,128)(2,1)S(1)}, bf16[32,3200]{1,0:T(8,128)(2,1)S(1)}, u32[]{:S(2)}, u32[]{:S(2)}) collective-permute-start(bf16[32,3200]{1,0:T(8,128)(2,1)S(1)} %collective-permute-done.1.args_2_), channel_id=1, source_target_pairs={{0,1},{1,0},{2,3},{3,2},{4,5},{5,4},{6,7},{7,6},{8,9},{9,8},{10,11... | collective-permute-start | bytes 614408 | tf_op jit(solution)/shard_map/ppermute | solution.py:346
  45.2 5.9 %collective-permute-start.17 = (bf16[32,3200]{1,0:T(8,128)(2,1)S(1)}, bf16[32,3200]{1,0:T(8,128)(2,1)S(1)}, u32[]{:S(2)}, u32[]{:S(2)}) collective-permute-start(bf16[32,3200]{1,0:T(8,128)(2,1)S(1)} %collective-permute-done.5.args_6_), channel_id=1, source_target_pairs={{0,1},{1,0},{2,3},{3,2},{4,5},{5,4},{6,7},{7,6},{8,9},{9,8},{10,11... | collective-permute-start | bytes 614408 | tf_op jit(solution)/shard_map/ppermute | solution.py:346
  47.3 3.7 %collective-permute-start.14 = (bf16[32,3200]{1,0:T(8,128)(2,1)S(1)}, bf16[32,3200]{1,0:T(8,128)(2,1)S(1)}, u32[]{:S(2)}, u32[]{:S(2)}) collective-permute-start(bf16[32,3200]{1,0:T(8,128)(2,1)S(1)} %collective-permute-done.2.args_3_), channel_id=1, source_target_pairs={{0,1},{1,0},{2,3},{3,2},{4,5},{5,4},{6,7},{7,6},{8,9},{9,8},{10,11... | collective-permute-start | bytes 614408 | tf_op jit(solution)/shard_map/ppermute | solution.py:346
  50.4 1.5 %collective-permute-start.18 = (bf16[16,3200]{1,0:T(8,128)(2,1)S(1)}, bf16[16,3200]{1,0:T(8,128)(2,1)S(1)}, u32[]{:S(2)}, u32[]{:S(2)}) collective-permute-start(bf16[16,3200]{1,0:T(8,128)(2,1)S(1)} %collective-permute-done.6.args_7_), channel_id=1, source_target_pairs={{0,1},{1,0},{2,3},{3,2},{4,5},{5,4},{6,7},{7,6},{8,9},{9,8},{10,11... | collective-permute-start | bytes 307208 | tf_op jit(solution)/shard_map/ppermute | solution.py:346
  51.0 1.3 %collective-permute-start.19 = (bf16[16,3200]{1,0:T(8,128)(2,1)S(1)}, bf16[16,3200]{1,0:T(8,128)(2,1)S(1)}, u32[]{:S(2)}, u32[]{:S(2)}) collective-permute-start(bf16[16,3200]{1,0:T(8,128)(2,1)S(1)} %collective-permute-done.7.args_8_), channel_id=1, source_target_pairs={{0,1},{1,0},{2,3},{3,2},{4,5},{5,4},{6,7},{7,6},{8,9},{9,8},{10,11... | collective-permute-start | bytes 307208 | tf_op jit(solution)/shard_map/ppermute | solution.py:346

commit v6 on v5

--- a/solution.py
+++ b/solution.py
@@ -113,6 +113,31 @@
     )(images, offsets, class_lists, weight)
 
 
+COLS = 48
+
+
+def split_kernel(ref_ref, out_ref, tall):
+    tall[...] = jnp.zeros_like(tall)
+    tall[: GROUP * ROWS, :COLS] = ref_ref[...].astype(f32).reshape(GROUP * ROWS, COLS)
+    flat = tall[...].T[:COLS]
+    lane = lax.broadcasted_iota(jnp.int32, (COLS, LANES), 1)
+    for m in range(GROUP):
+        part = flat[:, m * ROWS : m * ROWS + LANES]
+        out_ref[m] = jnp.where(lane < ROWS, part, 0.0).astype(bf16)
+
+
+def split_refs(references):
+    return pl.pallas_call(
+        split_kernel,
+        in_specs=[VMEM],
+        out_specs=VMEM,
+        out_shape=jax.ShapeDtypeStruct((GROUP, COLS, LANES), bf16),
+        scratch_shapes=[pltpu.VMEM((6 * LANES, LANES), f32)],
+        compiler_params=pltpu.CompilerParams(vmem_limit_bytes=8 << 20),
+        cost_estimate=pl.CostEstimate(flops=1 << 20, bytes_accessed=1 << 20, transcendentals=0),
+    )(references)
+
+
 def y_shift(tab_ref, gy, lanes):
     row = 2 + 2 * abs(gy)
     c = tab_ref[row : row + 1, lanes]
@@ -120,57 +145,43 @@
     return c, (s if gy > 0 else -s)
 
 
-def shift_kernel(*args):
-    pieces, (tab_ref, out_ref, energy_ref, r_ref, total) = args[:4], args[4:]
+def columns_last(pieces, tab_ref, base, total):
     y, xh = lax.axis_index("y"), lax.axis_index("xh")
+    total[...] = jnp.zeros_like(total)
     for far, ref in enumerate(pieces):
         for n in range(2):
             place = ((y + 4 - far) & 3) * 2 + (xh if n == 0 else 1 - xh)
-            at = pl.multiple_of(place * CHUNK, CHUNK)
-            r_ref[pl.ds(at, CHUNK), :] = ref[n * CHUNK : (n + 1) * CHUNK, :]
-    total[...] = jnp.zeros_like(total)
+            for t in range(CHUNK // LANES):
+                at = place * CHUNK + t * LANES
+                lanes = pl.ds(pl.multiple_of(at, LANES), LANES)
+                wide = pl.ds(pl.multiple_of(at - HALF * (place >= 4), LANES), LANES)
+                row = n * CHUNK + t * LANES
+                value = ref[row : row + LANES, :].astype(f32).T[:PAD]
+                base[:, lanes] = value
+                total[...] += value * value * tab_ref[8:9, wide]
+
+
+def shift_block(gy, tab_ref, base, out_ref):
     for at in range(0, HALF, LANES):
         lanes, ims = slice(at, at + LANES), slice(HALF + at, HALF + at + LANES)
-        all_re = r_ref[lanes, :].astype(f32).T[:PAD]
-        all_im = r_ref[ims, :].astype(f32).T[:PAD]
-        total[...] += (all_re * all_re + all_im * all_im) * tab_ref[8:9, lanes]
         for p in range(0, PAD, 16):
-            for gy in range(-2, 3):
-                yr, yi = all_re[p : p + 16], all_im[p : p + 16]
-                if gy:
-                    c, s = y_shift(tab_ref, gy, lanes)
-                    yr, yi = yr * c - yi * s, yi * c + yr * s
-                mid = ((gy + 2) * GRID + 2) * PAD + p
-                out_ref[mid : mid + 16, lanes] = yr.astype(bf16)
-                out_ref[mid : mid + 16, ims] = yi.astype(bf16)
-                for gx in (1, 2):
-                    c = tab_ref[2 * gx - 2 : 2 * gx - 1, lanes]
-                    s = tab_ref[2 * gx - 1 : 2 * gx, lanes]
-                    cr, ci, sr, si = yr * c, yi * c, yr * s, yi * s
-                    hi = slice(mid + gx * PAD, mid + gx * PAD + 16)
-                    lo = slice(mid - gx * PAD, mid - gx * PAD + 16)
-                    out_ref[hi, lanes] = (cr - si).astype(bf16)
-                    out_ref[hi, ims] = (ci + sr).astype(bf16)
-                    out_ref[lo, lanes] = (cr + si).astype(bf16)
-                    out_ref[lo, ims] = (ci - sr).astype(bf16)
-    energy_ref[...] = jnp.broadcast_to(
-        0.5 * jnp.sum(total[...], axis=1, keepdims=True), energy_ref.shape
-    )
-
-
-def shift_refs(refs, table):
-    return pl.pallas_call(
-        shift_kernel,
-        in_specs=[VMEM] * 5,
-        out_specs=[VMEM] * 2,
-        out_shape=[
-            jax.ShapeDtypeStruct((SHIFTS * PAD, WIDTH), bf16),
-            jax.ShapeDtypeStruct((PAD, LANES), f32),
-        ],
-        scratch_shapes=[pltpu.VMEM((WIDTH, LANES), bf16), pltpu.VMEM((PAD, LANES), f32)],
-        compiler_params=pltpu.CompilerParams(vmem_limit_bytes=16 << 20),
-        cost_estimate=pl.CostEstimate(flops=1, bytes_accessed=1, transcendentals=0),
-    )(*refs, table)
+            yr, yi = base[p : p + 16, lanes], base[p : p + 16, ims]
+            if gy:
+                c, s = y_shift(tab_ref, gy, lanes)
+                yr, yi = yr * c - yi * s, yi * c + yr * s
+            mid = 2 * PAD + p
+            out_ref[mid : mid + 16, lanes] = yr.astype(bf16)
+            out_ref[mid : mid + 16, ims] = yi.astype(bf16)
+            for gx in (1, 2):
+                c = tab_ref[2 * gx - 2 : 2 * gx - 1, lanes]
+                s = tab_ref[2 * gx - 1 : 2 * gx, lanes]
+                cr, ci, sr, si = yr * c, yi * c, yr * s, yi * s
+                hi = slice(mid + gx * PAD, mid + gx * PAD + 16)
+                lo = slice(mid - gx * PAD, mid - gx * PAD + 16)
+                out_ref[hi, lanes] = (cr - si).astype(bf16)
+                out_ref[hi, ims] = (ci + sr).astype(bf16)
+                out_ref[lo, lanes] = (cr + si).astype(bf16)
+                out_ref[lo, ims] = (ci - sr).astype(bf16)
 
 
 def assemble(pieces, probes):
@@ -198,15 +209,18 @@
 
 
 def estep_kernel(*args):
-    pieces, (shifted, energy_ref, probes, expo_ref, stat_ref) = args[:PIECES], args[PIECES:]
+    pieces, refs = args[:PIECES], args[PIECES : PIECES + 4]
+    tab_ref, probes, expo_ref, stat_ref, base, total, *shifted = args[PIECES + 4 :]
+    columns_last(refs, tab_ref, base, total)
+    shift_block(-2, tab_ref, base, shifted[0])
     assemble(name_pieces(pieces), probes)
     cls = lax.axis_index("xl") * 2 + lax.axis_index("co")
-    base = cls * (ROWS * GROUP) + lax.axis_index("z") * ROWS
+    first_row = cls * (ROWS * GROUP) + lax.axis_index("z") * ROWS
     row = lax.broadcasted_iota(jnp.int32, (PAD, LANES), 0)
-    number = ((base + row) * 2731) >> 16
+    number = ((first_row + row) * 2731) >> 16
     lane = lax.broadcasted_iota(jnp.int32, (PAD, LANES), 1)
     pick = jnp.where((number == lane) & (row < ROWS), 1.0, 0.0).astype(bf16)
-    half_energy = energy_ref[:, 0:1]
+    half_energy = 0.5 * jnp.sum(total[...], axis=1, keepdims=True)
     keep = (
         lax.dot_general(
             pick, probes[:, WIDTH:], (((1,), (1,)), ((), ())), preferred_element_type=f32
@@ -215,11 +229,13 @@
     )
     for b in range(GRID):
         cross = lax.dot_general(
-            shifted[b * BLOCK : (b + 1) * BLOCK, :],
+            shifted[b % 2][...],
             probes[:, :WIDTH],
             (((1,), (1,)), ((), ())),
             preferred_element_type=f32,
         )
+        if b < GRID - 1:
+            shift_block(b - 1, tab_ref, base, shifted[(b + 1) % 2])
         best = jnp.full((8, NPART), EXCLUDED, f32)
         for gx in range(GRID):
             at = (b * GRID + gx) * PAD
@@ -244,15 +260,21 @@
     )
 
 
-def estep(pieces, shifted, energy):
+def estep(pieces, refs, table):
     return pl.pallas_call(
         estep_kernel,
-        in_specs=[VMEM] * (PIECES + 2),
+        in_specs=[VMEM] * (PIECES + 5),
         out_specs=[VMEM] * 3,
         out_shape=[
             jax.ShapeDtypeStruct((NPART, WIDTH + LANES), bf16),
             jax.ShapeDtypeStruct((SHIFTS * PAD, NPART), f32),
             jax.ShapeDtypeStruct((16, NPART), f32),
+        ],
+        scratch_shapes=[
+            pltpu.VMEM((PAD, WIDTH), f32),
+            pltpu.VMEM((PAD, LANES), f32),
+            pltpu.VMEM((BLOCK, WIDTH), bf16),
+            pltpu.VMEM((BLOCK, WIDTH), bf16),
         ],
         compiler_params=pltpu.CompilerParams(vmem_limit_bytes=30 << 20),
         cost_estimate=pl.CostEstimate(
@@ -260,7 +282,7 @@
             bytes_accessed=24 << 20,
             transcendentals=SHIFTS * PAD * NPART,
         ),
-    )(*pieces, shifted, energy)
+    )(*pieces, *refs, table)
 
 
 STRIP = 256
@@ -349,15 +371,13 @@
 def per_device(images, offsets, class_lists, noise_weight, references):
     own, half, table = prep(images, offsets.T, class_lists.T, noise_weight)
 
-    part = references.reshape(GROUP, ROWS, 48)
-    part = jnp.pad(jnp.transpose(part, (0, 2, 1)), ((0, 0), (0, 0), (0, LANES - ROWS)))
+    part = split_refs(references)
     part = lax.all_to_all(part, "z", 0, 0).reshape(CHUNK, LANES)
     part, table = lax.optimization_barrier((part, table))
     part = jnp.concatenate([part, lax.ppermute(part, "xh", [(0, 1), (1, 0)])])
     refs = [part]
     for far in (1, 2, 3):
         refs.append(lax.ppermute(part, "y", [(i, (i + far) % 4) for i in range(4)]))
-    shifted, energy = shift_refs(refs, table)
 
     up, down = [half], [half]
     for _ in range(3):
@@ -365,10 +385,10 @@
         down.append(along_z(down[-1], -1))
     cut = PARTS // 4
     mine = up[1:] + down[1:] + [along_z(up[-1][:cut], 1), along_z(down[-1][cut:], -1)]
-    mine[6], mine[7], shifted = lax.optimization_barrier((mine[6], mine[7], shifted))
+    mine[6], mine[7], *refs = lax.optimization_barrier((mine[6], mine[7], *refs))
     pieces = [own] + mine + [to_other_core(x) for x in mine]
 
-    probes, expo, stat = estep(pieces, shifted, energy)
+    probes, expo, stat = estep(pieces, refs, table)
     stats = lax.all_to_all(
         jnp.broadcast_to(stat[5:7], (32, 2, NPART)), ("z", "xl", "co"), 0, 0
     )

time: 116 us -> 116 us (level)
  waiting for transfers between devices: 16.1 us -> 18.7 us
  blocking collectives: 46.9 us -> 45 us
    ppermute x8, waiting for transfers between devices: 1.68 us -> 4.21 us  [along_z(): return lax.ppermute(x, 'z', [(i, (i + far) % GROUP) for i in range(GROUP)])]
    unnamed x11 -> x12, local copies, waits for them, and re-layouts: 3.33 us -> 4.1 us
  transfers between devices with their start and end apart: 21 -> 21, of which waited for: 8 -> 8; matrix products, arithmetic and copies ran while one was open for 2% -> 0% of each run, Pallas kernels for 3% -> 1%
where the time goes in v6:
time: 116 us; the launch traced here: 115 us
  blocking collectives  45 us (39%)
  starting transfers between devices  27.1 us (23%)
  Pallas kernels  19 us (16%)
  waiting for transfers between devices  18.7 us (16%)
  local copies, waits for them, and re-layouts  5.03 us (4%)
    all_to_all x1, blocking collectives, per_device(): sums = jnp.sum(lax.all_to_all(sums, ('y', 'xh'), 0, 0), axis=0)  20.3 us
    ppermute x8, starting transfers between devices, along_z(): return lax.ppermute(x, 'z', [(i, (i + far) % GROUP) for i in range(GROUP)])  13.9 us
    all_to_all x1, blocking collectives, per_device(): lax.all_to_all(jnp.broadcast_to(stat[5:7], (32, 2, NPART)), ('z', 'xl', '...  12.5 us
    all_to_all x1, blocking collectives, per_device(): sums = lax.all_to_all(sums, 'z', 0, 0)[:, :, :ROWS]  12.2 us
    pallas_call x1, Pallas kernels, estep(): pl.pallas_call(estep_kernel, in_specs=[VMEM] * (PIECES + 5), out_specs=[V...  10.2 us
    pallas_call x1, Pallas kernels, mstep(): pl.pallas_call(mstep_kernel, in_specs=[VMEM] * 5, out_specs=VMEM, out_sha...  7.01 us
    all_to_all x1, waiting for transfers between devices, per_device(): part = lax.all_to_all(part, 'z', 0, 0).reshape(CHUNK, LANES)  5.97 us
    ppermute x3, waiting for transfers between devices, per_device(): refs.append(lax.ppermute(part, 'y', [(i, (i + far) % 4) for i in range(4)]))  5.49 us
  transfers between devices with their start and end apart: 21, of which 8 were waited for; matrix products, arithmetic and copies ran while one was open for 0% of the time, Pallas kernels for 1%

profile of v6, /device:TPU:2, one launch (start us, length us, event | category | flops | bytes accessed | tf_op | source)
XLA Modules:
  0.0 115.1 jit_solution(5674937790734133098)
XLA Ops:
  0.0 1.0 copy-done
  1.0 0.7 copy-done.2
  1.7 0.7 copy-done.3
  2.4 0.7 copy-done.4
  3.1 1.0 shard_map.55
  4.0 5.9 %collective-permute-start.3 = (bf16[32,3200]{1,0:T(8,128)(2,1)S(1)}, bf16[32,3200]{1,0:T(8,128)(2,1)S(1)}, u32[]{:S(2)}, u32[]{:S(2)}) collective-permute-start(bf16[32,3200]{1,0:T(8,128)(2,1)S(1)} %get-tuple-element.20), channel_id=1, source_target_pairs={{0,28},{4,0},{8,4},{12,8},{16,12},{20,16},{24,20},{28,24},{1,29},{... | collective-permute-start | bytes 614408 | tf_op jit(solution)/shard_map/ppermute | solution.py:364
  10.0 0.9 copy-done.1
  10.9 0.9 shard_map.56
  11.8 4.6 %all-to-all-start = ((bf16[8,48,128]{2,1,0:T(8,128)(2,1)}), bf16[8,48,128]{2,1,0:T(8,128)(2,1)S(1)}, u32[]{:S(2)}, u32[]{:S(2)}) async-start(bf16[8,48,128]{2,1,0:T(8,128)(2,1)} %shard_map.56), calls=%async_computation | async-start | bytes 196608 | tf_op jit(solution)/shard_map/all_to_all | solution.py:375
  16.4 3.2 %collective-permute-start.4 = (bf16[32,3200]{1,0:T(8,128)(2,1)S(1)}, bf16[32,3200]{1,0:T(8,128)(2,1)S(1)}, u32[]{:S(2)}, u32[]{:S(2)}) collective-permute-start(bf16[32,3200]{1,0:T(8,128)(2,1)S(1)} %collective-permute-done.3.args_4_), channel_id=1, source_target_pairs={{0,28},{4,0},{8,4},{12,8},{16,12},{20,16},{24,20},{28,24},{1,29},{... | collective-permute-start | bytes 614408 | tf_op jit(solution)/shard_map/ppermute | solution.py:364
  19.6 6.0 %all-to-all-done = bf16[8,48,128]{2,1,0:T(8,128)(2,1)S(1)} async-done(((bf16[8,48,128]{2,1,0:T(8,128)(2,1)}), bf16[8,48,128]{2,1,0:T(8,128)(2,1)S(1)}, u32[]{:S(2)}, u32[]{:S(2)}) %all-to-all-start) | async-done | bytes 98336 | tf_op jit(solution)/shard_map/all_to_all | solution.py:375
  25.6 2.1 %collective-permute-start.8 = (bf16[384,128]{1,0:T(8,128)(2,1)S(1)}, bf16[384,128]{1,0:T(8,128)(2,1)S(1)}, u32[]{:S(2)}, u32[]{:S(2)}) collective-permute-start(bf16[384,128]{1,0:T(8,128)(2,1)S(1)} %bitcast.11), channel_id=1, source_target_pairs={{0,32},{32,0},{1,33},{33,1},{2,34},{34,2},{3,35},{35,3},{4,36},{36... | collective-permute-start | bytes 294920 | tf_op jit(solution)/shard_map/ppermute | solution.py:377
  27.9 0.7 collective-permute-start.5
  28.6 1.4 %collective-permute-start.2 = (bf16[32,3200]{1,0:T(8,128)(2,1)S(1)}, bf16[32,3200]{1,0:T(8,128)(2,1)S(1)}, u32[]{:S(2)}, u32[]{:S(2)}) collective-permute-start(bf16[32,3200]{1,0:T(8,128)(2,1)S(1)} %collective-permute-done.1.args_2_), channel_id=1, source_target_pairs={{0,4},{4,8},{8,12},{12,16},{16,20},{20,24},{24,28},{28,0},{1,5},{5... | collective-permute-start | bytes 614408 | tf_op jit(solution)/shard_map/ppermute | solution.py:364
  30.0 1.8 %collective-permute-done.8 = bf16[384,128]{1,0:T(8,128)(2,1)S(1)} collective-permute-done((bf16[384,128]{1,0:T(8,128)(2,1)S(1)}, bf16[384,128]{1,0:T(8,128)(2,1)S(1)}, u32[]{:S(2)}, u32[]{:S(2)}) %collective-permute-start.8) | collective-permute-done | bytes 98336 | tf_op jit(solution)/shard_map/ppermute | solution.py:377
  31.8 3.1 %collective-permute-start.11 = (bf16[768,128]{1,0:T(8,128)(2,1)S(1)}, bf16[768,128]{1,0:T(8,128)(2,1)S(1)}, u32[]{:S(2)}, u32[]{:S(2)}) collective-permute-start(bf16[768,128]{1,0:T(8,128)(2,1)S(1)} %constant_dynamic-update-slice_fusion.args_17_), channel_id=1, source_target_pairs={{0,192},{64,0},{128,64},{192,128},{1,193},{65,1},{129,65},{193,129... | collective-permute-start | bytes 589832 | tf_op jit(solution)/shard_map/ppermute | solution.py:380
  34.8 0.6 collective-permute-start.10
  35.5 1.4 %collective-permute-start.9 = (bf16[768,128]{1,0:T(8,128)(2,1)S(1)}, bf16[768,128]{1,0:T(8,128)(2,1)S(1)}, u32[]{:S(2)}, u32[]{:S(2)}) collective-permute-start(bf16[768,128]{1,0:T(8,128)(2,1)S(1)} %constant_dynamic-update-slice_fusion.args_17_), channel_id=1, source_target_pairs={{0,64},{64,128},{128,192},{192,0},{1,65},{65,129},{129,193},{193,1... | collective-permute-start | bytes 589832 | tf_op jit(solution)/shard_map/ppermute | solution.py:380
  37.1 1.9 %collective-permute-start.7 = (bf16[16,3200]{1,0:T(8,128)(2,1)S(1)}, bf16[16,3200]{1,0:T(8,128)(2,1)S(1)}, u32[]{:S(2)}, u32[]{:S(2)}) collective-permute-start(bf16[16,3200]{1,0:T(8,128)(2,1)S(1)} %slice.17), channel_id=1, source_target_pairs={{0,28},{4,0},{8,4},{12,8},{16,12},{20,16},{24,20},{28,24},{1,29},{... | collective-permute-start | bytes 307208 | tf_op jit(solution)/shard_map/ppermute | solution.py:364
  39.0 2.5 %collective-permute-done.11.args_20_ = bf16[768,128]{1,0:T(8,128)(2,1)S(1)} collective-permute-done((bf16[768,128]{1,0:T(8,128)(2,1)S(1)}, bf16[768,128]{1,0:T(8,128)(2,1)S(1)}, u32[]{:S(2)}, u32[]{:S(2)}) %collective-permute-start.11) | collective-permute-done | bytes 196640 | tf_op jit(solution)/shard_map/ppermute | solution.py:380
  41.5 2.5 %collective-permute-done.10.args_19_ = bf16[768,128]{1,0:T(8,128)(2,1)S(1)} collective-permute-done((bf16[768,128]{1,0:T(8,128)(2,1)S(1)}, bf16[768,128]{1,0:T(8,128)(2,1)S(1)}, u32[]{:S(2)}, u32[]{:S(2)}) %collective-permute-start.10) | collective-permute-done | bytes 196640 | tf_op jit(solution)/shard_map/ppermute | solution.py:380
  44.0 0.7 collective-permute-start.6
  45.2 0.5 collective-permute-start.17
  45.7 4.2 %collective-permute-done.6.args_7_ = bf16[16,3200]{1,0:T(8,128)(2,1)S(1)} collective-permute-done((bf16[16,3200]{1,0:T(8,128)(2,1)S(1)}, bf16[16,3200]{1,0:T(8,128)(2,1)S(1)}, u32[]{:S(2)}, u32[]{:S(2)}) %collective-permute-start.6) | collective-permute-done | bytes 102432 | tf_op jit(solution)/shard_map/ppermute | solution.py:364
  49.9 0.5 collective-permute-start.18
  50.5 1.0 collective-permute-done.18.args_15_
  51.7 10.2 %shard_map.57 = (bf16[512,3200]{1,0:T(8,128)(2,1)S(1)}, f32[2000,512]{1,0:T(8,128)S(1)}, f32[16,512]{1,0:T(8,128)S(1)}) custom-call(bf16[64,3200]{1,0:T(8,128)(2,1)S(1)} %get-tuple-element.19.args_0_, bf16[32,3200]{1,0:T(8,128)(2,1)S(1)} %collective-permute-done.args_1_, bf16[32,3200]{1,0:T(8,128)(2,1)S(1)} %collective-permute-done.1.args_2_, ...), custom_call_target="tpu_custom_call" | custom-call | flops 6291456000 | bytes 25165824 | tf_op jit(solution)/shard_map/pallas_call | solution.py:264
  62.0 12.5 %all_to_all.20.all_ref = f32[32,2,512]{2,1,0:T(2,128)S(1)} all-to-all(f32[32,2,512]{2,1,0:T(2,128)S(1)} %broadcast_in_dim.3), channel_id=1, replica_groups=mesh['y'=4,'xh'=2,'z'=8,'xl'=2,'co'=2] {'z','xl','co'}, dimensions={0} | all-to-all | bytes 262144 | tf_op jit(solution)/shard_map/all_to_all | solution.py:392
  74.5 7.0 %shard_map.58 = f32[8,80,384]{2,1,0:T(8,128)S(1)} custom-call(f32[16,512]{1,0:T(8,128)S(1)} %get-tuple-element.30.stat_ref, f32[32,2,512]{2,1,0:T(2,128)S(1)} %all_to_all.20.all_ref, bf16[512,3200]{1,0:T(8,128)(2,1)S(1)} %get-tuple-element.31.p_ref, f32[2000,512]{1,0:T(8,128)S(1)} %get-tuple-element.32.expo_ref, ...), custom_call_target="tpu_custom_call" | custom-call | flops 6291456000 | bytes 9437184 | tf_op jit(solution)/shard_map/pallas_call | solution.py:347
  81.5 20.3 %all_to_all.21 = f32[8,80,384]{2,1,0:T(8,128)S(1)} all-to-all(f32[8,80,384]{2,1,0:T(8,128)S(1)} %shard_map.58), channel_id=1, replica_groups=mesh['y'=4,'xh'=2,'z'=8,'xl'=2,'co'=2] {'y','xh'}, dimensions={0} | all-to-all | bytes 1966080 | tf_op jit(solution)/shard_map/all_to_all | solution.py:397
  102.0 12.2 %all_to_all.22 = f32[8,48,128]{2,1,0:T(8,128)S(1)} all-to-all(f32[8,48,128]{2,1,0:T(8,128)S(1)} %bitcast.9), channel_id=1, replica_groups=mesh['y'=4,'xh'=2,'z'=8,'xl'=2,'co'=2] {'z'}, dimensions={0} | all-to-all | bytes 393216 | tf_op jit(solution)/shard_map/all_to_all | solution.py:399
  114.3 0.8 reshape.11
  (39 shorter events, 1.4 us)
Async XLA Ops:
  0.0 1.0 copy-start
  1.0 0.7 copy-start.2
  1.7 0.7 copy-start.3
  2.4 0.7 copy-start.4
  4.0 12.4 %collective-permute-start.3 = (bf16[32,3200]{1,0:T(8,128)(2,1)S(1)}, bf16[32,3200]{1,0:T(8,128)(2,1)S(1)}, u32[]{:S(2)}, u32[]{:S(2)}) collective-permute-start(bf16[32,3200]{1,0:T(8,128)(2,1)S(1)} %get-tuple-element.20), channel_id=1, source_target_pairs={{0,28},{4,0},{8,4},{12,8},{16,12},{20,16},{24,20},{28,24},{1,29},{... | collective-permute-start | bytes 614408 | tf_op jit(solution)/shard_map/ppermute | solution.py:364
  10.0 9.7 %collective-permute-start = (bf16[32,3200]{1,0:T(8,128)(2,1)S(1)}, bf16[32,3200]{1,0:T(8,128)(2,1)S(1)}, u32[]{:S(2)}, u32[]{:S(2)}) collective-permute-start(bf16[32,3200]{1,0:T(8,128)(2,1)S(1)} %get-tuple-element.20), channel_id=1, source_target_pairs={{0,4},{4,8},{8,12},{12,16},{16,20},{20,24},{24,28},{28,0},{1,5},{5... | collective-permute-start | bytes 614408 | tf_op jit(solution)/shard_map/ppermute | solution.py:364
  10.0 0.9 copy-start.1
  11.8 13.9 %all-to-all-start = ((bf16[8,48,128]{2,1,0:T(8,128)(2,1)}), bf16[8,48,128]{2,1,0:T(8,128)(2,1)S(1)}, u32[]{:S(2)}, u32[]{:S(2)}) async-start(bf16[8,48,128]{2,1,0:T(8,128)(2,1)} %shard_map.56), calls=%async_computation | async-start | bytes 196608 | tf_op jit(solution)/shard_map/all_to_all | solution.py:375
  16.4 11.4 %collective-permute-start.4 = (bf16[32,3200]{1,0:T(8,128)(2,1)S(1)}, bf16[32,3200]{1,0:T(8,128)(2,1)S(1)}, u32[]{:S(2)}, u32[]{:S(2)}) collective-permute-start(bf16[32,3200]{1,0:T(8,128)(2,1)S(1)} %collective-permute-done.3.args_4_), channel_id=1, source_target_pairs={{0,28},{4,0},{8,4},{12,8},{16,12},{20,16},{24,20},{28,24},{1,29},{... | collective-permute-start | bytes 614408 | tf_op jit(solution)/shard_map/ppermute | solution.py:364
  19.6 9.0 %collective-permute-start.1 = (bf16[32,3200]{1,0:T(8,128)(2,1)S(1)}, bf16[32,3200]{1,0:T(8,128)(2,1)S(1)}, u32[]{:S(2)}, u32[]{:S(2)}) collective-permute-start(bf16[32,3200]{1,0:T(8,128)(2,1)S(1)} %collective-permute-done.args_1_), channel_id=1, source_target_pairs={{0,4},{4,8},{8,12},{12,16},{16,20},{20,24},{24,28},{28,0},{1,5},{5... | collective-permute-start | bytes 614408 | tf_op jit(solution)/shard_map/ppermute | solution.py:364
  25.6 6.1 %collective-permute-start.8 = (bf16[384,128]{1,0:T(8,128)(2,1)S(1)}, bf16[384,128]{1,0:T(8,128)(2,1)S(1)}, u32[]{:S(2)}, u32[]{:S(2)}) collective-permute-start(bf16[384,128]{1,0:T(8,128)(2,1)S(1)} %bitcast.11), channel_id=1, source_target_pairs={{0,32},{32,0},{1,33},{33,1},{2,34},{34,2},{3,35},{35,3},{4,36},{36... | collective-permute-start | bytes 294920 | tf_op jit(solution)/shard_map/ppermute | solution.py:377
  27.7 9.3 %collective-permute-start.15 = (bf16[32,3200]{1,0:T(8,128)(2,1)S(1)}, bf16[32,3200]{1,0:T(8,128)(2,1)S(1)}, u32[]{:S(2)}, u32[]{:S(2)}) collective-permute-start(bf16[32,3200]{1,0:T(8,128)(2,1)S(1)} %collective-permute-done.3.args_4_), channel_id=1, source_target_pairs={{0,1},{1,0},{2,3},{3,2},{4,5},{5,4},{6,7},{7,6},{8,9},{9,8},{10,11... | collective-permute-start | bytes 614408 | tf_op jit(solution)/shard_map/ppermute | solution.py:368
  27.9 7.6 %collective-permute-start.5 = (bf16[32,3200]{1,0:T(8,128)(2,1)S(1)}, bf16[32,3200]{1,0:T(8,128)(2,1)S(1)}, u32[]{:S(2)}, u32[]{:S(2)}) collective-permute-start(bf16[32,3200]{1,0:T(8,128)(2,1)S(1)} %collective-permute-done.4.args_5_), channel_id=1, source_target_pairs={{0,28},{4,0},{8,4},{12,8},{16,12},{20,16},{24,20},{28,24},{1,29},{... | collective-permute-start | bytes 614408 | tf_op jit(solution)/shard_map/ppermute | solution.py:364
  28.6 8.3 %collective-permute-start.2 = (bf16[32,3200]{1,0:T(8,128)(2,1)S(1)}, bf16[32,3200]{1,0:T(8,128)(2,1)S(1)}, u32[]{:S(2)}, u32[]{:S(2)}) collective-permute-start(bf16[32,3200]{1,0:T(8,128)(2,1)S(1)} %collective-permute-done.1.args_2_), channel_id=1, source_target_pairs={{0,4},{4,8},{8,12},{12,16},{16,20},{20,24},{24,28},{28,0},{1,5},{5... | collective-permute-start | bytes 614408 | tf_op jit(solution)/shard_map/ppermute | solution.py:364
  31.8 9.7 %collective-permute-start.11 = (bf16[768,128]{1,0:T(8,128)(2,1)S(1)}, bf16[768,128]{1,0:T(8,128)(2,1)S(1)}, u32[]{:S(2)}, u32[]{:S(2)}) collective-permute-start(bf16[768,128]{1,0:T(8,128)(2,1)S(1)} %constant_dynamic-update-slice_fusion.args_17_), channel_id=1, source_target_pairs={{0,192},{64,0},{128,64},{192,128},{1,193},{65,1},{129,65},{193,129... | collective-permute-start | bytes 589832 | tf_op jit(solution)/shard_map/ppermute | solution.py:380
  34.8 9.2 %collective-permute-start.10 = (bf16[768,128]{1,0:T(8,128)(2,1)S(1)}, bf16[768,128]{1,0:T(8,128)(2,1)S(1)}, u32[]{:S(2)}, u32[]{:S(2)}) collective-permute-start(bf16[768,128]{1,0:T(8,128)(2,1)S(1)} %constant_dynamic-update-slice_fusion.args_17_), channel_id=1, source_target_pairs={{0,128},{64,192},{128,0},{192,64},{1,129},{65,193},{129,1},{193,65... | collective-permute-start | bytes 589832 | tf_op jit(solution)/shard_map/ppermute | solution.py:380
  35.5 9.7 %collective-permute-start.9 = (bf16[768,128]{1,0:T(8,128)(2,1)S(1)}, bf16[768,128]{1,0:T(8,128)(2,1)S(1)}, u32[]{:S(2)}, u32[]{:S(2)}) collective-permute-start(bf16[768,128]{1,0:T(8,128)(2,1)S(1)} %constant_dynamic-update-slice_fusion.args_17_), channel_id=1, source_target_pairs={{0,64},{64,128},{128,192},{192,0},{1,65},{65,129},{129,193},{193,1... | collective-permute-start | bytes 589832 | tf_op jit(solution)/shard_map/ppermute | solution.py:380
  36.9 12.9 %collective-permute-start.12 = (bf16[32,3200]{1,0:T(8,128)(2,1)S(1)}, bf16[32,3200]{1,0:T(8,128)(2,1)S(1)}, u32[]{:S(2)}, u32[]{:S(2)}) collective-permute-start(bf16[32,3200]{1,0:T(8,128)(2,1)S(1)} %collective-permute-done.args_1_), channel_id=1, source_target_pairs={{0,1},{1,0},{2,3},{3,2},{4,5},{5,4},{6,7},{7,6},{8,9},{9,8},{10,11... | collective-permute-start | bytes 614408 | tf_op jit(solution)/shard_map/ppermute | solution.py:368
  37.1 8.1 %collective-permute-start.7 = (bf16[16,3200]{1,0:T(8,128)(2,1)S(1)}, bf16[16,3200]{1,0:T(8,128)(2,1)S(1)}, u32[]{:S(2)}, u32[]{:S(2)}) collective-permute-start(bf16[16,3200]{1,0:T(8,128)(2,1)S(1)} %slice.17), channel_id=1, source_target_pairs={{0,28},{4,0},{8,4},{12,8},{16,12},{20,16},{24,20},{28,24},{1,29},{... | collective-permute-start | bytes 307208 | tf_op jit(solution)/shard_map/ppermute | solution.py:364
  41.5 8.9 %collective-permute-start.16 = (bf16[32,3200]{1,0:T(8,128)(2,1)S(1)}, bf16[32,3200]{1,0:T(8,128)(2,1)S(1)}, u32[]{:S(2)}, u32[]{:S(2)}) collective-permute-start(bf16[32,3200]{1,0:T(8,128)(2,1)S(1)} %collective-permute-done.4.args_5_), channel_id=1, source_target_pairs={{0,1},{1,0},{2,3},{3,2},{4,5},{5,4},{6,7},{7,6},{8,9},{9,8},{10,11... | collective-permute-start | bytes 614408 | tf_op jit(solution)/shard_map/ppermute | solution.py:368
  44.0 5.9 %collective-permute-start.6 = (bf16[16,3200]{1,0:T(8,128)(2,1)S(1)}, bf16[16,3200]{1,0:T(8,128)(2,1)S(1)}, u32[]{:S(2)}, u32[]{:S(2)}) collective-permute-start(bf16[16,3200]{1,0:T(8,128)(2,1)S(1)} %slice.16), channel_id=1, source_target_pairs={{0,4},{4,8},{8,12},{12,16},{16,20},{20,24},{24,28},{28,0},{1,5},{5... | collective-permute-start | bytes 307208 | tf_op jit(solution)/shard_map/ppermute | solution.py:364
  45.2 5.3 %collective-permute-start.13 = (bf16[32,3200]{1,0:T(8,128)(2,1)S(1)}, bf16[32,3200]{1,0:T(8,128)(2,1)S(1)}, u32[]{:S(2)}, u32[]{:S(2)}) collective-permute-start(bf16[32,3200]{1,0:T(8,128)(2,1)S(1)} %collective-permute-done.1.args_2_), channel_id=1, source_target_pairs={{0,1},{1,0},{2,3},{3,2},{4,5},{5,4},{6,7},{7,6},{8,9},{9,8},{10,11... | collective-permute-start | bytes 614408 | tf_op jit(solution)/shard_map/ppermute | solution.py:368
  45.2 5.3 %collective-permute-start.17 = (bf16[32,3200]{1,0:T(8,128)(2,1)S(1)}, bf16[32,3200]{1,0:T(8,128)(2,1)S(1)}, u32[]{:S(2)}, u32[]{:S(2)}) collective-permute-start(bf16[32,3200]{1,0:T(8,128)(2,1)S(1)} %collective-permute-done.5.args_6_), channel_id=1, source_target_pairs={{0,1},{1,0},{2,3},{3,2},{4,5},{5,4},{6,7},{7,6},{8,9},{9,8},{10,11... | collective-permute-start | bytes 614408 | tf_op jit(solution)/shard_map/ppermute | solution.py:368
  49.9 1.8 %collective-permute-start.14 = (bf16[32,3200]{1,0:T(8,128)(2,1)S(1)}, bf16[32,3200]{1,0:T(8,128)(2,1)S(1)}, u32[]{:S(2)}, u32[]{:S(2)}) collective-permute-start(bf16[32,3200]{1,0:T(8,128)(2,1)S(1)} %collective-permute-done.2.args_3_), channel_id=1, source_target_pairs={{0,1},{1,0},{2,3},{3,2},{4,5},{5,4},{6,7},{7,6},{8,9},{9,8},{10,11... | collective-permute-start | bytes 614408 | tf_op jit(solution)/shard_map/ppermute | solution.py:368
  49.9 1.6 %collective-permute-start.18 = (bf16[16,3200]{1,0:T(8,128)(2,1)S(1)}, bf16[16,3200]{1,0:T(8,128)(2,1)S(1)}, u32[]{:S(2)}, u32[]{:S(2)}) collective-permute-start(bf16[16,3200]{1,0:T(8,128)(2,1)S(1)} %collective-permute-done.6.args_7_), channel_id=1, source_target_pairs={{0,1},{1,0},{2,3},{3,2},{4,5},{5,4},{6,7},{7,6},{8,9},{9,8},{10,11... | collective-permute-start | bytes 307208 | tf_op jit(solution)/shard_map/ppermute | solution.py:368
  50.4 1.3 %collective-permute-start.19 = (bf16[16,3200]{1,0:T(8,128)(2,1)S(1)}, bf16[16,3200]{1,0:T(8,128)(2,1)S(1)}, u32[]{:S(2)}, u32[]{:S(2)}) collective-permute-start(bf16[16,3200]{1,0:T(8,128)(2,1)S(1)} %collective-permute-done.7.args_8_), channel_id=1, source_target_pairs={{0,1},{1,0},{2,3},{3,2},{4,5},{5,4},{6,7},{7,6},{8,9},{9,8},{10,11... | collective-permute-start | bytes 307208 | tf_op jit(solution)/shard_map/ppermute | solution.py:368

commit v7 on v6

--- a/solution.py
+++ b/solution.py
@@ -161,8 +161,8 @@
                 total[...] += value * value * tab_ref[8:9, wide]
 
 
-def shift_block(gy, tab_ref, base, out_ref):
-    for at in range(0, HALF, LANES):
+def shift_block(gy, tab_ref, base, out_ref, first=0, end=HALF):
+    for at in range(first, end, LANES):
         lanes, ims = slice(at, at + LANES), slice(HALF + at, HALF + at + LANES)
         for p in range(0, PAD, 16):
             yr, yi = base[p : p + 16, lanes], base[p : p + 16, ims]
@@ -228,14 +228,20 @@
         > 0.5
     )
     for b in range(GRID):
-        cross = lax.dot_general(
-            shifted[b % 2][...],
-            probes[:, :WIDTH],
-            (((1,), (1,)), ((), ())),
-            preferred_element_type=f32,
-        )
-        if b < GRID - 1:
-            shift_block(b - 1, tab_ref, base, shifted[(b + 1) % 2])
+        cross = []
+        for h in range(2):
+            cross.append(
+                lax.dot_general(
+                    shifted[b % 2][...],
+                    probes[h * NPART // 2 : (h + 1) * NPART // 2, :WIDTH],
+                    (((1,), (1,)), ((), ())),
+                    preferred_element_type=f32,
+                )
+            )
+            if b < GRID - 1:
+                first, end = h * HALF // 2, (h + 1) * HALF // 2
+                shift_block(b - 1, tab_ref, base, shifted[(b + 1) % 2], first, end)
+        cross = jnp.concatenate(cross, axis=1)
         best = jnp.full((8, NPART), EXCLUDED, f32)
         for gx in range(GRID):
             at = (b * GRID + gx) * PAD

time: 116 us -> 115 us (level)
  no operation moved by 1% of the time
where the time goes in v7:
time: 115 us
  blocking collectives  45 us (39%)
  starting transfers between devices  27.1 us (24%)
  Pallas kernels  18.9 us (16%)
  waiting for transfers between devices  18.7 us (16%)
  local copies, waits for them, and re-layouts  5.03 us (4%)
    all_to_all x1, blocking collectives, per_device(): sums = jnp.sum(lax.all_to_all(sums, ('y', 'xh'), 0, 0), axis=0)  20.3 us
    ppermute x8, starting transfers between devices, along_z(): return lax.ppermute(x, 'z', [(i, (i + far) % GROUP) for i in range(GROUP)])  13.9 us
    all_to_all x1, blocking collectives, per_device(): lax.all_to_all(jnp.broadcast_to(stat[5:7], (32, 2, NPART)), ('z', 'xl', '...  12.5 us
    all_to_all x1, blocking collectives, per_device(): sums = lax.all_to_all(sums, 'z', 0, 0)[:, :, :ROWS]  12.2 us
    pallas_call x1, Pallas kernels, estep(): pl.pallas_call(estep_kernel, in_specs=[VMEM] * (PIECES + 5), out_specs=[V...  10 us
    pallas_call x1, Pallas kernels, mstep(): pl.pallas_call(mstep_kernel, in_specs=[VMEM] * 5, out_specs=VMEM, out_sha...  7 us
    all_to_all x1, waiting for transfers between devices, per_device(): part = lax.all_to_all(part, 'z', 0, 0).reshape(CHUNK, LANES)  5.97 us
    ppermute x3, waiting for transfers between devices, per_device(): refs.append(lax.ppermute(part, 'y', [(i, (i + far) % 4) for i in range(4)]))  5.49 us
  transfers between devices with their start and end apart: 21, of which 8 were waited for; matrix products, arithmetic and copies ran while one was open for 0% of the time, Pallas kernels for 1%

profile of v7, /device:TPU:2, one launch (start us, length us, event | category | flops | bytes accessed | tf_op | source)
XLA Modules:
  0.0 114.9 jit_solution(4251015759179516756)
XLA Ops:
  0.0 1.0 copy-done
  1.0 0.7 copy-done.2
  1.7 0.7 copy-done.3
  2.4 0.7 copy-done.4
  3.1 1.0 shard_map.55
  4.0 5.9 %collective-permute-start.3 = (bf16[32,3200]{1,0:T(8,128)(2,1)S(1)}, bf16[32,3200]{1,0:T(8,128)(2,1)S(1)}, u32[]{:S(2)}, u32[]{:S(2)}) collective-permute-start(bf16[32,3200]{1,0:T(8,128)(2,1)S(1)} %get-tuple-element.20), channel_id=1, source_target_pairs={{0,28},{4,0},{8,4},{12,8},{16,12},{20,16},{24,20},{28,24},{1,29},{... | collective-permute-start | bytes 614408 | tf_op jit(solution)/shard_map/ppermute | solution.py:370
  10.0 0.9 copy-done.1
  10.9 0.9 shard_map.56
  11.8 4.6 %all-to-all-start = ((bf16[8,48,128]{2,1,0:T(8,128)(2,1)}), bf16[8,48,128]{2,1,0:T(8,128)(2,1)S(1)}, u32[]{:S(2)}, u32[]{:S(2)}) async-start(bf16[8,48,128]{2,1,0:T(8,128)(2,1)} %shard_map.56), calls=%async_computation | async-start | bytes 196608 | tf_op jit(solution)/shard_map/all_to_all | solution.py:381
  16.4 3.2 %collective-permute-start.4 = (bf16[32,3200]{1,0:T(8,128)(2,1)S(1)}, bf16[32,3200]{1,0:T(8,128)(2,1)S(1)}, u32[]{:S(2)}, u32[]{:S(2)}) collective-permute-start(bf16[32,3200]{1,0:T(8,128)(2,1)S(1)} %collective-permute-done.3.args_4_), channel_id=1, source_target_pairs={{0,28},{4,0},{8,4},{12,8},{16,12},{20,16},{24,20},{28,24},{1,29},{... | collective-permute-start | bytes 614408 | tf_op jit(solution)/shard_map/ppermute | solution.py:370
  19.6 6.0 %all-to-all-done = bf16[8,48,128]{2,1,0:T(8,128)(2,1)S(1)} async-done(((bf16[8,48,128]{2,1,0:T(8,128)(2,1)}), bf16[8,48,128]{2,1,0:T(8,128)(2,1)S(1)}, u32[]{:S(2)}, u32[]{:S(2)}) %all-to-all-start) | async-done | bytes 98336 | tf_op jit(solution)/shard_map/all_to_all | solution.py:381
  25.6 2.1 %collective-permute-start.8 = (bf16[384,128]{1,0:T(8,128)(2,1)S(1)}, bf16[384,128]{1,0:T(8,128)(2,1)S(1)}, u32[]{:S(2)}, u32[]{:S(2)}) collective-permute-start(bf16[384,128]{1,0:T(8,128)(2,1)S(1)} %bitcast.11), channel_id=1, source_target_pairs={{0,32},{32,0},{1,33},{33,1},{2,34},{34,2},{3,35},{35,3},{4,36},{36... | collective-permute-start | bytes 294920 | tf_op jit(solution)/shard_map/ppermute | solution.py:383
  27.9 0.7 collective-permute-start.5
  28.6 1.4 %collective-permute-start.2 = (bf16[32,3200]{1,0:T(8,128)(2,1)S(1)}, bf16[32,3200]{1,0:T(8,128)(2,1)S(1)}, u32[]{:S(2)}, u32[]{:S(2)}) collective-permute-start(bf16[32,3200]{1,0:T(8,128)(2,1)S(1)} %collective-permute-done.1.args_2_), channel_id=1, source_target_pairs={{0,4},{4,8},{8,12},{12,16},{16,20},{20,24},{24,28},{28,0},{1,5},{5... | collective-permute-start | bytes 614408 | tf_op jit(solution)/shard_map/ppermute | solution.py:370
  30.0 1.8 %collective-permute-done.8 = bf16[384,128]{1,0:T(8,128)(2,1)S(1)} collective-permute-done((bf16[384,128]{1,0:T(8,128)(2,1)S(1)}, bf16[384,128]{1,0:T(8,128)(2,1)S(1)}, u32[]{:S(2)}, u32[]{:S(2)}) %collective-permute-start.8) | collective-permute-done | bytes 98336 | tf_op jit(solution)/shard_map/ppermute | solution.py:383
  31.8 3.1 %collective-permute-start.11 = (bf16[768,128]{1,0:T(8,128)(2,1)S(1)}, bf16[768,128]{1,0:T(8,128)(2,1)S(1)}, u32[]{:S(2)}, u32[]{:S(2)}) collective-permute-start(bf16[768,128]{1,0:T(8,128)(2,1)S(1)} %constant_dynamic-update-slice_fusion.args_17_), channel_id=1, source_target_pairs={{0,192},{64,0},{128,64},{192,128},{1,193},{65,1},{129,65},{193,129... | collective-permute-start | bytes 589832 | tf_op jit(solution)/shard_map/ppermute | solution.py:386
  34.8 0.6 collective-permute-start.10
  35.5 1.4 %collective-permute-start.9 = (bf16[768,128]{1,0:T(8,128)(2,1)S(1)}, bf16[768,128]{1,0:T(8,128)(2,1)S(1)}, u32[]{:S(2)}, u32[]{:S(2)}) collective-permute-start(bf16[768,128]{1,0:T(8,128)(2,1)S(1)} %constant_dynamic-update-slice_fusion.args_17_), channel_id=1, source_target_pairs={{0,64},{64,128},{128,192},{192,0},{1,65},{65,129},{129,193},{193,1... | collective-permute-start | bytes 589832 | tf_op jit(solution)/shard_map/ppermute | solution.py:386
  37.1 1.9 %collective-permute-start.7 = (bf16[16,3200]{1,0:T(8,128)(2,1)S(1)}, bf16[16,3200]{1,0:T(8,128)(2,1)S(1)}, u32[]{:S(2)}, u32[]{:S(2)}) collective-permute-start(bf16[16,3200]{1,0:T(8,128)(2,1)S(1)} %slice.17), channel_id=1, source_target_pairs={{0,28},{4,0},{8,4},{12,8},{16,12},{20,16},{24,20},{28,24},{1,29},{... | collective-permute-start | bytes 307208 | tf_op jit(solution)/shard_map/ppermute | solution.py:370
  39.0 2.5 %collective-permute-done.11.args_20_ = bf16[768,128]{1,0:T(8,128)(2,1)S(1)} collective-permute-done((bf16[768,128]{1,0:T(8,128)(2,1)S(1)}, bf16[768,128]{1,0:T(8,128)(2,1)S(1)}, u32[]{:S(2)}, u32[]{:S(2)}) %collective-permute-start.11) | collective-permute-done | bytes 196640 | tf_op jit(solution)/shard_map/ppermute | solution.py:386
  41.5 2.5 %collective-permute-done.10.args_19_ = bf16[768,128]{1,0:T(8,128)(2,1)S(1)} collective-permute-done((bf16[768,128]{1,0:T(8,128)(2,1)S(1)}, bf16[768,128]{1,0:T(8,128)(2,1)S(1)}, u32[]{:S(2)}, u32[]{:S(2)}) %collective-permute-start.10) | collective-permute-done | bytes 196640 | tf_op jit(solution)/shard_map/ppermute | solution.py:386
  44.0 0.7 collective-permute-start.6
  45.2 0.5 collective-permute-start.17
  45.7 4.2 %collective-permute-done.6.args_7_ = bf16[16,3200]{1,0:T(8,128)(2,1)S(1)} collective-permute-done((bf16[16,3200]{1,0:T(8,128)(2,1)S(1)}, bf16[16,3200]{1,0:T(8,128)(2,1)S(1)}, u32[]{:S(2)}, u32[]{:S(2)}) %collective-permute-start.6) | collective-permute-done | bytes 102432 | tf_op jit(solution)/shard_map/ppermute | solution.py:370
  49.9 0.5 collective-permute-start.18
  50.5 1.0 collective-permute-done.18.args_15_
  51.7 10.0 %shard_map.57 = (bf16[512,3200]{1,0:T(8,128)(2,1)S(1)}, f32[2000,512]{1,0:T(8,128)S(1)}, f32[16,512]{1,0:T(8,128)S(1)}) custom-call(bf16[64,3200]{1,0:T(8,128)(2,1)S(1)} %get-tuple-element.19.args_0_, bf16[32,3200]{1,0:T(8,128)(2,1)S(1)} %collective-permute-done.args_1_, bf16[32,3200]{1,0:T(8,128)(2,1)S(1)} %collective-permute-done.1.args_2_, ...), custom_call_target="tpu_custom_call" | custom-call | flops 6291456000 | bytes 25165824 | tf_op jit(solution)/shard_map/pallas_call | solution.py:270
  61.8 12.5 %all_to_all.20.all_ref = f32[32,2,512]{2,1,0:T(2,128)S(1)} all-to-all(f32[32,2,512]{2,1,0:T(2,128)S(1)} %broadcast_in_dim.3), channel_id=1, replica_groups=mesh['y'=4,'xh'=2,'z'=8,'xl'=2,'co'=2] {'z','xl','co'}, dimensions={0} | all-to-all | bytes 262144 | tf_op jit(solution)/shard_map/all_to_all | solution.py:398
  74.3 7.0 %shard_map.58 = f32[8,80,384]{2,1,0:T(8,128)S(1)} custom-call(f32[16,512]{1,0:T(8,128)S(1)} %get-tuple-element.30.stat_ref, f32[32,2,512]{2,1,0:T(2,128)S(1)} %all_to_all.20.all_ref, bf16[512,3200]{1,0:T(8,128)(2,1)S(1)} %get-tuple-element.31.p_ref, f32[2000,512]{1,0:T(8,128)S(1)} %get-tuple-element.32.expo_ref, ...), custom_call_target="tpu_custom_call" | custom-call | flops 6291456000 | bytes 9437184 | tf_op jit(solution)/shard_map/pallas_call | solution.py:353
  81.3 20.3 %all_to_all.21 = f32[8,80,384]{2,1,0:T(8,128)S(1)} all-to-all(f32[8,80,384]{2,1,0:T(8,128)S(1)} %shard_map.58), channel_id=1, replica_groups=mesh['y'=4,'xh'=2,'z'=8,'xl'=2,'co'=2] {'y','xh'}, dimensions={0} | all-to-all | bytes 1966080 | tf_op jit(solution)/shard_map/all_to_all | solution.py:403
  101.9 12.2 %all_to_all.22 = f32[8,48,128]{2,1,0:T(8,128)S(1)} all-to-all(f32[8,48,128]{2,1,0:T(8,128)S(1)} %bitcast.9), channel_id=1, replica_groups=mesh['y'=4,'xh'=2,'z'=8,'xl'=2,'co'=2] {'z'}, dimensions={0} | all-to-all | bytes 393216 | tf_op jit(solution)/shard_map/all_to_all | solution.py:405
  114.1 0.8 reshape.11
  (39 shorter events, 1.4 us)
Async XLA Ops:
  0.0 1.0 copy-start
  1.0 0.7 copy-start.2
  1.7 0.7 copy-start.3
  2.4 0.7 copy-start.4
  4.0 12.4 %collective-permute-start.3 = (bf16[32,3200]{1,0:T(8,128)(2,1)S(1)}, bf16[32,3200]{1,0:T(8,128)(2,1)S(1)}, u32[]{:S(2)}, u32[]{:S(2)}) collective-permute-start(bf16[32,3200]{1,0:T(8,128)(2,1)S(1)} %get-tuple-element.20), channel_id=1, source_target_pairs={{0,28},{4,0},{8,4},{12,8},{16,12},{20,16},{24,20},{28,24},{1,29},{... | collective-permute-start | bytes 614408 | tf_op jit(solution)/shard_map/ppermute | solution.py:370
  10.0 9.7 %collective-permute-start = (bf16[32,3200]{1,0:T(8,128)(2,1)S(1)}, bf16[32,3200]{1,0:T(8,128)(2,1)S(1)}, u32[]{:S(2)}, u32[]{:S(2)}) collective-permute-start(bf16[32,3200]{1,0:T(8,128)(2,1)S(1)} %get-tuple-element.20), channel_id=1, source_target_pairs={{0,4},{4,8},{8,12},{12,16},{16,20},{20,24},{24,28},{28,0},{1,5},{5... | collective-permute-start | bytes 614408 | tf_op jit(solution)/shard_map/ppermute | solution.py:370
  10.0 0.9 copy-start.1
  11.8 13.9 %all-to-all-start = ((bf16[8,48,128]{2,1,0:T(8,128)(2,1)}), bf16[8,48,128]{2,1,0:T(8,128)(2,1)S(1)}, u32[]{:S(2)}, u32[]{:S(2)}) async-start(bf16[8,48,128]{2,1,0:T(8,128)(2,1)} %shard_map.56), calls=%async_computation | async-start | bytes 196608 | tf_op jit(solution)/shard_map/all_to_all | solution.py:381
  16.4 11.4 %collective-permute-start.4 = (bf16[32,3200]{1,0:T(8,128)(2,1)S(1)}, bf16[32,3200]{1,0:T(8,128)(2,1)S(1)}, u32[]{:S(2)}, u32[]{:S(2)}) collective-permute-start(bf16[32,3200]{1,0:T(8,128)(2,1)S(1)} %collective-permute-done.3.args_4_), channel_id=1, source_target_pairs={{0,28},{4,0},{8,4},{12,8},{16,12},{20,16},{24,20},{28,24},{1,29},{... | collective-permute-start | bytes 614408 | tf_op jit(solution)/shard_map/ppermute | solution.py:370
  19.6 9.0 %collective-permute-start.1 = (bf16[32,3200]{1,0:T(8,128)(2,1)S(1)}, bf16[32,3200]{1,0:T(8,128)(2,1)S(1)}, u32[]{:S(2)}, u32[]{:S(2)}) collective-permute-start(bf16[32,3200]{1,0:T(8,128)(2,1)S(1)} %collective-permute-done.args_1_), channel_id=1, source_target_pairs={{0,4},{4,8},{8,12},{12,16},{16,20},{20,24},{24,28},{28,0},{1,5},{5... | collective-permute-start | bytes 614408 | tf_op jit(solution)/shard_map/ppermute | solution.py:370
  25.6 6.1 %collective-permute-start.8 = (bf16[384,128]{1,0:T(8,128)(2,1)S(1)}, bf16[384,128]{1,0:T(8,128)(2,1)S(1)}, u32[]{:S(2)}, u32[]{:S(2)}) collective-permute-start(bf16[384,128]{1,0:T(8,128)(2,1)S(1)} %bitcast.11), channel_id=1, source_target_pairs={{0,32},{32,0},{1,33},{33,1},{2,34},{34,2},{3,35},{35,3},{4,36},{36... | collective-permute-start | bytes 294920 | tf_op jit(solution)/shard_map/ppermute | solution.py:383
  27.7 9.3 %collective-permute-start.15 = (bf16[32,3200]{1,0:T(8,128)(2,1)S(1)}, bf16[32,3200]{1,0:T(8,128)(2,1)S(1)}, u32[]{:S(2)}, u32[]{:S(2)}) collective-permute-start(bf16[32,3200]{1,0:T(8,128)(2,1)S(1)} %collective-permute-done.3.args_4_), channel_id=1, source_target_pairs={{0,1},{1,0},{2,3},{3,2},{4,5},{5,4},{6,7},{7,6},{8,9},{9,8},{10,11... | collective-permute-start | bytes 614408 | tf_op jit(solution)/shard_map/ppermute | solution.py:374
  27.9 7.6 %collective-permute-start.5 = (bf16[32,3200]{1,0:T(8,128)(2,1)S(1)}, bf16[32,3200]{1,0:T(8,128)(2,1)S(1)}, u32[]{:S(2)}, u32[]{:S(2)}) collective-permute-start(bf16[32,3200]{1,0:T(8,128)(2,1)S(1)} %collective-permute-done.4.args_5_), channel_id=1, source_target_pairs={{0,28},{4,0},{8,4},{12,8},{16,12},{20,16},{24,20},{28,24},{1,29},{... | collective-permute-start | bytes 614408 | tf_op jit(solution)/shard_map/ppermute | solution.py:370
  28.6 8.3 %collective-permute-start.2 = (bf16[32,3200]{1,0:T(8,128)(2,1)S(1)}, bf16[32,3200]{1,0:T(8,128)(2,1)S(1)}, u32[]{:S(2)}, u32[]{:S(2)}) collective-permute-start(bf16[32,3200]{1,0:T(8,128)(2,1)S(1)} %collective-permute-done.1.args_2_), channel_id=1, source_target_pairs={{0,4},{4,8},{8,12},{12,16},{16,20},{20,24},{24,28},{28,0},{1,5},{5... | collective-permute-start | bytes 614408 | tf_op jit(solution)/shard_map/ppermute | solution.py:370
  31.8 9.7 %collective-permute-start.11 = (bf16[768,128]{1,0:T(8,128)(2,1)S(1)}, bf16[768,128]{1,0:T(8,128)(2,1)S(1)}, u32[]{:S(2)}, u32[]{:S(2)}) collective-permute-start(bf16[768,128]{1,0:T(8,128)(2,1)S(1)} %constant_dynamic-update-slice_fusion.args_17_), channel_id=1, source_target_pairs={{0,192},{64,0},{128,64},{192,128},{1,193},{65,1},{129,65},{193,129... | collective-permute-start | bytes 589832 | tf_op jit(solution)/shard_map/ppermute | solution.py:386
  34.8 9.2 %collective-permute-start.10 = (bf16[768,128]{1,0:T(8,128)(2,1)S(1)}, bf16[768,128]{1,0:T(8,128)(2,1)S(1)}, u32[]{:S(2)}, u32[]{:S(2)}) collective-permute-start(bf16[768,128]{1,0:T(8,128)(2,1)S(1)} %constant_dynamic-update-slice_fusion.args_17_), channel_id=1, source_target_pairs={{0,128},{64,192},{128,0},{192,64},{1,129},{65,193},{129,1},{193,65... | collective-permute-start | bytes 589832 | tf_op jit(solution)/shard_map/ppermute | solution.py:386
  35.5 9.7 %collective-permute-start.9 = (bf16[768,128]{1,0:T(8,128)(2,1)S(1)}, bf16[768,128]{1,0:T(8,128)(2,1)S(1)}, u32[]{:S(2)}, u32[]{:S(2)}) collective-permute-start(bf16[768,128]{1,0:T(8,128)(2,1)S(1)} %constant_dynamic-update-slice_fusion.args_17_), channel_id=1, source_target_pairs={{0,64},{64,128},{128,192},{192,0},{1,65},{65,129},{129,193},{193,1... | collective-permute-start | bytes 589832 | tf_op jit(solution)/shard_map/ppermute | solution.py:386
  36.9 12.9 %collective-permute-start.12 = (bf16[32,3200]{1,0:T(8,128)(2,1)S(1)}, bf16[32,3200]{1,0:T(8,128)(2,1)S(1)}, u32[]{:S(2)}, u32[]{:S(2)}) collective-permute-start(bf16[32,3200]{1,0:T(8,128)(2,1)S(1)} %collective-permute-done.args_1_), channel_id=1, source_target_pairs={{0,1},{1,0},{2,3},{3,2},{4,5},{5,4},{6,7},{7,6},{8,9},{9,8},{10,11... | collective-permute-start | bytes 614408 | tf_op jit(solution)/shard_map/ppermute | solution.py:374
  37.1 8.1 %collective-permute-start.7 = (bf16[16,3200]{1,0:T(8,128)(2,1)S(1)}, bf16[16,3200]{1,0:T(8,128)(2,1)S(1)}, u32[]{:S(2)}, u32[]{:S(2)}) collective-permute-start(bf16[16,3200]{1,0:T(8,128)(2,1)S(1)} %slice.17), channel_id=1, source_target_pairs={{0,28},{4,0},{8,4},{12,8},{16,12},{20,16},{24,20},{28,24},{1,29},{... | collective-permute-start | bytes 307208 | tf_op jit(solution)/shard_map/ppermute | solution.py:370
  41.5 8.9 %collective-permute-start.16 = (bf16[32,3200]{1,0:T(8,128)(2,1)S(1)}, bf16[32,3200]{1,0:T(8,128)(2,1)S(1)}, u32[]{:S(2)}, u32[]{:S(2)}) collective-permute-start(bf16[32,3200]{1,0:T(8,128)(2,1)S(1)} %collective-permute-done.4.args_5_), channel_id=1, source_target_pairs={{0,1},{1,0},{2,3},{3,2},{4,5},{5,4},{6,7},{7,6},{8,9},{9,8},{10,11... | collective-permute-start | bytes 614408 | tf_op jit(solution)/shard_map/ppermute | solution.py:374
  44.0 5.9 %collective-permute-start.6 = (bf16[16,3200]{1,0:T(8,128)(2,1)S(1)}, bf16[16,3200]{1,0:T(8,128)(2,1)S(1)}, u32[]{:S(2)}, u32[]{:S(2)}) collective-permute-start(bf16[16,3200]{1,0:T(8,128)(2,1)S(1)} %slice.16), channel_id=1, source_target_pairs={{0,4},{4,8},{8,12},{12,16},{16,20},{20,24},{24,28},{28,0},{1,5},{5... | collective-permute-start | bytes 307208 | tf_op jit(solution)/shard_map/ppermute | solution.py:370
  45.2 5.3 %collective-permute-start.13 = (bf16[32,3200]{1,0:T(8,128)(2,1)S(1)}, bf16[32,3200]{1,0:T(8,128)(2,1)S(1)}, u32[]{:S(2)}, u32[]{:S(2)}) collective-permute-start(bf16[32,3200]{1,0:T(8,128)(2,1)S(1)} %collective-permute-done.1.args_2_), channel_id=1, source_target_pairs={{0,1},{1,0},{2,3},{3,2},{4,5},{5,4},{6,7},{7,6},{8,9},{9,8},{10,11... | collective-permute-start | bytes 614408 | tf_op jit(solution)/shard_map/ppermute | solution.py:374
  45.2 5.3 %collective-permute-start.17 = (bf16[32,3200]{1,0:T(8,128)(2,1)S(1)}, bf16[32,3200]{1,0:T(8,128)(2,1)S(1)}, u32[]{:S(2)}, u32[]{:S(2)}) collective-permute-start(bf16[32,3200]{1,0:T(8,128)(2,1)S(1)} %collective-permute-done.5.args_6_), channel_id=1, source_target_pairs={{0,1},{1,0},{2,3},{3,2},{4,5},{5,4},{6,7},{7,6},{8,9},{9,8},{10,11... | collective-permute-start | bytes 614408 | tf_op jit(solution)/shard_map/ppermute | solution.py:374
  49.9 1.8 %collective-permute-start.14 = (bf16[32,3200]{1,0:T(8,128)(2,1)S(1)}, bf16[32,3200]{1,0:T(8,128)(2,1)S(1)}, u32[]{:S(2)}, u32[]{:S(2)}) collective-permute-start(bf16[32,3200]{1,0:T(8,128)(2,1)S(1)} %collective-permute-done.2.args_3_), channel_id=1, source_target_pairs={{0,1},{1,0},{2,3},{3,2},{4,5},{5,4},{6,7},{7,6},{8,9},{9,8},{10,11... | collective-permute-start | bytes 614408 | tf_op jit(solution)/shard_map/ppermute | solution.py:374
  49.9 1.6 %collective-permute-start.18 = (bf16[16,3200]{1,0:T(8,128)(2,1)S(1)}, bf16[16,3200]{1,0:T(8,128)(2,1)S(1)}, u32[]{:S(2)}, u32[]{:S(2)}) collective-permute-start(bf16[16,3200]{1,0:T(8,128)(2,1)S(1)} %collective-permute-done.6.args_7_), channel_id=1, source_target_pairs={{0,1},{1,0},{2,3},{3,2},{4,5},{5,4},{6,7},{7,6},{8,9},{9,8},{10,11... | collective-permute-start | bytes 307208 | tf_op jit(solution)/shard_map/ppermute | solution.py:374
  50.4 1.3 %collective-permute-start.19 = (bf16[16,3200]{1,0:T(8,128)(2,1)S(1)}, bf16[16,3200]{1,0:T(8,128)(2,1)S(1)}, u32[]{:S(2)}, u32[]{:S(2)}) collective-permute-start(bf16[16,3200]{1,0:T(8,128)(2,1)S(1)} %collective-permute-done.7.args_8_), channel_id=1, source_target_pairs={{0,1},{1,0},{2,3},{3,2},{4,5},{5,4},{6,7},{7,6},{8,9},{9,8},{10,11... | collective-permute-start | bytes 307208 | tf_op jit(solution)/shard_map/ppermute | solution.py:374
